TPU v7x, 32 devices: a whole 2x2x4 slice. The times are simulated.
32 devices in a mesh: dp: 8 (over z, x), seq: 4 (over y, core).
Axes of the slice: x: 2, y: 2, z: 4, core: 2. Of those that a mesh axis runs over, the one named last changes fastest.
Arguments:
- inputs: bfloat16 [32, 512, 768], P('dp', 'seq'), may hold values from -6 to 6
- cotangent: bfloat16 [32, 512, 768], P('dp', 'seq'), may hold values from -6 to 6
- masked: int32 [32, 512], P('dp', 'seq'), may hold values from 0 to 1, as said below
- w_query: bfloat16 [768, 768], replicated, may hold values from -0.21875 to 0.21875
- b_query: bfloat16 [768], replicated, may hold values from -3 to 3
- w_key: bfloat16 [768, 768], replicated, may hold values from -0.21875 to 0.21875
- w_value: bfloat16 [768, 768], replicated, may hold values from -0.21875 to 0.21875
- b_value: bfloat16 [768], replicated, may hold values from -3 to 3
- w_output: bfloat16 [768, 768], replicated, may hold values from -0.625 to 0.625
- b_output: bfloat16 [768], replicated, may hold values from -3 to 3
- attn_gain: bfloat16 [768], replicated, may hold values from 0.5 to 1.5
- attn_shift: bfloat16 [768], replicated, may hold values from -3 to 3
- w_inner: bfloat16 [768, 3072], replicated, may hold values from -0.21875 to 0.21875
- b_inner: bfloat16 [3072], replicated, may hold values from -3 to 3
- w_outer: bfloat16 [3072, 768], replicated, may hold values from -0.109375 to 0.109375
- b_outer: bfloat16 [768], replicated, may hold values from -3 to 3
- ffn_gain: bfloat16 [768], replicated, may hold values from 0.5 to 1.5
- ffn_shift: bfloat16 [768], replicated, may hold values from -3 to 3
Outputs:
- outputs: bfloat16 [32, 512, 768], P('dp', 'seq')
- grad_inputs: bfloat16 [32, 512, 768], P('dp', 'seq')
- grad_w_query: float32 [768, 768], P('dp')
- grad_b_query: float32 [768], P('dp')
- grad_w_key: float32 [768, 768], P('dp')
- grad_w_value: float32 [768, 768], P('dp')
- grad_b_value: float32 [768], P('dp')
- grad_w_output: float32 [768, 768], P('dp')
- grad_b_output: float32 [768], P('dp')
- grad_attn_gain: float32 [768], P('dp')
- grad_attn_shift: float32 [768], P('dp')
- grad_w_inner: float32 [768, 3072], P('dp')
- grad_b_inner: float32 [3072], P('dp')
- grad_w_outer: float32 [3072, 768], P('dp')
- grad_b_outer: float32 [768], P('dp')
- grad_ffn_gain: float32 [768], P('dp')
- grad_ffn_shift: float32 [768], P('dp')
Inputs may be any that keep to these rules, and one draw needn't show every extreme that they name: The share of masked positions may differ from one block of 128 positions of a sentence to the next.
All inputs are finite; a program needn't handle non-finite values.
Results may differ from a plain program's by a relative error of at most 0.019.
Values may be sent and summed in bfloat16 or wider, within the bound.
No kernel may reach another device: no remote copies, remote signals or barrier semaphores. Data moves between devices by JAX's collectives and lax.ppermute only.
A program may use at most 128 MiB of HBM per device.

v0:
```python
import jax
import jax.numpy as jnp
from jax import lax
from jax.experimental import pallas as pl
from jax.experimental.pallas import tpu as pltpu
from jax.sharding import PartitionSpec as P

HD = 64
PAIR = 2 * HD
TILE = 256
EPSILON = 1e-05
F32, BF16 = jnp.float32, jnp.bfloat16
CORE, SEQ, DP, SLOTS = 0, 1, 2, 3
TABLE = 16
SCALE = 3e9
ORDER = (
    "ho", "hm", "go", "co", "gi", "fb", "ao", "o", "am", "o", "gr", "i", "r", "ib", "i", "o", "r",
    "i", "o", "ci", "r", "fo", "i", "r", "fi", "fr",
)
OUTER, INNER, REST = ((0, 1, 2), (1, 0, 2)), ((2, 0, 1), (1, 2, 0)), ((0, 1, 2), (1, 0, 2))


def nn(a, b):
    return lax.dot_general(a, b, (((1,), (0,)), ((), ())), preferred_element_type=F32)


def nt(a, b):
    return lax.dot_general(a, b, (((1,), (1,)), ((), ())), preferred_element_type=F32)


def tn(a, b):
    return lax.dot_general(a, b, (((0,), (0,)), ((), ())), preferred_element_type=F32)


def like(shape, dtype=BF16):
    return jax.ShapeDtypeStruct(shape, dtype)


def call(kernel, name, info, ins, outs, us, mb=14, after=(), hbm=0, scratch=()):
    n, skip = len(ins), len(after)

    def run(info_ref, *refs):
        kernel(info_ref, *refs[:n], *refs[n + skip :])

    return pl.pallas_call(
        run,
        in_specs=[pl.BlockSpec(memory_space=pltpu.SMEM)]
        + [pl.BlockSpec(memory_space=pltpu.VMEM)] * (n - hbm)
        + [pl.BlockSpec(memory_space=pltpu.HBM)] * hbm
        + [pl.BlockSpec(memory_space=pl.ANY)] * skip,
        out_shape=outs,
        scratch_shapes=list(scratch),
        compiler_params=pltpu.CompilerParams(vmem_limit_bytes=mb * 1024 * 1024),
        cost_estimate=pl.CostEstimate(
            flops=int(us * SCALE), bytes_accessed=1, transcendentals=0
        ),
        name=name,
    )(info, *ins, *after)


def fetch(sources, targets, sems):
    copies = [pltpu.make_async_copy(a, b, sems.at[i]) for i, (a, b) in enumerate(zip(sources, targets))]
    for c in copies:
        c.start()
    return copies


def halves(value):
    lane = lax.broadcasted_iota(jnp.int32, value.shape, 1)
    zero = jnp.zeros_like(value)
    return jnp.where(lane < HD, value, zero), jnp.where(lane < HD, zero, value)


def standardize(v):
    mean = jnp.mean(v, axis=-1, keepdims=True)
    c = v - mean
    r = lax.rsqrt(jnp.mean(c * c, axis=-1, keepdims=True) + EPSILON)
    return c * r, r


def norm_back(e, n, r):
    return r * (e - jnp.mean(e, axis=-1, keepdims=True) - n * jnp.mean(e * n, axis=-1, keepdims=True))


def columns(width):
    return [slice(j, j + TILE) for j in range(0, width, TILE)]


def tiles_loop(width, each, body):
    def step(i, carry):
        for j in range(each):
            body(pl.ds(pl.multiple_of((i * each + j) * TILE, TILE), TILE))
        return carry

    lax.fori_loop(0, width // (TILE * each), step, 0)


def total(value):
    return jnp.sum(value, axis=0, keepdims=True)


def attention_kernel(
    info_ref, x0, x1, x2, x3, bq_ref, bv_ref, bo_ref, gain_ref, shift_ref, wq_hbm, wk_hbm, wv_hbm, wo_hbm,
    x_ref, q_ref, k_ref, v_ref, p_ref, ctx_ref, n_ref, r_ref, low_ref,
    wq_ref, wk_ref, wv_ref, wo_ref, sems,
):
    rows, width = x_ref.shape
    block = x0.shape[0]
    copies = fetch((wq_hbm, wk_hbm, wv_hbm, wo_hbm), (wq_ref, wk_ref, wv_ref, wo_ref), sems)
    for i, part in enumerate((x0, x1, x2, x3)):
        x_ref[i * block : (i + 1) * block, :] = part[...]
    x = x_ref[...]
    copies[0].wait()
    for at in columns(width):
        q = (nn(x, wq_ref[:, at]) + bq_ref[:, at].astype(F32)).astype(BF16)
        q_ref[:, at] = q * jnp.asarray(HD ** -0.5, BF16)
    copies[1].wait()
    for at in columns(width):
        k_ref[:, at] = nn(x, wk_ref[:, at]).astype(BF16)
    copies[2].wait()
    for at in columns(width):
        v_ref[:, at] = (nn(x, wv_ref[:, at]) + bv_ref[:, at].astype(F32)).astype(BF16)
    def pair(p, carry):
        at = pl.ds(pl.multiple_of(p * PAIR, PAIR), PAIR)
        q, k, v = q_ref[:, at], k_ref[:, at], v_ref[:, at]
        vt = v.astype(F32).T.astype(BF16)
        out = []
        for i, kh in enumerate(halves(k)):
            s = nt(kh, q)
            e = jnp.exp(s - jnp.max(s, axis=0, keepdims=True))
            w = (e * (1.0 / total(e))).astype(BF16)
            p_ref[2 * p + i] = w
            out.append(nn(vt[i * HD : (i + 1) * HD], w))
        ctx_ref[:, at] = jnp.concatenate(out, axis=0).T.astype(BF16)
        return carry

    lax.fori_loop(0, width // PAIR, pair, 0)
    copies[3].wait()
    v1 = jnp.concatenate([nn(ctx_ref[...], wo_ref[:, at]) for at in columns(width)], axis=1)
    v1 = x_ref[...].astype(F32) + (v1 + bo_ref[...].astype(F32))
    n, r = standardize(v1)
    n_ref[...] = n
    r_ref[...] = r
    low_ref[...] = (n * gain_ref[...].astype(F32) + shift_ref[...].astype(F32)).astype(BF16)


def hidden_kernel(info_ref, low_ref, w_ref, b_ref, act_ref, slope_ref):
    def tile(at):
        h = nn(low_ref[...], w_ref[:, at]) + b_ref[:, at].astype(F32)
        z = h * 0.7071067811865476
        phi = 0.5 + 0.5 * lax.erf(z)
        bell = jnp.exp2(z * z * -1.4426950408889634)
        act_ref[:, at] = (h * phi).astype(BF16)
        slope_ref[:, at] = (phi + z * bell * 0.5641895835477563).astype(BF16)

    tiles_loop(w_ref.shape[1], 3, tile)


def split_store(core, value, mine_ref, other_ref):
    half = value.shape[1] // 2
    mine_ref[...] = jnp.where(core == 0, value[:, :half], value[:, half:])
    other_ref[...] = jnp.where(core == 0, value[:, half:], value[:, :half])


def branch_kernel(
    info_ref, act_ref, w_ref, b_ref, n_ref, gain1_ref, shift1_ref, gain_ref, shift_ref, c0, c1, c2, c3,
    o0, o1, o2, o3, mid_ref, low_ref, mine_ref, other_ref, sums_ref,
):
    width = mid_ref.shape[1]
    normed = n_ref[...] * gain1_ref[...].astype(F32) + shift1_ref[...].astype(F32)
    branch = jnp.concatenate([nn(act_ref[...], w_ref[:, at]) for at in columns(width)], axis=1)
    n, r = standardize(normed + (branch + b_ref[...].astype(F32)))
    gain = gain_ref[...].astype(F32)
    out = (n * gain + shift_ref[...].astype(F32)).astype(BF16)
    for i, ref in enumerate((o0, o1, o2, o3)):
        ref[...] = out[i * ref.shape[0] : (i + 1) * ref.shape[0]]
    go = jnp.concatenate([c[...] for c in (c0, c1, c2, c3)]).astype(F32)
    mid = norm_back(go * gain, n, r)
    mid_ref[...] = mid
    low = mid.astype(BF16)
    low_ref[...] = low
    split_store(info_ref[CORE], low, mine_ref, other_ref)
    sums_ref[0:1] = total(go * n)
    sums_ref[1:2] = total(go)
    sums_ref[2:3] = total(low.astype(F32))


def hidden_back_kernel(flip):
    def kernel(info_ref, low_ref, w_ref, slope_ref, out_ref, sums_ref):
        half = out_ref.shape[1]
        core = info_ref[CORE]
        first = ((1 - core) if flip else core) * half
        for to in columns(half):
            at = pl.ds(pl.multiple_of(first + to.start, TILE), TILE)
            g = (nt(low_ref[...], w_ref[at, :]) * slope_ref[:, at].astype(F32)).astype(BF16)
            out_ref[:, to] = g
            sums_ref[:, to] = total(g.astype(F32))

    return kernel


def first_back_kernel(
    info_ref, gm_ref, go_ref, w_ref, mid_ref, n_ref, r_ref, gain_ref, wo_ref,
    sum_ref, gctx_ref, mine_ref, other_ref, sums_ref,
):
    width, half = mid_ref.shape[1], gm_ref.shape[1]
    core = info_ref[CORE]
    mine = pl.ds(pl.multiple_of(core * half, half), half)
    other = pl.ds(pl.multiple_of((1 - core) * half, half), half)
    gn = jnp.concatenate(
        [nt(gm_ref[...], w_ref[at, mine]) + nt(go_ref[...], w_ref[at, other]) for at in columns(width)], axis=1
    )
    gn = gn + mid_ref[...]
    n = n_ref[...]
    gs = norm_back(gn * gain_ref[...].astype(F32), n, r_ref[...])
    sum_ref[...] = gs
    low = gs.astype(BF16)
    split_store(core, low, mine_ref, other_ref)
    sums_ref[0:1] = total(gn * n)
    sums_ref[1:2] = total(gn)
    sums_ref[2:3] = total(low.astype(F32))
    for at in columns(width):
        gctx_ref[:, at] = nt(low, wo_ref[at, :]).astype(BF16)


def attention_back_kernel(flip):
    def kernel(info_ref, q_ref, k_ref, v_ref, p_ref, g_ref, out_ref, sums_ref):
        rows, width = q_ref.shape
        per = width // PAIR // 2
        core = info_ref[CORE]
        first = ((1 - core) if flip else core) * per

        def pair(p, carry):
            at = pl.ds(pl.multiple_of((first + p) * PAIR, PAIR), PAIR)
            to = pl.ds(pl.multiple_of(p * PAIR, PAIR), PAIR)
            q, k, v, g = q_ref[:, at], k_ref[:, at], v_ref[:, at], g_ref[:, at]
            kt = k.astype(F32).T.astype(BF16)
            gk = jnp.zeros((rows, PAIR), F32)
            gv = jnp.zeros((rows, PAIR), F32)
            gq = []
            for i, (qh, vh, gh) in enumerate(zip(halves(q), halves(v), halves(g))):
                w = p_ref[2 * (first + p) + i]
                w32 = w.astype(F32)
                prod = w32 * nt(vh, g)
                gs = (prod - w32 * total(prod)).astype(BF16)
                gk = gk + nn(gs, qh)
                gv = gv + nn(w, gh)
                gq.append(nn(kt[i * HD : (i + 1) * HD], gs))
            gq = jnp.concatenate(gq, axis=0).T * HD ** -0.5
            for i, value in enumerate((gq, gk, gv)):
                value = value.astype(BF16)
                out_ref[i, :, to] = value
                sums_ref[i : i + 1, to] = total(value.astype(F32))
            return carry

        lax.fori_loop(0, per, pair, 0)

    return kernel


def input_back_kernel(info_ref, gm_ref, go_ref, sum_ref, wq_hbm, wk_hbm, wv_hbm, o0, o1, o2, o3, wq_ref, wk_ref, wv_ref, sems):
    half = gm_ref.shape[2]
    copies = fetch((wq_hbm, wk_hbm, wv_hbm), (wq_ref, wk_ref, wv_ref), sems)
    core = info_ref[CORE]
    mine = pl.ds(pl.multiple_of(core * half, half), half)
    other = pl.ds(pl.multiple_of((1 - core) * half, half), half)
    tiles = columns(sum_ref.shape[1])
    values = [sum_ref[:, at] for at in tiles]
    for i, w in enumerate((wq_ref, wk_ref, wv_ref)):
        copies[i].wait()
        for j, at in enumerate(tiles):
            values[j] = values[j] + nt(gm_ref[i], w[at, mine]) + nt(go_ref[i], w[at, other])
    for value, at in zip(values, tiles):
        value = value.astype(BF16)
        for i, ref in enumerate((o0, o1, o2, o3)):
            ref[:, at] = value[i * ref.shape[0] : (i + 1) * ref.shape[0]]


def place(info_ref, base, rows, buf_ref, keep_ref, send_ref):
    slots = buf_ref.shape[0] // rows
    for slot in range(slots):
        chunk = buf_ref[pl.ds(pl.multiple_of(info_ref[base + slot] * rows, 16), rows), :]
        ref, to = (keep_ref, slot) if slot < slots // 2 else (send_ref, slot - slots // 2)
        ref[to * rows : (to + 1) * rows, :] = chunk


def outer_kernel(base, rows):
    def kernel(info_ref, la, lb, ra, rb, keep_ref, send_ref, buf_ref):
        def tile(at):
            buf_ref[at, :] = (tn(la[:, at], ra[...]) + tn(lb[:, at], rb[...])).astype(BF16)

        tiles_loop(la.shape[1], 3, tile)
        place(info_ref, base, rows, buf_ref, keep_ref, send_ref)

    return kernel


def inner_kernel(base, rows):
    def kernel(info_ref, la, lb, ra, rb, keep_ref, send_ref, buf_ref):
        for at in columns(ra.shape[1]):
            buf_ref[:, at] = (tn(la[...], ra[:, at]) + tn(lb[...], rb[:, at])).astype(BF16)
        place(info_ref, base, rows, buf_ref, keep_ref, send_ref)

    return kernel


def fill_table(info_ref, table_ref, s0m, s0o, s1, s2, sim, sio):
    half = s0m.shape[1]
    core = info_ref[CORE]
    own = pl.ds(pl.multiple_of(core * half, half), half)
    others = pl.ds(pl.multiple_of((1 - core) * half, half), half)
    table_ref[...] = jnp.zeros_like(table_ref)
    table_ref[0:3, own] = s0m[...]
    table_ref[0:3, others] = s0o[...]
    table_ref[3:6] = s1[...]
    table_ref[6:9] = s2[...]
    per = sim.shape[1] // half
    for part, which in ((sim, core), (sio, 1 - core)):
        for i in range(per):
            flat = which * per + i
            at = pl.ds(pl.multiple_of(lax.rem(flat, 2) * half, half), half)
            table_ref[pl.ds(9 + lax.div(flat, 2), 1), at] = part[:, i * half : (i + 1) * half]


def rest_kernel(base, rows):
    def kernel(
        info_ref, xa, xb, ca, cb, ga, gb, oa, ob, s0m, s0o, s1, s2, sim, sio, keep_ref, send_ref, table_ref, buf_ref
    ):
        half = s0m.shape[1]
        slots = xa.shape[1] // rows
        for i in range(4):
            la, lb, ra, rb = (xa, xb, ga.at[i], gb.at[i]) if i < 3 else (ca, cb, oa, ob)
            buf_ref[i] = (tn(la[...], ra[...]) + tn(lb[...], rb[...])).astype(BF16)
            for slot in range(slots):
                chunk = buf_ref[i, pl.ds(pl.multiple_of(info_ref[base + slot] * rows, 16), rows), :]
                ref, to = (keep_ref, slot) if slot < slots // 2 else (send_ref, slot - slots // 2)
                ref[(4 * to + i) * rows : (4 * to + i + 1) * rows, :] = chunk
        fill_table(info_ref, table_ref, s0m, s0o, s1, s2, sim, sio)
        at = keep_ref.shape[0]
        for i in range(2):
            send_ref[at + i * TABLE : at + (i + 1) * TABLE] = table_ref[:, i * half : (i + 1) * half].astype(BF16)

    return kernel


def stage_kernel(low, high, out_dtype, tables):
    def kernel(info_ref, *refs):
        ins, out_ref = refs[:-1], refs[-1]
        if tables:
            sent_ref, ins = ins[-1], ins[:-1]
        value = ins[0][low:high].astype(F32)
        for ref in ins[1:]:
            value = value + ref[low:high].astype(F32)
        out_ref[0 : high - low] = value.astype(out_dtype)
        if tables:
            rows = sent_ref.shape[0]
            value = sent_ref[rows - 2 * TABLE :].astype(F32) + ins[-1][rows - 2 * TABLE :].astype(F32)
            out_ref[high - low :] = value.astype(out_dtype)

    return kernel


def deal_kernel(info_ref, in_hbm, *refs):
    outs, sems = refs[:-1], refs[-1]
    for c in fetch([in_hbm.at[info_ref[SEQ] ^ k] for k in range(len(outs))], outs, sems):
        c.wait()


def collect_kernel(info_ref, *refs):
    for k, part in enumerate(refs[:-1]):
        refs[-1][info_ref[SEQ] ^ k] = part[...]


def finish_kernel(part, tables):
    def kernel(info_ref, *refs):
        quarters, outs = refs[:4], refs[4:]
        core, ybit = info_ref[CORE], info_ref[SEQ] // 2
        half = quarters[0].shape[1]
        if tables:
            outs, small_ref, wide_ref = outs[:-2], outs[-2], outs[-1]
        for i, ref in enumerate(quarters):
            row = pl.multiple_of((ybit ^ (i & 1)) * part, 8)
            column = pl.multiple_of((core ^ (i >> 1)) * half, 128)
            for j, out_ref in enumerate(outs):
                out_ref[pl.ds(row, part), pl.ds(column, half)] = ref[j * part : (j + 1) * part].astype(F32)
        if tables:
            at = len(outs) * part
            table = [
                quarters[0][at + i * TABLE : at + (i + 1) * TABLE].astype(F32)
                + quarters[2][at + i * TABLE : at + (i + 1) * TABLE].astype(F32)
                for i in range(2)
            ]
            d = info_ref[DP]
            lanes = 2 * half
            step = 2 * part
            rolled = pltpu.roll(jnp.concatenate(table, axis=1), lax.rem(lanes - d * step, lanes), 1)
            small_ref[...] = rolled[:, : small_ref.shape[1]]
            per = wide_ref.shape[1]
            count = lanes // per
            for row in range(TABLE - 9):
                for k in range(count):
                    line = jnp.concatenate([t[9 + row : 10 + row] for t in table], axis=1)

                    @pl.when(d == row * count + k)
                    def _():
                        wide_ref[...] = line[:, k * per : (k + 1) * per]

    return kernel


def swap(value, axis, size, bit):
    return lax.ppermute(value, axis, [(i, i ^ bit) for i in range(size)])


def make_body(sizes):
    size, dp = sizes["seq"], sizes["dp"]
    nbits = dp.bit_length()
    chunks = 2 * dp
    rest_bits = list(range(3, nbits))
    orders = {
        name: [[*bits, *rest_bits] for bits in order]
        for name, order in (("outer", OUTER), ("inner", INNER), ("rest", REST))
    }
    bases = {name: SLOTS + i * chunks for i, name in enumerate(orders)}

    def my_bit(axis, bit):
        return (lax.axis_index(axis) & bit) // bit

    def pair(value):
        return swap(value, "seq", size, 1)

    def exchange(value, bits):
        moves = []
        for d in range(dp):
            for s in range(size):
                bit = bits[s % 2]
                to = (d, s ^ 2) if bit == 0 else (d ^ (1 << (bit - 1)), s)
                moves.append((d * size + s, to[0] * size + to[1]))
        return lax.ppermute(value, ("dp", "seq"), moves)

    def chunk_table(me, core, order):
        slot = jnp.arange(chunks, dtype=jnp.int32)
        rel = [sum(((slot >> (nbits - 1 - s)) & 1) << bit for s, bit in enumerate(bits)) for bits in order]
        return jnp.where(core == 0, rel[0], rel[1]) ^ me

    class Halving:
        def __init__(self, info, keep, send, name, part, tables=False):
            self.info, self.keep, self.send, self.name, self.part = info, keep, send, name, part
            self.tables, self.got, self.left, self.stage = tables, [], chunks // 2, 0
            self.move()

        def move(self):
            first, second = orders[self.name]
            self.got.append(exchange(self.send, (first[self.stage], second[self.stage])))

        def step(self, *after):
            part, n = self.part, self.left
            last = self.stage == nbits - 1
            low, high = (0, part) if last else (n // 2 * part, n * part)
            ins = [self.keep, *self.got] + ([self.send] if self.tables else [])
            shape = like((high - low + (2 * TABLE if self.tables else 0), self.keep.shape[1]))
            self.send = call(
                stage_kernel(low, high, BF16, self.tables),
                f"{self.name}{self.stage}", self.info, ins, shape, 1, after=after,
            )
            self.left, self.stage = n // 2, self.stage + 1
            if not last:
                self.move()
            return self.send

    def spread(value, bit):
        other = swap(value, "seq", size, bit)
        first = my_bit("seq", bit) == 0
        return jnp.where(first, value, other), jnp.where(first, other, value)

    def plain_halving(value, order, me, core):
        kept = [jnp.take(value, chunk_table(me, core, order), axis=0)]
        n = chunks
        for s in range(nbits):
            n //= 2
            send = sum(v[n : 2 * n].astype(F32) for v in kept).astype(BF16)
            kept.append(exchange(send, (order[0][s], order[1][s])))
        return sum(v[0].astype(F32) for v in kept).astype(BF16)

    def body(
        inputs,
        cotangent,
        masked,
        w_query,
        b_query,
        w_key,
        w_value,
        b_value,
        w_output,
        b_output,
        attn_gain,
        attn_shift,
        w_inner,
        b_inner,
        w_outer,
        b_outer,
        ffn_gain,
        ffn_shift,
    ):
        shape = inputs.shape
        count, block, width = shape
        rows, wide, half = count * block, w_inner.shape[1], width // 2
        assert count == size == 4
        seq = lax.axis_index("seq")
        core, ybit = my_bit("seq", 1), my_bit("seq", 2)
        me = lax.axis_index("dp") * 2 + ybit
        info = jnp.concatenate(
            [jnp.stack([core, seq, lax.axis_index("dp")])] + [chunk_table(me, core, order) for order in orders.values()]
        ).astype(jnp.int32)
        row = lambda v: v.reshape(1, -1)
        full = like((rows, width))

        part_o, part_i = wide // dp // 2, width // dp // 2
        fast = nbits == 4 and part_i % 16 == 0 and (2 * part_o) % 128 == 0 and width % (2 * part_o) == 0
        blocks = [like((block, width))] * size

        def gather(value, name):
            parts = call(
                deal_kernel, name, info, [value], blocks, 1, hbm=1,
                scratch=[pltpu.SemaphoreType.DMA((size,))],
            )
            return [swap(v, "seq", size, k) if k else v for k, v in enumerate(parts)]

        def scatter(parts):
            return [parts[0]] + [swap(parts[k], "seq", size, k) for k in range(1, size)]

        def collect(parts, name, *after):
            return call(collect_kernel, name, info, parts, like(shape), 1, after=after)

        x_parts = gather(inputs, "deal_inputs")
        cot_parts = gather(cotangent * masked[:, :, None].astype(BF16), "deal_cotangent")
        square = pltpu.VMEM((width, width), BF16)
        x, q, k, v, p, ctx, n1, r1, low1 = call(
            attention_kernel, "attention", info,
            [*x_parts, row(b_query), row(b_value), row(b_output), row(attn_gain), row(attn_shift),
             w_query, w_key, w_value, w_output],
            (full, full, full, full, like((width // HD, rows, rows)), full, like((rows, width), F32),
             like((rows, 1), F32), full),
            13, 20, hbm=4, scratch=[square] * 4 + [pltpu.SemaphoreType.DMA((4,))],
        )
        x_other, ctx_other, low_other = pair(x), pair(ctx), pair(low1)
        act, slope = call(
            hidden_kernel, "hidden", info, [low1, w_inner, row(b_inner)],
            (like((rows, wide)), like((rows, wide))), 9, after=cot_parts,
        )
        act_other = pair(act)
        *out, mid, gb, gb_mine, gb_send, sums2 = call(
            branch_kernel, "branch", info,
            [act, w_outer, row(b_outer), n1, row(attn_gain), row(attn_shift), row(ffn_gain), row(ffn_shift),
             *cot_parts],
            (*blocks, like((rows, width), F32), full, like((rows, half)), like((rows, half)), like((3, width), F32)),
            4, 16,
        )
        gb_other = pair(gb_send)
        out = scatter(out)
        env, groups, token = {}, {}, []

        def buffers(part, columns, extra=0):
            return like((dp * part, columns)), like((dp * part + extra, columns))

        def product(a, b):
            return (tn(a[0], b[0]) + tn(a[1], b[1])).astype(BF16)

        def quarters(own):
            other = swap(own, "seq", size, 2)
            return [own, other, pair(own), pair(other)]

        def hidden_back(name, flip):
            shapes = (like((rows, wide // 2)), like((1, wide // 2), F32))
            env["gh_" + name], env["sumi_" + name] = call(
                hidden_back_kernel(flip), "hidden_back_" + name, info, [gb, w_outer, slope], shapes, 3,
                after=[*token, act_other] if flip else [*token, gb_other],
            )
            if flip:
                env["gh_pair"] = pair(env["gh_other"])
            return env["sumi_" + name]

        def grad_outer():
            keep, send = call(
                outer_kernel(bases["outer"], part_o), "grad_outer", info, [act, act_other, gb_mine, gb_other],
                buffers(part_o, half), 5, after=token, scratch=[pltpu.VMEM((wide, half), BF16)],
            )
            groups["o"] = Halving(info, keep, send, "outer", part_o)
            return send

        def grad_inner():
            keep, send = call(
                inner_kernel(bases["inner"], part_i), "grad_inner", info,
                [low1, low_other, env["gh_mine"], env["gh_pair"]], buffers(part_i, wide // 2), 4, after=token,
                scratch=[pltpu.VMEM((width, wide // 2), BF16)],
            )
            groups["i"] = Halving(info, keep, send, "inner", part_i)
            return send

        def first_back():
            env["gsum"], env["gctx"], env["ga"], ga_send, env["sums1"] = call(
                first_back_kernel, "first_back", info,
                [env["gh_mine"], env["gh_other"], w_inner, mid, n1, r1, row(attn_gain), w_output],
                (like((rows, width), F32), full, like((rows, half)), like((rows, half)), like((3, width), F32)),
                6, after=token,
            )
            env["ga_pair"] = pair(ga_send)
            return env["sums1"]

        def attention_back(name, flip):
            env["g3_" + name], env["sums0_" + name] = call(
                attention_back_kernel(flip), "attention_back_" + name, info, [q, k, v, p, env["gctx"]],
                (like((3, rows, half)), like((3, half), F32)), 1, after=token,
            )
            if flip:
                env["g3_pair"] = pair(env["g3_other"])
            return env["sums0_" + name]

        def grad_rest():
            sums = [env["sums0_mine"], env["sums0_other"], env["sums1"], sums2, env["sumi_mine"], env["sumi_other"]]
            keep, send, table = call(
                rest_kernel(bases["rest"], part_i), "grad_rest", info,
                [x, x_other, ctx, ctx_other, env["g3_mine"], env["g3_pair"], env["ga"], env["ga_pair"], *sums],
                (*buffers(4 * part_i, half, 2 * TABLE), like((TABLE, width), F32)), 1, after=token,
                scratch=[pltpu.VMEM((4, width, half), BF16)],
            )
            groups["r"] = Halving(info, keep, send, "rest", 4 * part_i, True)
            return table

        def input_back():
            parts = call(
                input_back_kernel, "input_back", info,
                [env["g3_mine"], env["g3_other"], env["gsum"], w_query, w_key, w_value], blocks, 2, after=token,
                hbm=3, mb=52, scratch=[square] * 3 + [pltpu.SemaphoreType.DMA((3,))],
            )
            env["back"] = scatter(parts)
            return parts[0]

        def step(name):
            own = groups[name].step(*token)
            if groups[name].stage == nbits:
                env["q" + name] = quarters(own)
            return own

        def finish_group(name, part, columns, title):
            env["g" + name] = call(
                finish_kernel(part, False), title, info, env["q" + name], like((2 * part, columns), F32), 1, after=token
            )
            return env["g" + name]

        def finish_rest():
            matrix, thin = like((2 * part_i, width), F32), like((TABLE, 128), F32)
            env["gr"] = call(
                finish_kernel(part_i, True), "finish_rest", info, env["qr"],
                (matrix, matrix, matrix, matrix, thin, like((1, 2 * part_o), F32)), 1, after=token,
            )
            return env["gr"][4]

        def collect(name, parts):
            env[name] = call(collect_kernel, "collect_" + name, info, parts, like(shape), 1, after=token)
            return env[name]

        tasks = {
            "ho": lambda: hidden_back("other", True),
            "hm": lambda: hidden_back("mine", False),
            "go": grad_outer,
            "gi": grad_inner,
            "fb": first_back,
            "ao": lambda: attention_back("other", True),
            "am": lambda: attention_back("mine", False),
            "gr": grad_rest,
            "ib": input_back,
            "o": lambda: step("o"),
            "i": lambda: step("i"),
            "r": lambda: step("r"),
            "fo": lambda: finish_group("o", part_o, width, "finish_outer"),
            "fi": lambda: finish_group("i", part_i, wide, "finish_inner"),
            "fr": finish_rest,
            "co": lambda: collect("outputs", out),
            "ci": lambda: collect("inputs", env["back"]),
        }
        for name in ORDER:
            if fast or name in ("ho", "hm", "fb", "ao", "am", "ib", "co", "ci"):
                token = [tasks[name]()]

        def finish(value, group, part, columns):
            value = jnp.stack(spread(value.reshape(group, part, columns // 2), 2), axis=1)
            value = value.reshape(group, 2 * part, columns // 2)
            return jnp.concatenate(spread(value, 1), axis=-1).astype(F32)

        if fast:
            g_outer, g_inner = env["go"], env["gi"]
            g_query, g_key, g_value, g_output, small, wide_row = env["gr"]
            small = [small[i, : 2 * part_i] for i in range(9)] + [wide_row[0]]
        else:
            me_core = (me, core)

            def cut(value, part):
                return value.reshape(chunks, part, value.shape[1])

            own_o = plain_halving(
                cut(product((act, act_other), (gb_mine, gb_other)), part_o), orders["outer"], *me_core
            )
            own_i = plain_halving(
                cut(product((low1, low_other), (env["gh_mine"], env["gh_pair"])), part_i), orders["inner"], *me_core
            )
            four = [product((x, x_other), (env["g3_mine"][i], env["g3_pair"][i])) for i in range(3)]
            four.append(product((ctx, ctx_other), (env["ga"], env["ga_pair"])))
            four = jnp.stack([cut(f, part_i) for f in four], axis=1)
            own_r = plain_halving(four, orders["rest"], *me_core)

            def both(mine, other):
                return jnp.where(
                    core == 0,
                    jnp.concatenate([mine, other], axis=1),
                    jnp.concatenate([other, mine], axis=1),
                )

            table = jnp.concatenate(
                [
                    both(env["sums0_mine"], env["sums0_other"]),
                    env["sums1"],
                    sums2,
                    both(env["sumi_mine"], env["sumi_other"]).reshape(-1, width),
                ]
            )
            table = lax.psum(table, ("dp", "seq"))
            (g_outer,) = finish(own_o, 1, part_o, width)
            (g_inner,) = finish(own_i, 1, part_i, wide)
            g_query, g_key, g_value, g_output = finish(own_r, 4, part_i, width)
            lines = [table[i] for i in range(9)] + [table[9:].reshape(-1)]
            small = []
            for line in lines:
                n = line.shape[0] // dp
                small.append(lax.dynamic_slice_in_dim(line, lax.axis_index("dp") * n, n))
        return (
            env["outputs"],
            env["inputs"],
            g_query,
            small[0],
            g_key,
            g_value,
            small[2],
            g_output,
            small[5],
            small[3],
            small[4],
            g_inner,
            small[9],
            g_outer,
            small[8],
            small[6],
            small[7],
        )

    return body


def solution(mesh):
    rows = P("dp", "seq", None)
    matrix, vector = P("dp", None), P("dp")
    in_specs = (rows, rows, P("dp", "seq"), *[P()] * 15)
    out_specs = (
        rows,
        rows,
        matrix,
        vector,
        matrix,
        matrix,
        vector,
        matrix,
        vector,
        vector,
        vector,
        matrix,
        vector,
        matrix,
        vector,
        vector,
        vector,
    )
    body = make_body(dict(mesh.shape))
    return jax.shard_map(
        body, mesh=mesh, in_specs=in_specs, out_specs=out_specs, check_vma=False
    )
```

profile of v0, /device:TPU:1, one launch (start us, length us, event | category | flops | bytes accessed | tf_op | source)
XLA Modules:
  0.0 165.0 jit_solution(10641719200992144688)
XLA Ops:
  0.8 1.1 copy-done.5
  1.9 1.6 deal_inputs.1
  3.7 2.7 %collective-permute-start.1 = (bf16[128,768]{1,0:T(8,128)(2,1)S(1)}, bf16[128,768]{1,0:T(8,128)(2,1)S(1)}, u32[]{:S(2)}, u32[]{:S(2)}) collective-permute-start(bf16[128,768]{1,0:T(8,128)(2,1)S(1)} %get-tuple-element.77), channel_id=1, source_target_pairs={{0,2},{1,3},{2,0},{3,1},{4,6},{5,7},{6,4},{7,5},{8,10},{9,11},{10,... | collective-permute-start | bytes 589832 | tf_op jit(solution)/shard_map/ppermute | solution.py:412
  6.7 1.6 deal_cotangent.1
  8.7 1.4 collective-permute-start.4
  10.7 0.8 collective-permute-done.1.refs_2_
  11.5 4.4 %collective-permute-done.2.refs_3_ = bf16[128,768]{1,0:T(8,128)(2,1)S(1)} collective-permute-done((bf16[128,768]{1,0:T(8,128)(2,1)S(1)}, bf16[128,768]{1,0:T(8,128)(2,1)S(1)}, u32[]{:S(2)}, u32[]{:S(2)}) %collective-permute-start.2) | collective-permute-done | bytes 196640 | tf_op jit(solution)/shard_map/ppermute | solution.py:412
  16.0 14.2 %attention.1 = (bf16[512,768]{1,0:T(8,128)(2,1)S(1)}, bf16[512,768]{1,0:T(8,128)(2,1)S(1)}, bf16[512,768]{1,0:T(8,128)(2,1)S(1)}, bf16[512,768]{1,0:T(8,128)(2,1...) custom-call(s32[51]{0:T(128)S(1)} %concatenate.3.info_ref, ...), custom_call_target="tpu_custom_call" | custom-call | flops 38999998464 | bytes 1 | tf_op jit(solution)/shard_map/attention/pallas_call | solution.py:45
  30.3 6.1 %hidden.1 = (bf16[512,3072]{1,0:T(8,128)(2,1)S(1)}, bf16[512,3072]{1,0:T(8,128)(2,1)S(1)}) custom-call(s32[51]{0:T(128)S(1)} %concatenate.3.info_ref, bf16[512,768]{1,0:T(8,128)(2,1)S(1)} %get-tuple-element.79.refs_0_, bf16[768,3072]{1,0:T(8,128)(2,1)S(1)} %bitcast.22, bf16[1,3072]{1,0:T(2,128)(2,1)S(1)} %reshape.71.refs_2_, ...), custom_call_target="tpu_custom_call" | custom-call | flops 27000000512 | bytes 1 | tf_op jit(solution)/shard_map/hidden/pallas_call | solution.py:45
  37.1 4.5 %branch.1 = (bf16[128,768]{1,0:T(8,128)(2,1)S(1)}, bf16[128,768]{1,0:T(8,128)(2,1)S(1)}, bf16[128,768]{1,0:T(8,128)(2,1)S(1)}, bf16[128,768]{1,0:T(8,128)(2,1)S(...) custom-call(s32[51]{0:T(128)S(1)} %concatenate.3.info_ref, ...), custom_call_target="tpu_custom_call" | custom-call | flops 12000000000 | bytes 1 | tf_op jit(solution)/shard_map/branch/pallas_call | solution.py:45
  42.2 1.7 %collective-permute-start.7 = (bf16[128,768]{1,0:T(8,128)(2,1)S(1)}, bf16[128,768]{1,0:T(8,128)(2,1)S(1)}, u32[]{:S(2)}, u32[]{:S(2)}) collective-permute-start(bf16[128,768]{1,0:T(8,128)(2,1)S(1)} %get-tuple-element.88), channel_id=1, source_target_pairs={{0,2},{1,3},{2,0},{3,1},{4,6},{5,7},{6,4},{7,5},{8,10},{9,11},{10,... | collective-permute-start | bytes 589832 | tf_op jit(solution)/shard_map/ppermute | solution.py:412
  44.0 2.0 %hidden_back_other.1 = (bf16[512,1536]{1,0:T(8,128)(2,1)S(1)}, f32[1,1536]{1,0:T(1,128)S(1)}) custom-call(s32[51]{0:T(128)S(1)} %concatenate.3.info_ref, bf16[512,768]{1,0:T(8,128)(2,1)S(1)} %get-tuple-element.92.refs_0_, bf16[3072,768]{1,0:T(8,128)(2,1)S(1)} %bitcast.20, bf16[512,3072]{1,0:T(8,128)(2,1)S(1)} %get-tuple-element.93.refs_2_, ...), custom_call_target="tpu_custom_call" | custom-call | flops 8999999488 | bytes 1 | tf_op jit(solution)/shard_map/hidden_back_other/pallas_call | solution.py:45
  46.4 2.0 %hidden_back_mine.1 = (bf16[512,1536]{1,0:T(8,128)(2,1)S(1)}, f32[1,1536]{1,0:T(1,128)S(1)}) custom-call(s32[51]{0:T(128)S(1)} %concatenate.3.info_ref, bf16[512,768]{1,0:T(8,128)(2,1)S(1)} %get-tuple-element.92.refs_0_, bf16[3072,768]{1,0:T(8,128)(2,1)S(1)} %bitcast.20, bf16[512,3072]{1,0:T(8,128)(2,1)S(1)} %get-tuple-element.93.refs_2_, ...), custom_call_target="tpu_custom_call" | custom-call | flops 8999999488 | bytes 1 | tf_op jit(solution)/shard_map/hidden_back_mine/pallas_call | solution.py:45
  48.5 5.2 %grad_outer.1 = (bf16[1536,384]{1,0:T(8,128)(2,1)S(1)}, bf16[1536,384]{1,0:T(8,128)(2,1)S(1)}) custom-call(s32[51]{0:T(128)S(1)} %concatenate.3.info_ref, bf16[512,3072]{1,0:T(8,128)(2,1)S(1)} %get-tuple-element.84.refs_0_, bf16[512,3072]{1,0:T(8,128)(2,1)S(1)} %collective-permute-done.9.refs_3_.refs_1_, bf16[512,384]{1,0:T(8,128)(2,1)S(1)} %get-tuple-element.90.refs_2_, ...), custom_call_target="tpu_custom_call" | custom-call | flops 15000000512 | bytes 1 | tf_op jit(solution)/shard_map/grad_outer/pallas_call | solution.py:45
  53.7 1.5 collective-permute-start.13
  55.2 1.5 collect_outputs.1.refs_4_
  56.7 1.1 copy-done.8
  57.8 3.3 %grad_inner.1 = (bf16[384,1536]{1,0:T(8,128)(2,1)S(1)}, bf16[384,1536]{1,0:T(8,128)(2,1)S(1)}) custom-call(s32[51]{0:T(128)S(1)} %concatenate.3.info_ref, bf16[512,768]{1,0:T(8,128)(2,1)S(1)} %get-tuple-element.79.refs_0_, bf16[512,768]{1,0:T(8,128)(2,1)S(1)} %collective-permute-done.11.refs_1_, bf16[512,1536]{1,0:T(8,128)(2,1)S(1)} %get-tuple-element.101.refs_2_.refs_0_, ...), custom_call_target="tpu_custom_call" | custom-call | flops 12000000000 | bytes 1 | tf_op jit(solution)/shard_map/grad_inner/pallas_call | solution.py:45
  61.2 5.5 %first_back.1 = (f32[512,768]{1,0:T(8,128)S(1)}, bf16[512,768]{1,0:T(8,128)(2,1)S(1)}, bf16[512,384]{1,0:T(8,128)(2,1)S(1)}, bf16[512,384]{1,0:T(8,128)(2,1)S(1)}, f32[3,768]{1,0:T(4,128)S(1)}) custom-call(s32[51]{0:T(128)S(1)} %concatenate.3.info_ref, bf16[512,1536]{1,0:T(8,128)(2,1)S(1)} %get-tuple-element.101.refs_2_.refs_0_, ...), custom_call_target="tpu_custom_call" | custom-call | flops 17999998976 | bytes 1 | tf_op jit(solution)/shard_map/first_back/pallas_call | solution.py:45
  66.7 5.5 %attention_back_other.1 = (bf16[3,512,384]{2,1,0:T(8,128)(2,1)S(1)}, f32[3,384]{1,0:T(4,128)S(1)}) custom-call(s32[51]{0:T(128)S(1)} %concatenate.3.info_ref, bf16[512,768]{1,0:T(8,128)(2,1)S(1)} %get-tuple-element.97.refs_0_, bf16[512,768]{1,0:T(8,128)(2,1)S(1)} %get-tuple-element.98.refs_1_, bf16[512,768]{1,0:T(8,128)(2,1)S(1)} %get-tuple-element.99.refs_2_, ...), custom_call_target="tpu_custom_call" | custom-call | flops 3000000000 | bytes 1 | tf_op jit(solution)/shard_map/attention_back_other/pallas_call | solution.py:45
  72.3 0.7 collective-permute-start.16
  73.0 0.7 outer0.1.refs_5_
  73.7 0.8 collective-permute-start.18
  74.5 0.9 collective-permute-start.14
  76.0 5.8 %attention_back_mine.1 = (bf16[3,512,384]{2,1,0:T(8,128)(2,1)S(1)}, f32[3,384]{1,0:T(4,128)S(1)}) custom-call(s32[51]{0:T(128)S(1)} %concatenate.3.info_ref, bf16[512,768]{1,0:T(8,128)(2,1)S(1)} %get-tuple-element.97.refs_0_, bf16[512,768]{1,0:T(8,128)(2,1)S(1)} %get-tuple-element.98.refs_1_, bf16[512,768]{1,0:T(8,128)(2,1)S(1)} %get-tuple-element.99.refs_2_, ...), custom_call_target="tpu_custom_call" | custom-call | flops 3000000000 | bytes 1 | tf_op jit(solution)/shard_map/attention_back_mine/pallas_call | solution.py:45
  81.8 1.0 collective-permute-done.18.refs_2_
  82.8 1.2 collective-permute-start.20
  84.0 0.7 outer1.1.refs_14_
  84.8 4.1 %grad_rest.1 = (bf16[1536,384]{1,0:T(8,128)(2,1)S(1)}, bf16[1568,384]{1,0:T(8,128)(2,1)S(1)}, f32[16,768]{1,0:T(8,128)S(1)}) custom-call(s32[51]{0:T(128)S(1)} %concatenate.3.info_ref, bf16[512,768]{1,0:T(8,128)(2,1)S(1)} %get-tuple-element.113.refs_0_, bf16[512,768]{1,0:T(8,128)(2,1)S(1)} %collective-permute-done.14.refs_1_, ...), custom_call_target="tpu_custom_call" | custom-call | flops 3000000000 | bytes 1 | tf_op jit(solution)/shard_map/grad_rest/pallas_call | solution.py:45
  89.2 1.3 collective-permute-start.24
  90.5 7.7 %collective-permute-done.20.refs_1_ = bf16[384,1536]{1,0:T(8,128)(2,1)S(1)} collective-permute-done((bf16[384,1536]{1,0:T(8,128)(2,1)S(1)}, bf16[384,1536]{1,0:T(8,128)(2,1)S(1)}, u32[]{:S(2)}, u32[]{:S(2)}) %collective-permute-start.20) | collective-permute-done | bytes 1179680 | tf_op jit(solution)/shard_map/ppermute | solution.py:439
  98.2 0.7 inner0.1.refs_3_
  98.9 1.4 collective-permute-start.25
  100.2 11.2 %collective-permute-done.19.refs_1_ = bf16[1568,384]{1,0:T(8,128)(2,1)S(1)} collective-permute-done((bf16[1568,384]{1,0:T(8,128)(2,1)S(1)}, bf16[1568,384]{1,0:T(8,128)(2,1)S(1)}, u32[]{:S(2)}, u32[]{:S(2)}) %collective-permute-start.19) | collective-permute-done | bytes 1204256 | tf_op jit(solution)/shard_map/ppermute | solution.py:439
  111.4 0.7 rest0.1.refs_6_.refs_3_
  112.1 0.6 collective-permute-start.28
  112.7 7.2 %input_back.1 = (bf16[128,768]{1,0:T(8,128)(2,1)S(1)}, bf16[128,768]{1,0:T(8,128)(2,1)S(1)}, bf16[128,768]{1,0:T(8,128)(2,1)S(1)}, bf16[128,768]{1,0:T(8,128)(2,1)S(1)}) custom-call(s32[51]{0:T(128)S(1)} %concatenate.3.info_ref, bf16[3,512,384]{2,1,0:T(8,128)(2,1)} %copy-done.12, bf16[3,512,384]{2,1,0:T(8,128)(2,1)} %copy-done.4, f32[512,768]{1,0:T(8,128)} %copy-done.17, ...), custom_call_target="tpu_custom_call" | custom-call | flops 6000000000 | bytes 1 | tf_op jit(solution)/shard_map/input_back/pallas_call | solution.py:45
  120.0 0.7 inner1.1.refs_4_
  120.7 0.9 collective-permute-start.27
  122.3 2.4 %collective-permute-start.26 = (bf16[192,384]{1,0:T(8,128)(2,1)S(1)}, bf16[192,384]{1,0:T(8,128)(2,1)S(1)}, u32[]{:S(2)}, u32[]{:S(2)}) collective-permute-start(bf16[192,384]{1,0:T(8,128)(2,1)S(1)} %outer2.1.refs_4_), channel_id=1, source_target_pairs={{0,16},{1,17},{2,18},{3,19},{4,20},{5,21},{6,22},{7,23},{8,24},{9,... | collective-permute-start | bytes 442376 | tf_op jit(solution)/shard_map/ppermute | solution.py:439
  125.2 1.6 collective-permute-start.23
  126.8 0.7 rest1.1.refs_4_
  127.5 1.9 %collective-permute-start.29 = (bf16[416,384]{1,0:T(8,128)(2,1)S(1)}, bf16[416,384]{1,0:T(8,128)(2,1)S(1)}, u32[]{:S(2)}, u32[]{:S(2)}) collective-permute-start(bf16[416,384]{1,0:T(8,128)(2,1)S(1)} %rest1.1.refs_4_), channel_id=1, source_target_pairs={{0,8},{1,9},{2,10},{3,11},{4,12},{5,13},{6,14},{7,15},{8,0},{9,1},... | collective-permute-start | bytes 958472 | tf_op jit(solution)/shard_map/ppermute | solution.py:439
  129.9 0.6 outer3.1.refs_4_.refs_0_
  130.6 1.0 collective-permute-start.32
  131.9 1.6 collective-permute-start.31
  133.5 3.2 %collective-permute-done.23.refs_3_ = bf16[128,768]{1,0:T(8,128)(2,1)S(1)} collective-permute-done((bf16[128,768]{1,0:T(8,128)(2,1)S(1)}, bf16[128,768]{1,0:T(8,128)(2,1)S(1)}, u32[]{:S(2)}, u32[]{:S(2)}) %collective-permute-start.23) | collective-permute-done | bytes 196640 | tf_op jit(solution)/shard_map/ppermute | solution.py:412
  136.7 1.5 collect_inputs.1.refs_5_
  138.2 1.1 collective-permute-start.34
  139.3 1.1 copy-done.9
  141.1 1.2 collective-permute-start.30
  142.3 1.6 finish_outer.1.refs_5_
  144.0 1.3 copy-done.6
  145.2 0.6 inner3.1.refs_6_.refs_0_
  145.9 1.0 collective-permute-start.38
  146.9 4.9 %collective-permute-done.30.refs_4_ = bf16[224,384]{1,0:T(8,128)(2,1)S(1)} collective-permute-done((bf16[224,384]{1,0:T(8,128)(2,1)S(1)}, bf16[224,384]{1,0:T(8,128)(2,1)S(1)}, u32[]{:S(2)}, u32[]{:S(2)}) %collective-permute-start.30) | collective-permute-done | bytes 172064 | tf_op jit(solution)/shard_map/ppermute | solution.py:439
  151.7 0.7 rest3.1.refs_4_.refs_0_
  152.4 0.8 collective-permute-start.35
  153.2 1.4 collective-permute-start.39
  155.1 2.5 %collective-permute-done.35.refs_1_ = bf16[224,384]{1,0:T(8,128)(2,1)S(1)} collective-permute-done((bf16[224,384]{1,0:T(8,128)(2,1)S(1)}, bf16[224,384]{1,0:T(8,128)(2,1)S(1)}, u32[]{:S(2)}, u32[]{:S(2)}) %collective-permute-start.35) | collective-permute-done | bytes 172064 | tf_op jit(solution)/shard_map/ppermute | solution.py:412
  157.6 1.7 %collective-permute-start.37 = (bf16[224,384]{1,0:T(8,128)(2,1)S(1)}, bf16[224,384]{1,0:T(8,128)(2,1)S(1)}, u32[]{:S(2)}, u32[]{:S(2)}) collective-permute-start(bf16[224,384]{1,0:T(8,128)(2,1)S(1)} %collective-permute-done.35.refs_1_), channel_id=1, source_target_pairs={{0,1},{1,0},{2,3},{3,2},{4,5},{5,4},{6,7},{7,6},{8,9},{9,8},{10,11... | collective-permute-start | bytes 516104 | tf_op jit(solution)/shard_map/ppermute | solution.py:412
  159.3 1.6 finish_inner.1.refs_4_
  160.9 1.3 copy-done.7
  162.2 1.7 %finish_rest.1 = (f32[96,768]{1,0:T(8,128)}, f32[96,768]{1,0:T(8,128)}, f32[96,768]{1,0:T(8,128)}, f32[96,768]{1,0:T(8,128)}, f32[16,128]{1,0:T(8,128)S(1)}, /*index=5*/f32[1,384]{1,0:T(1,128)S(1)}) custom-call(s32[51]{0:T(128)S(1)} %concatenate.3.info_ref, bf16[224,384]{1,0:T(8,128)(2,1)S(1)} %rest3.1.refs_4_.refs_0_, ...), custom_call_target="tpu_custom_call" | custom-call | flops 3000000000 | bytes 1 | tf_op jit(solution)/shard_map/finish_rest/pallas_call | solution.py:45
  (140 shorter events, 8.4 us)
Async XLA Ops:
  1.9 4.5 %copy-start.24 = (s32[4,128]{1,0:T(4,128)S(1)}, s32[4,128]{1,0:T(4,128)}, u32[]{:S(2)}) copy-start(s32[4,128]{1,0:T(4,128)} %param.20) | copy-start | bytes 6148
  1.9 4.5 %copy-start.22 = (bf16[4,128,768]{2,1,0:T(8,128)(2,1)S(1)}, bf16[4,128,768]{2,1,0:T(8,128)(2,1)}, u32[]{:S(2)}) copy-start(bf16[4,128,768]{2,1,0:T(8,128)(2,1)} %param.19) | copy-start | bytes 2359300
  1.9 14.1 %copy-start.3 = (bf16[768,768]{1,0:T(8,128)(2,1)S(1)}, bf16[768,768]{1,0:T(8,128)(2,1)}, u32[]{:S(2)}) copy-start(bf16[768,768]{1,0:T(8,128)(2,1)} %refs_5_.1) | copy-start | bytes 3538948
  3.5 6.8 %collective-permute-start = (bf16[128,768]{1,0:T(8,128)(2,1)S(1)}, bf16[128,768]{1,0:T(8,128)(2,1)S(1)}, u32[]{:S(2)}, u32[]{:S(2)}) collective-permute-start(bf16[128,768]{1,0:T(8,128)(2,1)S(1)} %get-tuple-element.76), channel_id=1, source_target_pairs={{0,1},{1,0},{2,3},{3,2},{4,5},{5,4},{6,7},{7,6},{8,9},{9,8},{10,11... | collective-permute-start | bytes 589832 | tf_op jit(solution)/shard_map/ppermute | solution.py:412
  3.7 7.9 %collective-permute-start.1 = (bf16[128,768]{1,0:T(8,128)(2,1)S(1)}, bf16[128,768]{1,0:T(8,128)(2,1)S(1)}, u32[]{:S(2)}, u32[]{:S(2)}) collective-permute-start(bf16[128,768]{1,0:T(8,128)(2,1)S(1)} %get-tuple-element.77), channel_id=1, source_target_pairs={{0,2},{1,3},{2,0},{3,1},{4,6},{5,7},{6,4},{7,5},{8,10},{9,11},{10,... | collective-permute-start | bytes 589832 | tf_op jit(solution)/shard_map/ppermute | solution.py:412
  6.4 9.6 %collective-permute-start.2 = (bf16[128,768]{1,0:T(8,128)(2,1)S(1)}, bf16[128,768]{1,0:T(8,128)(2,1)S(1)}, u32[]{:S(2)}, u32[]{:S(2)}) collective-permute-start(bf16[128,768]{1,0:T(8,128)(2,1)S(1)} %get-tuple-element.78), channel_id=1, source_target_pairs={{0,3},{1,2},{2,1},{3,0},{4,7},{5,6},{6,5},{7,4},{8,11},{9,10},{10,... | collective-permute-start | bytes 589832 | tf_op jit(solution)/shard_map/ppermute | solution.py:412
  6.4 9.6 %copy-start.2 = (bf16[768,768]{1,0:T(8,128)(2,1)S(1)}, bf16[768,768]{1,0:T(8,128)(2,1)}, u32[]{:S(2)}) copy-start(bf16[768,768]{1,0:T(8,128)(2,1)} %refs_4_.1) | copy-start | bytes 3538948
  6.6 3.6 %copy-start.28 = (bf16[768]{0:T(1024)(128)(2,1)S(1)}, bf16[768]{0:T(1024)(128)(2,1)}, u32[]{:S(2)}) copy-start(bf16[768]{0:T(1024)(128)(2,1)} %param.25) | copy-start | bytes 4612
  6.6 3.6 %copy-start.29 = (bf16[768]{0:T(1024)(128)(2,1)S(1)}, bf16[768]{0:T(1024)(128)(2,1)}, u32[]{:S(2)}) copy-start(bf16[768]{0:T(1024)(128)(2,1)} %param.27) | copy-start | bytes 4612
  6.6 3.7 %copy-start.23 = (bf16[3072]{0:T(1024)(128)(2,1)S(1)}, bf16[3072]{0:T(1024)(128)(2,1)}, u32[]{:S(2)}) copy-start(bf16[3072]{0:T(1024)(128)(2,1)} %param.31) | copy-start | bytes 18436
  6.6 9.3 %copy-start = (bf16[768,768]{1,0:T(8,128)(2,1)S(1)}, bf16[768,768]{1,0:T(8,128)(2,1)}, u32[]{:S(2)}) copy-start(bf16[768,768]{1,0:T(8,128)(2,1)} %refs_7_.1) | copy-start | bytes 3538948
  6.7 9.3 %copy-start.1 = (bf16[768,768]{1,0:T(8,128)(2,1)S(1)}, bf16[768,768]{1,0:T(8,128)(2,1)}, u32[]{:S(2)}) copy-start(bf16[768,768]{1,0:T(8,128)(2,1)} %refs_3_.1) | copy-start | bytes 3538948
  6.7 23.6 %slice-start.2 = ((s8[4718592]{0:T(1024)(128)(4,1)}), s8[4194304]{0:T(1024)(128)(4,1)S(1)}, s32[]{:S(2)}) async-start(s8[4718592]{0:T(1024)(128)(4,1)} %bitcast.21), calls=%async_computation.2 | async-start | bytes 8388608
  6.7 30.4 %slice-start = ((s8[4718592]{0:T(1024)(128)(4,1)}), s8[4194304]{0:T(1024)(128)(4,1)S(1)}, s32[]{:S(2)}) async-start(s8[4718592]{0:T(1024)(128)(4,1)} %bitcast.19), calls=%async_computation | async-start | bytes 8388608
  8.3 21.9 %collective-permute-start.3 = (bf16[128,768]{1,0:T(8,128)(2,1)S(1)}, bf16[128,768]{1,0:T(8,128)(2,1)S(1)}, u32[]{:S(2)}, u32[]{:S(2)}) collective-permute-start(bf16[128,768]{1,0:T(8,128)(2,1)S(1)} %get-tuple-element.81), channel_id=1, source_target_pairs={{0,1},{1,0},{2,3},{3,2},{4,5},{5,4},{6,7},{7,6},{8,9},{9,8},{10,11... | collective-permute-start | bytes 589832 | tf_op jit(solution)/shard_map/ppermute | solution.py:412
  8.7 21.5 %collective-permute-start.4 = (bf16[128,768]{1,0:T(8,128)(2,1)S(1)}, bf16[128,768]{1,0:T(8,128)(2,1)S(1)}, u32[]{:S(2)}, u32[]{:S(2)}) collective-permute-start(bf16[128,768]{1,0:T(8,128)(2,1)S(1)} %get-tuple-element.82), channel_id=1, source_target_pairs={{0,2},{1,3},{2,0},{3,1},{4,6},{5,7},{6,4},{7,5},{8,10},{9,11},{10,... | collective-permute-start | bytes 589832 | tf_op jit(solution)/shard_map/ppermute | solution.py:412
  10.3 19.9 %collective-permute-start.5 = (bf16[128,768]{1,0:T(8,128)(2,1)S(1)}, bf16[128,768]{1,0:T(8,128)(2,1)S(1)}, u32[]{:S(2)}, u32[]{:S(2)}) collective-permute-start(bf16[128,768]{1,0:T(8,128)(2,1)S(1)} %get-tuple-element.83), channel_id=1, source_target_pairs={{0,3},{1,2},{2,1},{3,0},{4,7},{5,6},{6,5},{7,4},{8,11},{9,10},{10,... | collective-permute-start | bytes 589832 | tf_op jit(solution)/shard_map/ppermute | solution.py:412
  16.0 14.3 %slice-start.3 = ((s8[4718592]{0:T(1024)(128)(4,1)}), s8[524288]{0:T(1024)(128)(4,1)S(1)}, s32[]{:S(2)}) async-start(s8[4718592]{0:T(1024)(128)(4,1)} %bitcast.21), calls=%async_computation.3 | async-start | bytes 1048576
  16.0 21.1 %slice-start.1 = ((s8[4718592]{0:T(1024)(128)(4,1)}), s8[524288]{0:T(1024)(128)(4,1)S(1)}, s32[]{:S(2)}) async-start(s8[4718592]{0:T(1024)(128)(4,1)} %bitcast.19), calls=%async_computation.1 | async-start | bytes 1048576
  30.2 6.9 %copy-start.18 = (f32[512,768]{1,0:T(8,128)}, f32[512,768]{1,0:T(8,128)S(1)}, u32[]{:S(2)}) copy-start(f32[512,768]{1,0:T(8,128)S(1)} %get-tuple-element.85.refs_3_.refs_4_) | copy-start | bytes 4718596
  30.2 36.5 %copy-start.10 = (bf16[12,512,512]{2,1,0:T(8,128)(2,1)}, bf16[12,512,512]{2,1,0:T(8,128)(2,1)S(1)}, u32[]{:S(2)}) copy-start(bf16[12,512,512]{2,1,0:T(8,128)(2,1)S(1)} %get-tuple-element.100.refs_3_) | copy-start | bytes 18874372
  30.3 6.3 %copy-start.30 = (bf16[768]{0:T(1024)(128)(2,1)S(1)}, bf16[768]{0:T(1024)(128)(2,1)}, u32[]{:S(2)}) copy-start(bf16[768]{0:T(1024)(128)(2,1)} %param.33) | copy-start | bytes 4612
  30.3 6.3 %copy-start.31 = (bf16[768]{0:T(1024)(128)(2,1)S(1)}, bf16[768]{0:T(1024)(128)(2,1)}, u32[]{:S(2)}) copy-start(bf16[768]{0:T(1024)(128)(2,1)} %param.34) | copy-start | bytes 4612
  30.3 6.3 %copy-start.32 = (bf16[768]{0:T(1024)(128)(2,1)S(1)}, bf16[768]{0:T(1024)(128)(2,1)}, u32[]{:S(2)}) copy-start(bf16[768]{0:T(1024)(128)(2,1)} %param.35) | copy-start | bytes 4612
  36.4 7.5 %collective-permute-start.9 = (bf16[512,3072]{1,0:T(8,128)(2,1)S(1)}, bf16[512,3072]{1,0:T(8,128)(2,1)S(1)}, u32[]{:S(2)}, u32[]{:S(2)}) collective-permute-start(bf16[512,3072]{1,0:T(8,128)(2,1)S(1)} %get-tuple-element.84.refs_0_), channel_id=1, source_target_pairs={{0,1},{1,0},{2,3},{3,2},{4,5},{5,4},{6,7},{7,6},{8,9},{9,8},{10,11... | collective-permute-start | bytes 9437192 | tf_op jit(solution)/shard_map/ppermute | solution.py:412
  36.7 20.0 %collective-permute-start.11 = (bf16[512,768]{1,0:T(8,128)(2,1)S(1)}, bf16[512,768]{1,0:T(8,128)(2,1)S(1)}, u32[]{:S(2)}, u32[]{:S(2)}) collective-permute-start(bf16[512,768]{1,0:T(8,128)(2,1)S(1)} %get-tuple-element.79.refs_0_), channel_id=1, source_target_pairs={{0,1},{1,0},{2,3},{3,2},{4,5},{5,4},{6,7},{7,6},{8,9},{9,8},{10,11... | collective-permute-start | bytes 2359304 | tf_op jit(solution)/shard_map/ppermute | solution.py:412
  41.6 4.5 %copy-start.20 = (f32[512,768]{1,0:T(8,128)}, f32[512,768]{1,0:T(8,128)S(1)}, u32[]{:S(2)}) copy-start(f32[512,768]{1,0:T(8,128)S(1)} %get-tuple-element.103.refs_3_) | copy-start | bytes 4718596
  41.6 4.5 %collective-permute-start.10 = (bf16[512,384]{1,0:T(8,128)(2,1)S(1)}, bf16[512,384]{1,0:T(8,128)(2,1)S(1)}, u32[]{:S(2)}, u32[]{:S(2)}) collective-permute-start(bf16[512,384]{1,0:T(8,128)(2,1)S(1)} %get-tuple-element.91), channel_id=1, source_target_pairs={{0,1},{1,0},{2,3},{3,2},{4,5},{5,4},{6,7},{7,6},{8,9},{9,8},{10,11... | collective-permute-start | bytes 1179656 | tf_op jit(solution)/shard_map/ppermute | solution.py:412
  41.9 11.9 %collective-permute-start.6 = (bf16[128,768]{1,0:T(8,128)(2,1)S(1)}, bf16[128,768]{1,0:T(8,128)(2,1)S(1)}, u32[]{:S(2)}, u32[]{:S(2)}) collective-permute-start(bf16[128,768]{1,0:T(8,128)(2,1)S(1)} %get-tuple-element.87), channel_id=1, source_target_pairs={{0,1},{1,0},{2,3},{3,2},{4,5},{5,4},{6,7},{7,6},{8,9},{9,8},{10,11... | collective-permute-start | bytes 589832 | tf_op jit(solution)/shard_map/ppermute | solution.py:412
  42.2 13.0 %collective-permute-start.7 = (bf16[128,768]{1,0:T(8,128)(2,1)S(1)}, bf16[128,768]{1,0:T(8,128)(2,1)S(1)}, u32[]{:S(2)}, u32[]{:S(2)}) collective-permute-start(bf16[128,768]{1,0:T(8,128)(2,1)S(1)} %get-tuple-element.88), channel_id=1, source_target_pairs={{0,2},{1,3},{2,0},{3,1},{4,6},{5,7},{6,4},{7,5},{8,10},{9,11},{10,... | collective-permute-start | bytes 589832 | tf_op jit(solution)/shard_map/ppermute | solution.py:412
  43.9 11.3 %collective-permute-start.8 = (bf16[128,768]{1,0:T(8,128)(2,1)S(1)}, bf16[128,768]{1,0:T(8,128)(2,1)S(1)}, u32[]{:S(2)}, u32[]{:S(2)}) collective-permute-start(bf16[128,768]{1,0:T(8,128)(2,1)S(1)} %get-tuple-element.89), channel_id=1, source_target_pairs={{0,3},{1,2},{2,1},{3,0},{4,7},{5,6},{6,5},{7,4},{8,11},{9,10},{10,... | collective-permute-start | bytes 589832 | tf_op jit(solution)/shard_map/ppermute | solution.py:412
  46.1 10.6 %collective-permute-start.12 = (bf16[512,1536]{1,0:T(8,128)(2,1)S(1)}, bf16[512,1536]{1,0:T(8,128)(2,1)S(1)}, u32[]{:S(2)}, u32[]{:S(2)}) collective-permute-start(bf16[512,1536]{1,0:T(8,128)(2,1)S(1)} %get-tuple-element.102.refs_1_), channel_id=1, source_target_pairs={{0,1},{1,0},{2,3},{3,2},{4,5},{5,4},{6,7},{7,6},{8,9},{9,8},{10,11... | collective-permute-start | bytes 4718600 | tf_op jit(solution)/shard_map/ppermute | solution.py:412
  53.7 30.3 %copy-start.15 = (bf16[1536,384]{1,0:T(8,128)(2,1)}, bf16[1536,384]{1,0:T(8,128)(2,1)S(1)}, u32[]{:S(2)}) copy-start(bf16[1536,384]{1,0:T(8,128)(2,1)S(1)} %get-tuple-element.107.refs_0_) | copy-start | bytes 3538948
  53.7 19.3 %collective-permute-start.13 = (bf16[1536,384]{1,0:T(8,128)(2,1)S(1)}, bf16[1536,384]{1,0:T(8,128)(2,1)S(1)}, u32[]{:S(2)}, u32[]{:S(2)}) collective-permute-start(bf16[1536,384]{1,0:T(8,128)(2,1)S(1)} %get-tuple-element.96.refs_4_), channel_id=1, source_target_pairs={{0,2},{1,5},{2,0},{3,7},{4,6},{5,1},{6,4},{7,3},{8,10},{9,13},{10,... | collective-permute-start | bytes 3538952 | tf_op jit(solution)/shard_map/ppermute | solution.py:439
  61.2 37.0 %copy-start.13 = (bf16[384,1536]{1,0:T(8,128)(2,1)}, bf16[384,1536]{1,0:T(8,128)(2,1)S(1)}, u32[]{:S(2)}) copy-start(bf16[384,1536]{1,0:T(8,128)(2,1)S(1)} %get-tuple-element.121.refs_0_) | copy-start | bytes 3538948
  66.7 5.6 %copy-start.17 = (f32[512,768]{1,0:T(8,128)}, f32[512,768]{1,0:T(8,128)S(1)}, u32[]{:S(2)}) copy-start(f32[512,768]{1,0:T(8,128)S(1)} %get-tuple-element.112.refs_2_) | copy-start | bytes 4718596
  72.3 12.5 %collective-permute-start.16 = (bf16[3,512,384]{2,1,0:T(8,128)(2,1)S(1)}, bf16[3,512,384]{2,1,0:T(8,128)(2,1)S(1)}, u32[]{:S(2)}, u32[]{:S(2)}) collective-permute-start(bf16[3,512,384]{2,1,0:T(8,128)(2,1)S(1)} %get-tuple-element.111.refs_1_), channel_id=1, source_target_pairs={{0,1},{1,0},{2,3},{3,2},{4,5},{5,4},{6,7},{7,6},{8,9},{9,8},{10,11... | collective-permute-start | bytes 3538952 | tf_op jit(solution)/shard_map/ppermute | solution.py:412
  73.7 9.1 %collective-permute-start.18 = (bf16[768,384]{1,0:T(8,128)(2,1)S(1)}, bf16[768,384]{1,0:T(8,128)(2,1)S(1)}, u32[]{:S(2)}, u32[]{:S(2)}) collective-permute-start(bf16[768,384]{1,0:T(8,128)(2,1)S(1)} %outer0.1.refs_5_), channel_id=1, source_target_pairs={{0,4},{1,3},{2,6},{3,1},{4,0},{5,7},{6,2},{7,5},{8,12},{9,11},{10,... | collective-permute-start | bytes 1769480 | tf_op jit(solution)/shard_map/ppermute | solution.py:439
  74.5 10.2 %collective-permute-start.14 = (bf16[512,768]{1,0:T(8,128)(2,1)S(1)}, bf16[512,768]{1,0:T(8,128)(2,1)S(1)}, u32[]{:S(2)}, u32[]{:S(2)}) collective-permute-start(bf16[512,768]{1,0:T(8,128)(2,1)S(1)} %get-tuple-element.113.refs_0_), channel_id=1, source_target_pairs={{0,1},{1,0},{2,3},{3,2},{4,5},{5,4},{6,7},{7,6},{8,9},{9,8},{10,11... | collective-permute-start | bytes 2359304 | tf_op jit(solution)/shard_map/ppermute | solution.py:412
  75.5 9.3 %collective-permute-start.15 = (bf16[512,768]{1,0:T(8,128)(2,1)S(1)}, bf16[512,768]{1,0:T(8,128)(2,1)S(1)}, u32[]{:S(2)}, u32[]{:S(2)}) collective-permute-start(bf16[512,768]{1,0:T(8,128)(2,1)S(1)} %get-tuple-element.114.refs_2_), channel_id=1, source_target_pairs={{0,1},{1,0},{2,3},{3,2},{4,5},{5,4},{6,7},{7,6},{8,9},{9,8},{10,11... | collective-permute-start | bytes 2359304 | tf_op jit(solution)/shard_map/ppermute | solution.py:412
  75.5 9.3 %collective-permute-start.17 = (bf16[512,384]{1,0:T(8,128)(2,1)S(1)}, bf16[512,384]{1,0:T(8,128)(2,1)S(1)}, u32[]{:S(2)}, u32[]{:S(2)}) collective-permute-start(bf16[512,384]{1,0:T(8,128)(2,1)S(1)} %get-tuple-element.116), channel_id=1, source_target_pairs={{0,1},{1,0},{2,3},{3,2},{4,5},{5,4},{6,7},{7,6},{8,9},{9,8},{10,11... | collective-permute-start | bytes 1179656 | tf_op jit(solution)/shard_map/ppermute | solution.py:412
  82.8 15.3 %collective-permute-start.20 = (bf16[384,1536]{1,0:T(8,128)(2,1)S(1)}, bf16[384,1536]{1,0:T(8,128)(2,1)S(1)}, u32[]{:S(2)}, u32[]{:S(2)}) collective-permute-start(bf16[384,1536]{1,0:T(8,128)(2,1)S(1)} %get-tuple-element.105.refs_8_), channel_id=1, source_target_pairs={{0,8},{1,5},{2,10},{3,7},{4,12},{5,1},{6,14},{7,3},{8,0},{9,13},{1... | collective-permute-start | bytes 3538952 | tf_op jit(solution)/shard_map/ppermute | solution.py:439
  88.9 22.5 %collective-permute-start.19 = (bf16[1568,384]{1,0:T(8,128)(2,1)S(1)}, bf16[1568,384]{1,0:T(8,128)(2,1)S(1)}, u32[]{:S(2)}, u32[]{:S(2)}) collective-permute-start(bf16[1568,384]{1,0:T(8,128)(2,1)S(1)} %get-tuple-element.120.refs_2_), channel_id=1, source_target_pairs={{0,2},{1,5},{2,0},{3,7},{4,6},{5,1},{6,4},{7,3},{8,10},{9,13},{10,... | collective-permute-start | bytes 3612680 | tf_op jit(solution)/shard_map/ppermute | solution.py:439
  89.2 32.5 %collective-permute-start.24 = (bf16[384,384]{1,0:T(8,128)(2,1)S(1)}, bf16[384,384]{1,0:T(8,128)(2,1)S(1)}, u32[]{:S(2)}, u32[]{:S(2)}) collective-permute-start(bf16[384,384]{1,0:T(8,128)(2,1)S(1)} %outer1.1.refs_14_), channel_id=1, source_target_pairs={{0,8},{1,9},{2,10},{3,11},{4,12},{5,13},{6,14},{7,15},{8,0},{9,1},... | collective-permute-start | bytes 884744 | tf_op jit(solution)/shard_map/ppermute | solution.py:439
  98.9 21.1 %collective-permute-start.25 = (bf16[192,1536]{1,0:T(8,128)(2,1)S(1)}, bf16[192,1536]{1,0:T(8,128)(2,1)S(1)}, u32[]{:S(2)}, u32[]{:S(2)}) collective-permute-start(bf16[192,1536]{1,0:T(8,128)(2,1)S(1)} %inner0.1.refs_3_), channel_id=1, source_target_pairs={{0,2},{1,9},{2,0},{3,11},{4,6},{5,13},{6,4},{7,15},{8,10},{9,1},{1... | collective-permute-start | bytes 1769480 | tf_op jit(solution)/shard_map/ppermute | solution.py:439
  112.1 13.1 %collective-permute-start.28 = (bf16[800,384]{1,0:T(8,128)(2,1)S(1)}, bf16[800,384]{1,0:T(8,128)(2,1)S(1)}, u32[]{:S(2)}, u32[]{:S(2)}) collective-permute-start(bf16[800,384]{1,0:T(8,128)(2,1)S(1)} %rest0.1.refs_6_.refs_3_), channel_id=1, source_target_pairs={{0,4},{1,3},{2,6},{3,1},{4,0},{5,7},{6,2},{7,5},{8,12},{9,11},{10,... | collective-permute-start | bytes 1843208 | tf_op jit(solution)/shard_map/ppermute | solution.py:439
  112.7 7.3 %copy-start.14 = (bf16[384,1536]{1,0:T(8,128)(2,1)S(1)}, bf16[384,1536]{1,0:T(8,128)(2,1)}, u32[]{:S(2)}) copy-start(bf16[384,1536]{1,0:T(8,128)(2,1)} %copy-done.13) | copy-start | bytes 3538948
  120.7 6.8 %collective-permute-start.27 = (bf16[96,1536]{1,0:T(8,128)(2,1)S(1)}, bf16[96,1536]{1,0:T(8,128)(2,1)S(1)}, u32[]{:S(2)}, u32[]{:S(2)}) collective-permute-start(bf16[96,1536]{1,0:T(8,128)(2,1)S(1)} %inner1.1.refs_4_), channel_id=1, source_target_pairs={{0,4},{1,3},{2,6},{3,1},{4,0},{5,7},{6,2},{7,5},{8,12},{9,11},{10,... | collective-permute-start | bytes 884744 | tf_op jit(solution)/shard_map/ppermute | solution.py:439
  122.3 7.7 %collective-permute-start.26 = (bf16[192,384]{1,0:T(8,128)(2,1)S(1)}, bf16[192,384]{1,0:T(8,128)(2,1)S(1)}, u32[]{:S(2)}, u32[]{:S(2)}) collective-permute-start(bf16[192,384]{1,0:T(8,128)(2,1)S(1)} %outer2.1.refs_4_), channel_id=1, source_target_pairs={{0,16},{1,17},{2,18},{3,19},{4,20},{5,21},{6,22},{7,23},{8,24},{9,... | collective-permute-start | bytes 442376 | tf_op jit(solution)/shard_map/ppermute | solution.py:439
  124.6 7.0 %collective-permute-start.21 = (bf16[128,768]{1,0:T(8,128)(2,1)S(1)}, bf16[128,768]{1,0:T(8,128)(2,1)S(1)}, u32[]{:S(2)}, u32[]{:S(2)}) collective-permute-start(bf16[128,768]{1,0:T(8,128)(2,1)S(1)} %get-tuple-element.124), channel_id=1, source_target_pairs={{0,1},{1,0},{2,3},{3,2},{4,5},{5,4},{6,7},{7,6},{8,9},{9,8},{10,11... | collective-permute-start | bytes 589832 | tf_op jit(solution)/shard_map/ppermute | solution.py:412
  124.6 7.2 %collective-permute-start.22 = (bf16[128,768]{1,0:T(8,128)(2,1)S(1)}, bf16[128,768]{1,0:T(8,128)(2,1)S(1)}, u32[]{:S(2)}, u32[]{:S(2)}) collective-permute-start(bf16[128,768]{1,0:T(8,128)(2,1)S(1)} %get-tuple-element.125), channel_id=1, source_target_pairs={{0,2},{1,3},{2,0},{3,1},{4,6},{5,7},{6,4},{7,5},{8,10},{9,11},{10,... | collective-permute-start | bytes 589832 | tf_op jit(solution)/shard_map/ppermute | solution.py:412
  125.2 11.5 %collective-permute-start.23 = (bf16[128,768]{1,0:T(8,128)(2,1)S(1)}, bf16[128,768]{1,0:T(8,128)(2,1)S(1)}, u32[]{:S(2)}, u32[]{:S(2)}) collective-permute-start(bf16[128,768]{1,0:T(8,128)(2,1)S(1)} %get-tuple-element.126), channel_id=1, source_target_pairs={{0,3},{1,2},{2,1},{3,0},{4,7},{5,6},{6,5},{7,4},{8,11},{9,10},{10,... | collective-permute-start | bytes 589832 | tf_op jit(solution)/shard_map/ppermute | solution.py:412
  127.5 11.9 %collective-permute-start.29 = (bf16[416,384]{1,0:T(8,128)(2,1)S(1)}, bf16[416,384]{1,0:T(8,128)(2,1)S(1)}, u32[]{:S(2)}, u32[]{:S(2)}) collective-permute-start(bf16[416,384]{1,0:T(8,128)(2,1)S(1)} %rest1.1.refs_4_), channel_id=1, source_target_pairs={{0,8},{1,9},{2,10},{3,11},{4,12},{5,13},{6,14},{7,15},{8,0},{9,1},... | collective-permute-start | bytes 958472 | tf_op jit(solution)/shard_map/ppermute | solution.py:439
  130.6 7.6 %collective-permute-start.32 = (bf16[192,384]{1,0:T(8,128)(2,1)S(1)}, bf16[192,384]{1,0:T(8,128)(2,1)S(1)}, u32[]{:S(2)}, u32[]{:S(2)}) collective-permute-start(bf16[192,384]{1,0:T(8,128)(2,1)S(1)} %outer3.1.refs_4_.refs_0_), channel_id=1, source_target_pairs={{0,2},{1,3},{2,0},{3,1},{4,6},{5,7},{6,4},{7,5},{8,10},{9,11},{10,... | collective-permute-start | bytes 442376 | tf_op jit(solution)/shard_map/ppermute | solution.py:412
  131.6 10.7 %collective-permute-start.33 = (bf16[192,384]{1,0:T(8,128)(2,1)S(1)}, bf16[192,384]{1,0:T(8,128)(2,1)S(1)}, u32[]{:S(2)}, u32[]{:S(2)}) collective-permute-start(bf16[192,384]{1,0:T(8,128)(2,1)S(1)} %outer3.1.refs_4_.refs_0_), channel_id=1, source_target_pairs={{0,1},{1,0},{2,3},{3,2},{4,5},{5,4},{6,7},{7,6},{8,9},{9,8},{10,11... | collective-permute-start | bytes 442376 | tf_op jit(solution)/shard_map/ppermute | solution.py:412
  131.9 12.1 %collective-permute-start.31 = (bf16[48,1536]{1,0:T(8,128)(2,1)S(1)}, bf16[48,1536]{1,0:T(8,128)(2,1)S(1)}, u32[]{:S(2)}, u32[]{:S(2)}) collective-permute-start(bf16[48,1536]{1,0:T(8,128)(2,1)S(1)} %inner2.1.refs_5_), channel_id=1, source_target_pairs={{0,16},{1,17},{2,18},{3,19},{4,20},{5,21},{6,22},{7,23},{8,24},{9,... | collective-permute-start | bytes 442376 | tf_op jit(solution)/shard_map/ppermute | solution.py:439
  138.2 4.1 %collective-permute-start.34 = (bf16[192,384]{1,0:T(8,128)(2,1)S(1)}, bf16[192,384]{1,0:T(8,128)(2,1)S(1)}, u32[]{:S(2)}, u32[]{:S(2)}) collective-permute-start(bf16[192,384]{1,0:T(8,128)(2,1)S(1)} %collective-permute-done.32.refs_1_), channel_id=1, source_target_pairs={{0,1},{1,0},{2,3},{3,2},{4,5},{5,4},{6,7},{7,6},{8,9},{9,8},{10,11... | collective-permute-start | bytes 442376 | tf_op jit(solution)/shard_map/ppermute | solution.py:412
  141.1 10.6 %collective-permute-start.30 = (bf16[224,384]{1,0:T(8,128)(2,1)S(1)}, bf16[224,384]{1,0:T(8,128)(2,1)S(1)}, u32[]{:S(2)}, u32[]{:S(2)}) collective-permute-start(bf16[224,384]{1,0:T(8,128)(2,1)S(1)} %rest2.1.refs_4_.refs_5_), channel_id=1, source_target_pairs={{0,16},{1,17},{2,18},{3,19},{4,20},{5,21},{6,22},{7,23},{8,24},{9,... | collective-permute-start | bytes 516104 | tf_op jit(solution)/shard_map/ppermute | solution.py:439
  145.9 8.7 %collective-permute-start.38 = (bf16[48,1536]{1,0:T(8,128)(2,1)S(1)}, bf16[48,1536]{1,0:T(8,128)(2,1)S(1)}, u32[]{:S(2)}, u32[]{:S(2)}) collective-permute-start(bf16[48,1536]{1,0:T(8,128)(2,1)S(1)} %inner3.1.refs_6_.refs_0_), channel_id=1, source_target_pairs={{0,2},{1,3},{2,0},{3,1},{4,6},{5,7},{6,4},{7,5},{8,10},{9,11},{10,... | collective-permute-start | bytes 442376 | tf_op jit(solution)/shard_map/ppermute | solution.py:412
  152.4 5.2 %collective-permute-start.35 = (bf16[224,384]{1,0:T(8,128)(2,1)S(1)}, bf16[224,384]{1,0:T(8,128)(2,1)S(1)}, u32[]{:S(2)}, u32[]{:S(2)}) collective-permute-start(bf16[224,384]{1,0:T(8,128)(2,1)S(1)} %rest3.1.refs_4_.refs_0_), channel_id=1, source_target_pairs={{0,2},{1,3},{2,0},{3,1},{4,6},{5,7},{6,4},{7,5},{8,10},{9,11},{10,... | collective-permute-start | bytes 516104 | tf_op jit(solution)/shard_map/ppermute | solution.py:412
  153.2 6.1 %collective-permute-start.39 = (bf16[48,1536]{1,0:T(8,128)(2,1)S(1)}, bf16[48,1536]{1,0:T(8,128)(2,1)S(1)}, u32[]{:S(2)}, u32[]{:S(2)}) collective-permute-start(bf16[48,1536]{1,0:T(8,128)(2,1)S(1)} %inner3.1.refs_6_.refs_0_), channel_id=1, source_target_pairs={{0,1},{1,0},{2,3},{3,2},{4,5},{5,4},{6,7},{7,6},{8,9},{9,8},{10,11... | collective-permute-start | bytes 442376 | tf_op jit(solution)/shard_map/ppermute | solution.py:412
  154.6 4.7 %collective-permute-start.40 = (bf16[48,1536]{1,0:T(8,128)(2,1)S(1)}, bf16[48,1536]{1,0:T(8,128)(2,1)S(1)}, u32[]{:S(2)}, u32[]{:S(2)}) collective-permute-start(bf16[48,1536]{1,0:T(8,128)(2,1)S(1)} %collective-permute-done.38.refs_1_), channel_id=1, source_target_pairs={{0,1},{1,0},{2,3},{3,2},{4,5},{5,4},{6,7},{7,6},{8,9},{9,8},{10,11... | collective-permute-start | bytes 442376 | tf_op jit(solution)/shard_map/ppermute | solution.py:412
  154.6 6.3 %collective-permute-start.36 = (bf16[224,384]{1,0:T(8,128)(2,1)S(1)}, bf16[224,384]{1,0:T(8,128)(2,1)S(1)}, u32[]{:S(2)}, u32[]{:S(2)}) collective-permute-start(bf16[224,384]{1,0:T(8,128)(2,1)S(1)} %rest3.1.refs_4_.refs_0_), channel_id=1, source_target_pairs={{0,1},{1,0},{2,3},{3,2},{4,5},{5,4},{6,7},{7,6},{8,9},{9,8},{10,11... | collective-permute-start | bytes 516104 | tf_op jit(solution)/shard_map/ppermute | solution.py:412
  157.6 3.3 %collective-permute-start.37 = (bf16[224,384]{1,0:T(8,128)(2,1)S(1)}, bf16[224,384]{1,0:T(8,128)(2,1)S(1)}, u32[]{:S(2)}, u32[]{:S(2)}) collective-permute-start(bf16[224,384]{1,0:T(8,128)(2,1)S(1)} %collective-permute-done.35.refs_1_), channel_id=1, source_target_pairs={{0,1},{1,0},{2,3},{3,2},{4,5},{5,4},{6,7},{7,6},{8,9},{9,8},{10,11... | collective-permute-start | bytes 516104 | tf_op jit(solution)/shard_map/ppermute | solution.py:412
  (14 other events, 32.5 us)
where the time goes:
time: 165 us
  Pallas kernels  84.5 us (51%)
  starting transfers between devices  35.8 us (22%)
  waiting for transfers between devices  35.8 us (22%)
  local copies, waits for them, and re-layouts  6.8 us (4%)
    pallas_call x31, Pallas kernels, call(): pl.pallas_call(run, in_specs=[pl.BlockSpec(memory_space=pltpu.SMEM)] + [p...  84.5 us
    ppermute x12, waiting for transfers between devices, exchange(): return lax.ppermute(value, ('dp', 'seq'), moves)  24.8 us
    ppermute x29, starting transfers between devices, swap(): return lax.ppermute(value, axis, [(i, i ^ bit) for i in range(size)])  20.6 us
    ppermute x12, starting transfers between devices, exchange(): return lax.ppermute(value, ('dp', 'seq'), moves)  15.2 us
    ppermute x29, waiting for transfers between devices, swap(): return lax.ppermute(value, axis, [(i, i ^ bit) for i in range(size)])  11 us
    unnamed x74, local copies, waits for them, and re-layouts  6.12 us
  transfers between devices with their start and end apart: 41, of which 8 were waited for; matrix products, arithmetic and copies ran while one was open for 0% of the time, Pallas kernels for 46%

commit v1 on v0

--- a/solution.py
+++ b/solution.py
@@ -120,7 +120,7 @@
     copies[2].wait()
     for at in columns(width):
         v_ref[:, at] = (nn(x, wv_ref[:, at]) + bv_ref[:, at].astype(F32)).astype(BF16)
-    def pair(p, carry):
+    def pair(p):
         at = pl.ds(pl.multiple_of(p * PAIR, PAIR), PAIR)
         q, k, v = q_ref[:, at], k_ref[:, at], v_ref[:, at]
         vt = v.astype(F32).T.astype(BF16)
@@ -132,9 +132,13 @@
             p_ref[2 * p + i] = w
             out.append(nn(vt[i * HD : (i + 1) * HD], w))
         ctx_ref[:, at] = jnp.concatenate(out, axis=0).T.astype(BF16)
+
+    def step(i, carry):
+        for j in range(3):
+            pair(3 * i + j)
         return carry
 
-    lax.fori_loop(0, width // PAIR, pair, 0)
+    lax.fori_loop(0, width // PAIR // 3, step, 0)
     copies[3].wait()
     v1 = jnp.concatenate([nn(ctx_ref[...], wo_ref[:, at]) for at in columns(width)], axis=1)
     v1 = x_ref[...].astype(F32) + (v1 + bo_ref[...].astype(F32))
@@ -278,10 +282,14 @@
 
 def place(info_ref, base, rows, buf_ref, keep_ref, send_ref):
     slots = buf_ref.shape[0] // rows
-    for slot in range(slots):
-        chunk = buf_ref[pl.ds(pl.multiple_of(info_ref[base + slot] * rows, 16), rows), :]
-        ref, to = (keep_ref, slot) if slot < slots // 2 else (send_ref, slot - slots // 2)
-        ref[to * rows : (to + 1) * rows, :] = chunk
+    for ref, first in ((keep_ref, base), (send_ref, base + slots // 2)):
+
+        def copy(slot, carry):
+            at = pl.ds(pl.multiple_of(info_ref[first + slot] * rows, 16), rows)
+            ref[pl.ds(pl.multiple_of(slot * rows, 16), rows), :] = buf_ref[at, :]
+            return carry
+
+        lax.fori_loop(0, slots // 2, copy, 0)
 
 
 def outer_kernel(base, rows):

time: 165 us -> 165 us (level)
  transfers between devices with their start and end apart: 41 -> 41, of which waited for: 8 -> 8; matrix products, arithmetic and copies ran while one was open for 0% -> 0% of each run, Pallas kernels for 46% -> 45%
where the time goes in v1:
time: 165 us; the launch traced here: 164 us
  Pallas kernels  83.8 us (51%)
  starting transfers between devices  35.9 us (22%)
  waiting for transfers between devices  35.6 us (22%)
  local copies, waits for them, and re-layouts  6.8 us (4%)
    pallas_call x31, Pallas kernels, call(): pl.pallas_call(run, in_specs=[pl.BlockSpec(memory_space=pltpu.SMEM)] + [p...  83.8 us
    ppermute x12, waiting for transfers between devices, exchange(): return lax.ppermute(value, ('dp', 'seq'), moves)  24.7 us
    ppermute x29, starting transfers between devices, swap(): return lax.ppermute(value, axis, [(i, i ^ bit) for i in range(size)])  20.7 us
    ppermute x12, starting transfers between devices, exchange(): return lax.ppermute(value, ('dp', 'seq'), moves)  15.2 us
    ppermute x29, waiting for transfers between devices, swap(): return lax.ppermute(value, axis, [(i, i ^ bit) for i in range(size)])  10.8 us
    unnamed x74, local copies, waits for them, and re-layouts  6.12 us
  transfers between devices with their start and end apart: 41, of which 8 were waited for; matrix products, arithmetic and copies ran while one was open for 0% of the time, Pallas kernels for 45%

profile of v1, /device:TPU:1, one launch (start us, length us, event | category | flops | bytes accessed | tf_op | source)
XLA Modules:
  0.0 164.3 jit_solution(8216814500491689817)
XLA Ops:
  0.8 1.1 copy-done.5
  1.9 1.6 deal_inputs.1
  3.7 2.7 %collective-permute-start.1 = (bf16[128,768]{1,0:T(8,128)(2,1)S(1)}, bf16[128,768]{1,0:T(8,128)(2,1)S(1)}, u32[]{:S(2)}, u32[]{:S(2)}) collective-permute-start(bf16[128,768]{1,0:T(8,128)(2,1)S(1)} %get-tuple-element.77), channel_id=1, source_target_pairs={{0,2},{1,3},{2,0},{3,1},{4,6},{5,7},{6,4},{7,5},{8,10},{9,11},{10,... | collective-permute-start | bytes 589832 | tf_op jit(solution)/shard_map/ppermute | solution.py:420
  6.7 1.6 deal_cotangent.1
  8.7 1.4 collective-permute-start.4
  10.7 0.8 collective-permute-done.1.refs_2_
  11.5 4.4 %collective-permute-done.2.refs_3_ = bf16[128,768]{1,0:T(8,128)(2,1)S(1)} collective-permute-done((bf16[128,768]{1,0:T(8,128)(2,1)S(1)}, bf16[128,768]{1,0:T(8,128)(2,1)S(1)}, u32[]{:S(2)}, u32[]{:S(2)}) %collective-permute-start.2) | collective-permute-done | bytes 196640 | tf_op jit(solution)/shard_map/ppermute | solution.py:420
  16.0 13.2 %attention.1 = (bf16[512,768]{1,0:T(8,128)(2,1)S(1)}, bf16[512,768]{1,0:T(8,128)(2,1)S(1)}, bf16[512,768]{1,0:T(8,128)(2,1)S(1)}, bf16[512,768]{1,0:T(8,128)(2,1...) custom-call(s32[51]{0:T(128)S(1)} %concatenate.3.info_ref, ...), custom_call_target="tpu_custom_call" | custom-call | flops 38999998464 | bytes 1 | tf_op jit(solution)/shard_map/attention/pallas_call | solution.py:45
  29.3 6.1 %hidden.1 = (bf16[512,3072]{1,0:T(8,128)(2,1)S(1)}, bf16[512,3072]{1,0:T(8,128)(2,1)S(1)}) custom-call(s32[51]{0:T(128)S(1)} %concatenate.3.info_ref, bf16[512,768]{1,0:T(8,128)(2,1)S(1)} %get-tuple-element.79.refs_0_, bf16[768,3072]{1,0:T(8,128)(2,1)S(1)} %bitcast.22, bf16[1,3072]{1,0:T(2,128)(2,1)S(1)} %reshape.71.refs_2_, ...), custom_call_target="tpu_custom_call" | custom-call | flops 27000000512 | bytes 1 | tf_op jit(solution)/shard_map/hidden/pallas_call | solution.py:45
  36.1 4.5 %branch.1 = (bf16[128,768]{1,0:T(8,128)(2,1)S(1)}, bf16[128,768]{1,0:T(8,128)(2,1)S(1)}, bf16[128,768]{1,0:T(8,128)(2,1)S(1)}, bf16[128,768]{1,0:T(8,128)(2,1)S(...) custom-call(s32[51]{0:T(128)S(1)} %concatenate.3.info_ref, ...), custom_call_target="tpu_custom_call" | custom-call | flops 12000000000 | bytes 1 | tf_op jit(solution)/shard_map/branch/pallas_call | solution.py:45
  41.2 1.7 %collective-permute-start.7 = (bf16[128,768]{1,0:T(8,128)(2,1)S(1)}, bf16[128,768]{1,0:T(8,128)(2,1)S(1)}, u32[]{:S(2)}, u32[]{:S(2)}) collective-permute-start(bf16[128,768]{1,0:T(8,128)(2,1)S(1)} %get-tuple-element.88), channel_id=1, source_target_pairs={{0,2},{1,3},{2,0},{3,1},{4,6},{5,7},{6,4},{7,5},{8,10},{9,11},{10,... | collective-permute-start | bytes 589832 | tf_op jit(solution)/shard_map/ppermute | solution.py:420
  43.0 2.0 %hidden_back_other.1 = (bf16[512,1536]{1,0:T(8,128)(2,1)S(1)}, f32[1,1536]{1,0:T(1,128)S(1)}) custom-call(s32[51]{0:T(128)S(1)} %concatenate.3.info_ref, bf16[512,768]{1,0:T(8,128)(2,1)S(1)} %get-tuple-element.92.refs_0_, bf16[3072,768]{1,0:T(8,128)(2,1)S(1)} %bitcast.20, bf16[512,3072]{1,0:T(8,128)(2,1)S(1)} %get-tuple-element.93.refs_2_, ...), custom_call_target="tpu_custom_call" | custom-call | flops 8999999488 | bytes 1 | tf_op jit(solution)/shard_map/hidden_back_other/pallas_call | solution.py:45
  45.5 2.0 %hidden_back_mine.1 = (bf16[512,1536]{1,0:T(8,128)(2,1)S(1)}, f32[1,1536]{1,0:T(1,128)S(1)}) custom-call(s32[51]{0:T(128)S(1)} %concatenate.3.info_ref, bf16[512,768]{1,0:T(8,128)(2,1)S(1)} %get-tuple-element.92.refs_0_, bf16[3072,768]{1,0:T(8,128)(2,1)S(1)} %bitcast.20, bf16[512,3072]{1,0:T(8,128)(2,1)S(1)} %get-tuple-element.93.refs_2_, ...), custom_call_target="tpu_custom_call" | custom-call | flops 8999999488 | bytes 1 | tf_op jit(solution)/shard_map/hidden_back_mine/pallas_call | solution.py:45
  47.5 5.1 %grad_outer.1 = (bf16[1536,384]{1,0:T(8,128)(2,1)S(1)}, bf16[1536,384]{1,0:T(8,128)(2,1)S(1)}) custom-call(s32[51]{0:T(128)S(1)} %concatenate.3.info_ref, bf16[512,3072]{1,0:T(8,128)(2,1)S(1)} %get-tuple-element.84.refs_0_, bf16[512,3072]{1,0:T(8,128)(2,1)S(1)} %collective-permute-done.9.refs_3_.refs_1_, bf16[512,384]{1,0:T(8,128)(2,1)S(1)} %get-tuple-element.90.refs_2_, ...), custom_call_target="tpu_custom_call" | custom-call | flops 15000000512 | bytes 1 | tf_op jit(solution)/shard_map/grad_outer/pallas_call | solution.py:45
  52.7 1.5 collective-permute-start.13
  54.2 1.5 collect_outputs.1.refs_4_
  55.7 1.1 copy-done.8
  56.8 3.7 %grad_inner.1 = (bf16[384,1536]{1,0:T(8,128)(2,1)S(1)}, bf16[384,1536]{1,0:T(8,128)(2,1)S(1)}) custom-call(s32[51]{0:T(128)S(1)} %concatenate.3.info_ref, bf16[512,768]{1,0:T(8,128)(2,1)S(1)} %get-tuple-element.79.refs_0_, bf16[512,768]{1,0:T(8,128)(2,1)S(1)} %collective-permute-done.11.refs_1_, bf16[512,1536]{1,0:T(8,128)(2,1)S(1)} %get-tuple-element.101.refs_2_.refs_0_, ...), custom_call_target="tpu_custom_call" | custom-call | flops 12000000000 | bytes 1 | tf_op jit(solution)/shard_map/grad_inner/pallas_call | solution.py:45
  60.5 5.5 %first_back.1 = (f32[512,768]{1,0:T(8,128)S(1)}, bf16[512,768]{1,0:T(8,128)(2,1)S(1)}, bf16[512,384]{1,0:T(8,128)(2,1)S(1)}, bf16[512,384]{1,0:T(8,128)(2,1)S(1)}, f32[3,768]{1,0:T(4,128)S(1)}) custom-call(s32[51]{0:T(128)S(1)} %concatenate.3.info_ref, bf16[512,1536]{1,0:T(8,128)(2,1)S(1)} %get-tuple-element.101.refs_2_.refs_0_, ...), custom_call_target="tpu_custom_call" | custom-call | flops 17999998976 | bytes 1 | tf_op jit(solution)/shard_map/first_back/pallas_call | solution.py:45
  66.0 5.5 %attention_back_other.1 = (bf16[3,512,384]{2,1,0:T(8,128)(2,1)S(1)}, f32[3,384]{1,0:T(4,128)S(1)}) custom-call(s32[51]{0:T(128)S(1)} %concatenate.3.info_ref, bf16[512,768]{1,0:T(8,128)(2,1)S(1)} %get-tuple-element.97.refs_0_, bf16[512,768]{1,0:T(8,128)(2,1)S(1)} %get-tuple-element.98.refs_1_, bf16[512,768]{1,0:T(8,128)(2,1)S(1)} %get-tuple-element.99.refs_2_, ...), custom_call_target="tpu_custom_call" | custom-call | flops 3000000000 | bytes 1 | tf_op jit(solution)/shard_map/attention_back_other/pallas_call | solution.py:45
  71.6 0.7 collective-permute-start.16
  72.3 0.7 outer0.1.refs_5_
  73.0 0.8 collective-permute-start.18
  73.8 0.9 collective-permute-start.14
  75.2 5.8 %attention_back_mine.1 = (bf16[3,512,384]{2,1,0:T(8,128)(2,1)S(1)}, f32[3,384]{1,0:T(4,128)S(1)}) custom-call(s32[51]{0:T(128)S(1)} %concatenate.3.info_ref, bf16[512,768]{1,0:T(8,128)(2,1)S(1)} %get-tuple-element.97.refs_0_, bf16[512,768]{1,0:T(8,128)(2,1)S(1)} %get-tuple-element.98.refs_1_, bf16[512,768]{1,0:T(8,128)(2,1)S(1)} %get-tuple-element.99.refs_2_, ...), custom_call_target="tpu_custom_call" | custom-call | flops 3000000000 | bytes 1 | tf_op jit(solution)/shard_map/attention_back_mine/pallas_call | solution.py:45
  81.1 1.0 collective-permute-done.18.refs_2_
  82.1 1.2 collective-permute-start.20
  83.3 0.7 outer1.1.refs_14_
  84.0 4.1 %grad_rest.1 = (bf16[1536,384]{1,0:T(8,128)(2,1)S(1)}, bf16[1568,384]{1,0:T(8,128)(2,1)S(1)}, f32[16,768]{1,0:T(8,128)S(1)}) custom-call(s32[51]{0:T(128)S(1)} %concatenate.3.info_ref, bf16[512,768]{1,0:T(8,128)(2,1)S(1)} %get-tuple-element.113.refs_0_, bf16[512,768]{1,0:T(8,128)(2,1)S(1)} %collective-permute-done.14.refs_1_, ...), custom_call_target="tpu_custom_call" | custom-call | flops 3000000000 | bytes 1 | tf_op jit(solution)/shard_map/grad_rest/pallas_call | solution.py:45
  88.5 1.3 collective-permute-start.24
  89.8 7.7 %collective-permute-done.20.refs_1_ = bf16[384,1536]{1,0:T(8,128)(2,1)S(1)} collective-permute-done((bf16[384,1536]{1,0:T(8,128)(2,1)S(1)}, bf16[384,1536]{1,0:T(8,128)(2,1)S(1)}, u32[]{:S(2)}, u32[]{:S(2)}) %collective-permute-start.20) | collective-permute-done | bytes 1179680 | tf_op jit(solution)/shard_map/ppermute | solution.py:447
  97.5 0.7 inner0.1.refs_3_
  98.1 1.4 collective-permute-start.25
  99.5 11.2 %collective-permute-done.19.refs_1_ = bf16[1568,384]{1,0:T(8,128)(2,1)S(1)} collective-permute-done((bf16[1568,384]{1,0:T(8,128)(2,1)S(1)}, bf16[1568,384]{1,0:T(8,128)(2,1)S(1)}, u32[]{:S(2)}, u32[]{:S(2)}) %collective-permute-start.19) | collective-permute-done | bytes 1204256 | tf_op jit(solution)/shard_map/ppermute | solution.py:447
  110.7 0.7 rest0.1.refs_6_.refs_3_
  111.4 0.6 collective-permute-start.28
  112.0 7.2 %input_back.1 = (bf16[128,768]{1,0:T(8,128)(2,1)S(1)}, bf16[128,768]{1,0:T(8,128)(2,1)S(1)}, bf16[128,768]{1,0:T(8,128)(2,1)S(1)}, bf16[128,768]{1,0:T(8,128)(2,1)S(1)}) custom-call(s32[51]{0:T(128)S(1)} %concatenate.3.info_ref, bf16[3,512,384]{2,1,0:T(8,128)(2,1)} %copy-done.12, bf16[3,512,384]{2,1,0:T(8,128)(2,1)} %copy-done.4, f32[512,768]{1,0:T(8,128)} %copy-done.17, ...), custom_call_target="tpu_custom_call" | custom-call | flops 6000000000 | bytes 1 | tf_op jit(solution)/shard_map/input_back/pallas_call | solution.py:45
  119.3 0.7 inner1.1.refs_4_
  119.9 1.0 collective-permute-start.27
  121.5 2.4 %collective-permute-start.26 = (bf16[192,384]{1,0:T(8,128)(2,1)S(1)}, bf16[192,384]{1,0:T(8,128)(2,1)S(1)}, u32[]{:S(2)}, u32[]{:S(2)}) collective-permute-start(bf16[192,384]{1,0:T(8,128)(2,1)S(1)} %outer2.1.refs_4_), channel_id=1, source_target_pairs={{0,16},{1,17},{2,18},{3,19},{4,20},{5,21},{6,22},{7,23},{8,24},{9,... | collective-permute-start | bytes 442376 | tf_op jit(solution)/shard_map/ppermute | solution.py:447
  124.5 1.6 collective-permute-start.23
  126.1 0.7 rest1.1.refs_4_
  126.7 1.9 %collective-permute-start.29 = (bf16[416,384]{1,0:T(8,128)(2,1)S(1)}, bf16[416,384]{1,0:T(8,128)(2,1)S(1)}, u32[]{:S(2)}, u32[]{:S(2)}) collective-permute-start(bf16[416,384]{1,0:T(8,128)(2,1)S(1)} %rest1.1.refs_4_), channel_id=1, source_target_pairs={{0,8},{1,9},{2,10},{3,11},{4,12},{5,13},{6,14},{7,15},{8,0},{9,1},... | collective-permute-start | bytes 958472 | tf_op jit(solution)/shard_map/ppermute | solution.py:447
  129.3 0.6 outer3.1.refs_4_.refs_0_
  129.9 1.0 collective-permute-start.32
  131.2 1.6 %collective-permute-start.31 = (bf16[48,1536]{1,0:T(8,128)(2,1)S(1)}, bf16[48,1536]{1,0:T(8,128)(2,1)S(1)}, u32[]{:S(2)}, u32[]{:S(2)}) collective-permute-start(bf16[48,1536]{1,0:T(8,128)(2,1)S(1)} %inner2.1.refs_5_), channel_id=1, source_target_pairs={{0,16},{1,17},{2,18},{3,19},{4,20},{5,21},{6,22},{7,23},{8,24},{9,... | collective-permute-start | bytes 442376 | tf_op jit(solution)/shard_map/ppermute | solution.py:447
  132.8 3.2 %collective-permute-done.23.refs_3_ = bf16[128,768]{1,0:T(8,128)(2,1)S(1)} collective-permute-done((bf16[128,768]{1,0:T(8,128)(2,1)S(1)}, bf16[128,768]{1,0:T(8,128)(2,1)S(1)}, u32[]{:S(2)}, u32[]{:S(2)}) %collective-permute-start.23) | collective-permute-done | bytes 196640 | tf_op jit(solution)/shard_map/ppermute | solution.py:420
  136.0 1.5 collect_inputs.1.refs_5_
  137.5 1.1 collective-permute-start.34
  138.6 1.1 copy-done.9
  140.4 1.2 collective-permute-start.30
  141.6 1.6 %finish_outer.1.refs_5_ = f32[384,768]{1,0:T(8,128)} custom-call(s32[51]{0:T(128)S(1)} %concatenate.3.info_ref, bf16[192,384]{1,0:T(8,128)(2,1)S(1)} %outer3.1.refs_4_.refs_0_, bf16[192,384]{1,0:T(8,128)(2,1)S(1)} %collective-permute-done.32.refs_1_, bf16[192,384]{1,0:T(8,128)(2,1)S(1)} %collective-permute-done.33.refs_2_, ...), custom_call_target="tpu_custom_call" | custom-call | flops 3000000000 | bytes 1 | tf_op jit(solution)/shard_map/finish_outer/pallas_call | solution.py:45
  143.3 1.3 copy-done.6
  144.5 0.6 inner3.1.refs_6_.refs_0_
  145.2 1.0 collective-permute-start.38
  146.1 4.8 %collective-permute-done.30.refs_4_ = bf16[224,384]{1,0:T(8,128)(2,1)S(1)} collective-permute-done((bf16[224,384]{1,0:T(8,128)(2,1)S(1)}, bf16[224,384]{1,0:T(8,128)(2,1)S(1)}, u32[]{:S(2)}, u32[]{:S(2)}) %collective-permute-start.30) | collective-permute-done | bytes 172064 | tf_op jit(solution)/shard_map/ppermute | solution.py:447
  151.0 0.7 rest3.1.refs_4_.refs_0_
  151.6 0.9 collective-permute-start.35
  152.5 1.4 collective-permute-start.39
  154.4 2.3 %collective-permute-done.35.refs_1_ = bf16[224,384]{1,0:T(8,128)(2,1)S(1)} collective-permute-done((bf16[224,384]{1,0:T(8,128)(2,1)S(1)}, bf16[224,384]{1,0:T(8,128)(2,1)S(1)}, u32[]{:S(2)}, u32[]{:S(2)}) %collective-permute-start.35) | collective-permute-done | bytes 172064 | tf_op jit(solution)/shard_map/ppermute | solution.py:420
  156.8 1.7 %collective-permute-start.37 = (bf16[224,384]{1,0:T(8,128)(2,1)S(1)}, bf16[224,384]{1,0:T(8,128)(2,1)S(1)}, u32[]{:S(2)}, u32[]{:S(2)}) collective-permute-start(bf16[224,384]{1,0:T(8,128)(2,1)S(1)} %collective-permute-done.35.refs_1_), channel_id=1, source_target_pairs={{0,1},{1,0},{2,3},{3,2},{4,5},{5,4},{6,7},{7,6},{8,9},{9,8},{10,11... | collective-permute-start | bytes 516104 | tf_op jit(solution)/shard_map/ppermute | solution.py:420
  158.5 1.6 %finish_inner.1.refs_4_ = f32[96,3072]{1,0:T(8,128)} custom-call(s32[51]{0:T(128)S(1)} %concatenate.3.info_ref, bf16[48,1536]{1,0:T(8,128)(2,1)S(1)} %inner3.1.refs_6_.refs_0_, bf16[48,1536]{1,0:T(8,128)(2,1)S(1)} %collective-permute-done.38.refs_1_, bf16[48,1536]{1,0:T(8,128)(2,1)S(1)} %collective-permute-done.39.refs_2_, ...), custom_call_target="tpu_custom_call" | custom-call | flops 3000000000 | bytes 1 | tf_op jit(solution)/shard_map/finish_inner/pallas_call | solution.py:45
  160.2 1.3 copy-done.7
  161.4 1.7 %finish_rest.1 = (f32[96,768]{1,0:T(8,128)}, f32[96,768]{1,0:T(8,128)}, f32[96,768]{1,0:T(8,128)}, f32[96,768]{1,0:T(8,128)}, f32[16,128]{1,0:T(8,128)S(1)}, /*index=5*/f32[1,384]{1,0:T(1,128)S(1)}) custom-call(s32[51]{0:T(128)S(1)} %concatenate.3.info_ref, bf16[224,384]{1,0:T(8,128)(2,1)S(1)} %rest3.1.refs_4_.refs_0_, ...), custom_call_target="tpu_custom_call" | custom-call | flops 3000000000 | bytes 1 | tf_op jit(solution)/shard_map/finish_rest/pallas_call | solution.py:45
  (140 shorter events, 8.4 us)
Async XLA Ops:
  1.9 4.5 %copy-start.24 = (s32[4,128]{1,0:T(4,128)S(1)}, s32[4,128]{1,0:T(4,128)}, u32[]{:S(2)}) copy-start(s32[4,128]{1,0:T(4,128)} %param.20) | copy-start | bytes 6148
  1.9 4.5 %copy-start.22 = (bf16[4,128,768]{2,1,0:T(8,128)(2,1)S(1)}, bf16[4,128,768]{2,1,0:T(8,128)(2,1)}, u32[]{:S(2)}) copy-start(bf16[4,128,768]{2,1,0:T(8,128)(2,1)} %param.19) | copy-start | bytes 2359300
  1.9 14.1 %copy-start.3 = (bf16[768,768]{1,0:T(8,128)(2,1)S(1)}, bf16[768,768]{1,0:T(8,128)(2,1)}, u32[]{:S(2)}) copy-start(bf16[768,768]{1,0:T(8,128)(2,1)} %refs_5_.1) | copy-start | bytes 3538948
  3.5 6.8 %collective-permute-start = (bf16[128,768]{1,0:T(8,128)(2,1)S(1)}, bf16[128,768]{1,0:T(8,128)(2,1)S(1)}, u32[]{:S(2)}, u32[]{:S(2)}) collective-permute-start(bf16[128,768]{1,0:T(8,128)(2,1)S(1)} %get-tuple-element.76), channel_id=1, source_target_pairs={{0,1},{1,0},{2,3},{3,2},{4,5},{5,4},{6,7},{7,6},{8,9},{9,8},{10,11... | collective-permute-start | bytes 589832 | tf_op jit(solution)/shard_map/ppermute | solution.py:420
  3.7 7.9 %collective-permute-start.1 = (bf16[128,768]{1,0:T(8,128)(2,1)S(1)}, bf16[128,768]{1,0:T(8,128)(2,1)S(1)}, u32[]{:S(2)}, u32[]{:S(2)}) collective-permute-start(bf16[128,768]{1,0:T(8,128)(2,1)S(1)} %get-tuple-element.77), channel_id=1, source_target_pairs={{0,2},{1,3},{2,0},{3,1},{4,6},{5,7},{6,4},{7,5},{8,10},{9,11},{10,... | collective-permute-start | bytes 589832 | tf_op jit(solution)/shard_map/ppermute | solution.py:420
  6.4 9.6 %collective-permute-start.2 = (bf16[128,768]{1,0:T(8,128)(2,1)S(1)}, bf16[128,768]{1,0:T(8,128)(2,1)S(1)}, u32[]{:S(2)}, u32[]{:S(2)}) collective-permute-start(bf16[128,768]{1,0:T(8,128)(2,1)S(1)} %get-tuple-element.78), channel_id=1, source_target_pairs={{0,3},{1,2},{2,1},{3,0},{4,7},{5,6},{6,5},{7,4},{8,11},{9,10},{10,... | collective-permute-start | bytes 589832 | tf_op jit(solution)/shard_map/ppermute | solution.py:420
  6.4 9.6 %copy-start.2 = (bf16[768,768]{1,0:T(8,128)(2,1)S(1)}, bf16[768,768]{1,0:T(8,128)(2,1)}, u32[]{:S(2)}) copy-start(bf16[768,768]{1,0:T(8,128)(2,1)} %refs_4_.1) | copy-start | bytes 3538948
  6.6 3.7 %copy-start.23 = (bf16[3072]{0:T(1024)(128)(2,1)S(1)}, bf16[3072]{0:T(1024)(128)(2,1)}, u32[]{:S(2)}) copy-start(bf16[3072]{0:T(1024)(128)(2,1)} %param.31) | copy-start | bytes 18436
  6.6 9.3 %copy-start = (bf16[768,768]{1,0:T(8,128)(2,1)S(1)}, bf16[768,768]{1,0:T(8,128)(2,1)}, u32[]{:S(2)}) copy-start(bf16[768,768]{1,0:T(8,128)(2,1)} %refs_7_.1) | copy-start | bytes 3538948
  6.7 9.3 %copy-start.1 = (bf16[768,768]{1,0:T(8,128)(2,1)S(1)}, bf16[768,768]{1,0:T(8,128)(2,1)}, u32[]{:S(2)}) copy-start(bf16[768,768]{1,0:T(8,128)(2,1)} %refs_3_.1) | copy-start | bytes 3538948
  6.7 22.6 %slice-start.2 = ((s8[4718592]{0:T(1024)(128)(4,1)}), s8[4194304]{0:T(1024)(128)(4,1)S(1)}, s32[]{:S(2)}) async-start(s8[4718592]{0:T(1024)(128)(4,1)} %bitcast.21), calls=%async_computation.2 | async-start | bytes 8388608
  6.7 29.4 %slice-start = ((s8[4718592]{0:T(1024)(128)(4,1)}), s8[4194304]{0:T(1024)(128)(4,1)S(1)}, s32[]{:S(2)}) async-start(s8[4718592]{0:T(1024)(128)(4,1)} %bitcast.19), calls=%async_computation | async-start | bytes 8388608
  8.3 20.9 %collective-permute-start.3 = (bf16[128,768]{1,0:T(8,128)(2,1)S(1)}, bf16[128,768]{1,0:T(8,128)(2,1)S(1)}, u32[]{:S(2)}, u32[]{:S(2)}) collective-permute-start(bf16[128,768]{1,0:T(8,128)(2,1)S(1)} %get-tuple-element.81), channel_id=1, source_target_pairs={{0,1},{1,0},{2,3},{3,2},{4,5},{5,4},{6,7},{7,6},{8,9},{9,8},{10,11... | collective-permute-start | bytes 589832 | tf_op jit(solution)/shard_map/ppermute | solution.py:420
  8.7 20.5 %collective-permute-start.4 = (bf16[128,768]{1,0:T(8,128)(2,1)S(1)}, bf16[128,768]{1,0:T(8,128)(2,1)S(1)}, u32[]{:S(2)}, u32[]{:S(2)}) collective-permute-start(bf16[128,768]{1,0:T(8,128)(2,1)S(1)} %get-tuple-element.82), channel_id=1, source_target_pairs={{0,2},{1,3},{2,0},{3,1},{4,6},{5,7},{6,4},{7,5},{8,10},{9,11},{10,... | collective-permute-start | bytes 589832 | tf_op jit(solution)/shard_map/ppermute | solution.py:420
  10.3 18.9 %collective-permute-start.5 = (bf16[128,768]{1,0:T(8,128)(2,1)S(1)}, bf16[128,768]{1,0:T(8,128)(2,1)S(1)}, u32[]{:S(2)}, u32[]{:S(2)}) collective-permute-start(bf16[128,768]{1,0:T(8,128)(2,1)S(1)} %get-tuple-element.83), channel_id=1, source_target_pairs={{0,3},{1,2},{2,1},{3,0},{4,7},{5,6},{6,5},{7,4},{8,11},{9,10},{10,... | collective-permute-start | bytes 589832 | tf_op jit(solution)/shard_map/ppermute | solution.py:420
  16.0 13.3 %slice-start.3 = ((s8[4718592]{0:T(1024)(128)(4,1)}), s8[524288]{0:T(1024)(128)(4,1)S(1)}, s32[]{:S(2)}) async-start(s8[4718592]{0:T(1024)(128)(4,1)} %bitcast.21), calls=%async_computation.3 | async-start | bytes 1048576
  16.0 20.1 %slice-start.1 = ((s8[4718592]{0:T(1024)(128)(4,1)}), s8[524288]{0:T(1024)(128)(4,1)S(1)}, s32[]{:S(2)}) async-start(s8[4718592]{0:T(1024)(128)(4,1)} %bitcast.19), calls=%async_computation.1 | async-start | bytes 1048576
  29.2 6.9 %copy-start.18 = (f32[512,768]{1,0:T(8,128)}, f32[512,768]{1,0:T(8,128)S(1)}, u32[]{:S(2)}) copy-start(f32[512,768]{1,0:T(8,128)S(1)} %get-tuple-element.85.refs_3_.refs_4_) | copy-start | bytes 4718596
  29.2 36.8 %copy-start.10 = (bf16[12,512,512]{2,1,0:T(8,128)(2,1)}, bf16[12,512,512]{2,1,0:T(8,128)(2,1)S(1)}, u32[]{:S(2)}) copy-start(bf16[12,512,512]{2,1,0:T(8,128)(2,1)S(1)} %get-tuple-element.100.refs_3_) | copy-start | bytes 18874372
  29.3 6.3 %copy-start.30 = (bf16[768]{0:T(1024)(128)(2,1)S(1)}, bf16[768]{0:T(1024)(128)(2,1)}, u32[]{:S(2)}) copy-start(bf16[768]{0:T(1024)(128)(2,1)} %param.33) | copy-start | bytes 4612
  29.3 6.3 %copy-start.31 = (bf16[768]{0:T(1024)(128)(2,1)S(1)}, bf16[768]{0:T(1024)(128)(2,1)}, u32[]{:S(2)}) copy-start(bf16[768]{0:T(1024)(128)(2,1)} %param.34) | copy-start | bytes 4612
  29.3 6.3 %copy-start.32 = (bf16[768]{0:T(1024)(128)(2,1)S(1)}, bf16[768]{0:T(1024)(128)(2,1)}, u32[]{:S(2)}) copy-start(bf16[768]{0:T(1024)(128)(2,1)} %param.35) | copy-start | bytes 4612
  35.4 7.5 %collective-permute-start.9 = (bf16[512,3072]{1,0:T(8,128)(2,1)S(1)}, bf16[512,3072]{1,0:T(8,128)(2,1)S(1)}, u32[]{:S(2)}, u32[]{:S(2)}) collective-permute-start(bf16[512,3072]{1,0:T(8,128)(2,1)S(1)} %get-tuple-element.84.refs_0_), channel_id=1, source_target_pairs={{0,1},{1,0},{2,3},{3,2},{4,5},{5,4},{6,7},{7,6},{8,9},{9,8},{10,11... | collective-permute-start | bytes 9437192 | tf_op jit(solution)/shard_map/ppermute | solution.py:420
  35.7 20.0 %collective-permute-start.11 = (bf16[512,768]{1,0:T(8,128)(2,1)S(1)}, bf16[512,768]{1,0:T(8,128)(2,1)S(1)}, u32[]{:S(2)}, u32[]{:S(2)}) collective-permute-start(bf16[512,768]{1,0:T(8,128)(2,1)S(1)} %get-tuple-element.79.refs_0_), channel_id=1, source_target_pairs={{0,1},{1,0},{2,3},{3,2},{4,5},{5,4},{6,7},{7,6},{8,9},{9,8},{10,11... | collective-permute-start | bytes 2359304 | tf_op jit(solution)/shard_map/ppermute | solution.py:420
  40.6 4.5 %copy-start.20 = (f32[512,768]{1,0:T(8,128)}, f32[512,768]{1,0:T(8,128)S(1)}, u32[]{:S(2)}) copy-start(f32[512,768]{1,0:T(8,128)S(1)} %get-tuple-element.103.refs_3_) | copy-start | bytes 4718596
  40.6 4.5 %collective-permute-start.10 = (bf16[512,384]{1,0:T(8,128)(2,1)S(1)}, bf16[512,384]{1,0:T(8,128)(2,1)S(1)}, u32[]{:S(2)}, u32[]{:S(2)}) collective-permute-start(bf16[512,384]{1,0:T(8,128)(2,1)S(1)} %get-tuple-element.91), channel_id=1, source_target_pairs={{0,1},{1,0},{2,3},{3,2},{4,5},{5,4},{6,7},{7,6},{8,9},{9,8},{10,11... | collective-permute-start | bytes 1179656 | tf_op jit(solution)/shard_map/ppermute | solution.py:420
  40.9 11.8 %collective-permute-start.6 = (bf16[128,768]{1,0:T(8,128)(2,1)S(1)}, bf16[128,768]{1,0:T(8,128)(2,1)S(1)}, u32[]{:S(2)}, u32[]{:S(2)}) collective-permute-start(bf16[128,768]{1,0:T(8,128)(2,1)S(1)} %get-tuple-element.87), channel_id=1, source_target_pairs={{0,1},{1,0},{2,3},{3,2},{4,5},{5,4},{6,7},{7,6},{8,9},{9,8},{10,11... | collective-permute-start | bytes 589832 | tf_op jit(solution)/shard_map/ppermute | solution.py:420
  41.2 13.0 %collective-permute-start.7 = (bf16[128,768]{1,0:T(8,128)(2,1)S(1)}, bf16[128,768]{1,0:T(8,128)(2,1)S(1)}, u32[]{:S(2)}, u32[]{:S(2)}) collective-permute-start(bf16[128,768]{1,0:T(8,128)(2,1)S(1)} %get-tuple-element.88), channel_id=1, source_target_pairs={{0,2},{1,3},{2,0},{3,1},{4,6},{5,7},{6,4},{7,5},{8,10},{9,11},{10,... | collective-permute-start | bytes 589832 | tf_op jit(solution)/shard_map/ppermute | solution.py:420
  42.9 11.3 %collective-permute-start.8 = (bf16[128,768]{1,0:T(8,128)(2,1)S(1)}, bf16[128,768]{1,0:T(8,128)(2,1)S(1)}, u32[]{:S(2)}, u32[]{:S(2)}) collective-permute-start(bf16[128,768]{1,0:T(8,128)(2,1)S(1)} %get-tuple-element.89), channel_id=1, source_target_pairs={{0,3},{1,2},{2,1},{3,0},{4,7},{5,6},{6,5},{7,4},{8,11},{9,10},{10,... | collective-permute-start | bytes 589832 | tf_op jit(solution)/shard_map/ppermute | solution.py:420
  45.1 10.6 %collective-permute-start.12 = (bf16[512,1536]{1,0:T(8,128)(2,1)S(1)}, bf16[512,1536]{1,0:T(8,128)(2,1)S(1)}, u32[]{:S(2)}, u32[]{:S(2)}) collective-permute-start(bf16[512,1536]{1,0:T(8,128)(2,1)S(1)} %get-tuple-element.102.refs_1_), channel_id=1, source_target_pairs={{0,1},{1,0},{2,3},{3,2},{4,5},{5,4},{6,7},{7,6},{8,9},{9,8},{10,11... | collective-permute-start | bytes 4718600 | tf_op jit(solution)/shard_map/ppermute | solution.py:420
  52.7 30.7 %copy-start.15 = (bf16[1536,384]{1,0:T(8,128)(2,1)}, bf16[1536,384]{1,0:T(8,128)(2,1)S(1)}, u32[]{:S(2)}) copy-start(bf16[1536,384]{1,0:T(8,128)(2,1)S(1)} %get-tuple-element.107.refs_0_) | copy-start | bytes 3538948
  52.7 19.6 %collective-permute-start.13 = (bf16[1536,384]{1,0:T(8,128)(2,1)S(1)}, bf16[1536,384]{1,0:T(8,128)(2,1)S(1)}, u32[]{:S(2)}, u32[]{:S(2)}) collective-permute-start(bf16[1536,384]{1,0:T(8,128)(2,1)S(1)} %get-tuple-element.96.refs_4_), channel_id=1, source_target_pairs={{0,2},{1,5},{2,0},{3,7},{4,6},{5,1},{6,4},{7,3},{8,10},{9,13},{10,... | collective-permute-start | bytes 3538952 | tf_op jit(solution)/shard_map/ppermute | solution.py:447
  56.8 3.7 %copy-start.19 = (f32[512,768]{1,0:T(8,128)S(1)}, f32[512,768]{1,0:T(8,128)}, u32[]{:S(2)}) copy-start(f32[512,768]{1,0:T(8,128)} %copy-done.18) | copy-start | bytes 4718596
  56.8 3.7 %copy-start.21 = (f32[512,768]{1,0:T(8,128)S(1)}, f32[512,768]{1,0:T(8,128)}, u32[]{:S(2)}) copy-start(f32[512,768]{1,0:T(8,128)} %copy-done.20) | copy-start | bytes 4718596
  60.5 37.0 %copy-start.13 = (bf16[384,1536]{1,0:T(8,128)(2,1)}, bf16[384,1536]{1,0:T(8,128)(2,1)S(1)}, u32[]{:S(2)}) copy-start(bf16[384,1536]{1,0:T(8,128)(2,1)S(1)} %get-tuple-element.121.refs_0_) | copy-start | bytes 3538948
  66.0 5.6 %copy-start.17 = (f32[512,768]{1,0:T(8,128)}, f32[512,768]{1,0:T(8,128)S(1)}, u32[]{:S(2)}) copy-start(f32[512,768]{1,0:T(8,128)S(1)} %get-tuple-element.112.refs_2_) | copy-start | bytes 4718596
  71.6 12.4 %collective-permute-start.16 = (bf16[3,512,384]{2,1,0:T(8,128)(2,1)S(1)}, bf16[3,512,384]{2,1,0:T(8,128)(2,1)S(1)}, u32[]{:S(2)}, u32[]{:S(2)}) collective-permute-start(bf16[3,512,384]{2,1,0:T(8,128)(2,1)S(1)} %get-tuple-element.111.refs_1_), channel_id=1, source_target_pairs={{0,1},{1,0},{2,3},{3,2},{4,5},{5,4},{6,7},{7,6},{8,9},{9,8},{10,11... | collective-permute-start | bytes 3538952 | tf_op jit(solution)/shard_map/ppermute | solution.py:420
  73.0 9.1 %collective-permute-start.18 = (bf16[768,384]{1,0:T(8,128)(2,1)S(1)}, bf16[768,384]{1,0:T(8,128)(2,1)S(1)}, u32[]{:S(2)}, u32[]{:S(2)}) collective-permute-start(bf16[768,384]{1,0:T(8,128)(2,1)S(1)} %outer0.1.refs_5_), channel_id=1, source_target_pairs={{0,4},{1,3},{2,6},{3,1},{4,0},{5,7},{6,2},{7,5},{8,12},{9,11},{10,... | collective-permute-start | bytes 1769480 | tf_op jit(solution)/shard_map/ppermute | solution.py:447
  73.8 10.2 %collective-permute-start.14 = (bf16[512,768]{1,0:T(8,128)(2,1)S(1)}, bf16[512,768]{1,0:T(8,128)(2,1)S(1)}, u32[]{:S(2)}, u32[]{:S(2)}) collective-permute-start(bf16[512,768]{1,0:T(8,128)(2,1)S(1)} %get-tuple-element.113.refs_0_), channel_id=1, source_target_pairs={{0,1},{1,0},{2,3},{3,2},{4,5},{5,4},{6,7},{7,6},{8,9},{9,8},{10,11... | collective-permute-start | bytes 2359304 | tf_op jit(solution)/shard_map/ppermute | solution.py:420
  74.7 9.3 %collective-permute-start.15 = (bf16[512,768]{1,0:T(8,128)(2,1)S(1)}, bf16[512,768]{1,0:T(8,128)(2,1)S(1)}, u32[]{:S(2)}, u32[]{:S(2)}) collective-permute-start(bf16[512,768]{1,0:T(8,128)(2,1)S(1)} %get-tuple-element.114.refs_2_), channel_id=1, source_target_pairs={{0,1},{1,0},{2,3},{3,2},{4,5},{5,4},{6,7},{7,6},{8,9},{9,8},{10,11... | collective-permute-start | bytes 2359304 | tf_op jit(solution)/shard_map/ppermute | solution.py:420
  74.7 9.3 %collective-permute-start.17 = (bf16[512,384]{1,0:T(8,128)(2,1)S(1)}, bf16[512,384]{1,0:T(8,128)(2,1)S(1)}, u32[]{:S(2)}, u32[]{:S(2)}) collective-permute-start(bf16[512,384]{1,0:T(8,128)(2,1)S(1)} %get-tuple-element.116), channel_id=1, source_target_pairs={{0,1},{1,0},{2,3},{3,2},{4,5},{5,4},{6,7},{7,6},{8,9},{9,8},{10,11... | collective-permute-start | bytes 1179656 | tf_op jit(solution)/shard_map/ppermute | solution.py:420
  82.1 15.3 %collective-permute-start.20 = (bf16[384,1536]{1,0:T(8,128)(2,1)S(1)}, bf16[384,1536]{1,0:T(8,128)(2,1)S(1)}, u32[]{:S(2)}, u32[]{:S(2)}) collective-permute-start(bf16[384,1536]{1,0:T(8,128)(2,1)S(1)} %get-tuple-element.105.refs_8_), channel_id=1, source_target_pairs={{0,8},{1,5},{2,10},{3,7},{4,12},{5,1},{6,14},{7,3},{8,0},{9,13},{1... | collective-permute-start | bytes 3538952 | tf_op jit(solution)/shard_map/ppermute | solution.py:447
  88.1 22.5 %collective-permute-start.19 = (bf16[1568,384]{1,0:T(8,128)(2,1)S(1)}, bf16[1568,384]{1,0:T(8,128)(2,1)S(1)}, u32[]{:S(2)}, u32[]{:S(2)}) collective-permute-start(bf16[1568,384]{1,0:T(8,128)(2,1)S(1)} %get-tuple-element.120.refs_2_), channel_id=1, source_target_pairs={{0,2},{1,5},{2,0},{3,7},{4,6},{5,1},{6,4},{7,3},{8,10},{9,13},{10,... | collective-permute-start | bytes 3612680 | tf_op jit(solution)/shard_map/ppermute | solution.py:447
  88.5 32.5 %collective-permute-start.24 = (bf16[384,384]{1,0:T(8,128)(2,1)S(1)}, bf16[384,384]{1,0:T(8,128)(2,1)S(1)}, u32[]{:S(2)}, u32[]{:S(2)}) collective-permute-start(bf16[384,384]{1,0:T(8,128)(2,1)S(1)} %outer1.1.refs_14_), channel_id=1, source_target_pairs={{0,8},{1,9},{2,10},{3,11},{4,12},{5,13},{6,14},{7,15},{8,0},{9,1},... | collective-permute-start | bytes 884744 | tf_op jit(solution)/shard_map/ppermute | solution.py:447
  98.1 21.1 %collective-permute-start.25 = (bf16[192,1536]{1,0:T(8,128)(2,1)S(1)}, bf16[192,1536]{1,0:T(8,128)(2,1)S(1)}, u32[]{:S(2)}, u32[]{:S(2)}) collective-permute-start(bf16[192,1536]{1,0:T(8,128)(2,1)S(1)} %inner0.1.refs_3_), channel_id=1, source_target_pairs={{0,2},{1,9},{2,0},{3,11},{4,6},{5,13},{6,4},{7,15},{8,10},{9,1},{1... | collective-permute-start | bytes 1769480 | tf_op jit(solution)/shard_map/ppermute | solution.py:447
  111.4 13.1 %collective-permute-start.28 = (bf16[800,384]{1,0:T(8,128)(2,1)S(1)}, bf16[800,384]{1,0:T(8,128)(2,1)S(1)}, u32[]{:S(2)}, u32[]{:S(2)}) collective-permute-start(bf16[800,384]{1,0:T(8,128)(2,1)S(1)} %rest0.1.refs_6_.refs_3_), channel_id=1, source_target_pairs={{0,4},{1,3},{2,6},{3,1},{4,0},{5,7},{6,2},{7,5},{8,12},{9,11},{10,... | collective-permute-start | bytes 1843208 | tf_op jit(solution)/shard_map/ppermute | solution.py:447
  112.0 7.3 %copy-start.14 = (bf16[384,1536]{1,0:T(8,128)(2,1)S(1)}, bf16[384,1536]{1,0:T(8,128)(2,1)}, u32[]{:S(2)}) copy-start(bf16[384,1536]{1,0:T(8,128)(2,1)} %copy-done.13) | copy-start | bytes 3538948
  119.9 6.8 %collective-permute-start.27 = (bf16[96,1536]{1,0:T(8,128)(2,1)S(1)}, bf16[96,1536]{1,0:T(8,128)(2,1)S(1)}, u32[]{:S(2)}, u32[]{:S(2)}) collective-permute-start(bf16[96,1536]{1,0:T(8,128)(2,1)S(1)} %inner1.1.refs_4_), channel_id=1, source_target_pairs={{0,4},{1,3},{2,6},{3,1},{4,0},{5,7},{6,2},{7,5},{8,12},{9,11},{10,... | collective-permute-start | bytes 884744 | tf_op jit(solution)/shard_map/ppermute | solution.py:447
  121.5 7.7 %collective-permute-start.26 = (bf16[192,384]{1,0:T(8,128)(2,1)S(1)}, bf16[192,384]{1,0:T(8,128)(2,1)S(1)}, u32[]{:S(2)}, u32[]{:S(2)}) collective-permute-start(bf16[192,384]{1,0:T(8,128)(2,1)S(1)} %outer2.1.refs_4_), channel_id=1, source_target_pairs={{0,16},{1,17},{2,18},{3,19},{4,20},{5,21},{6,22},{7,23},{8,24},{9,... | collective-permute-start | bytes 442376 | tf_op jit(solution)/shard_map/ppermute | solution.py:447
  123.9 7.0 %collective-permute-start.21 = (bf16[128,768]{1,0:T(8,128)(2,1)S(1)}, bf16[128,768]{1,0:T(8,128)(2,1)S(1)}, u32[]{:S(2)}, u32[]{:S(2)}) collective-permute-start(bf16[128,768]{1,0:T(8,128)(2,1)S(1)} %get-tuple-element.124), channel_id=1, source_target_pairs={{0,1},{1,0},{2,3},{3,2},{4,5},{5,4},{6,7},{7,6},{8,9},{9,8},{10,11... | collective-permute-start | bytes 589832 | tf_op jit(solution)/shard_map/ppermute | solution.py:420
  123.9 7.3 %collective-permute-start.22 = (bf16[128,768]{1,0:T(8,128)(2,1)S(1)}, bf16[128,768]{1,0:T(8,128)(2,1)S(1)}, u32[]{:S(2)}, u32[]{:S(2)}) collective-permute-start(bf16[128,768]{1,0:T(8,128)(2,1)S(1)} %get-tuple-element.125), channel_id=1, source_target_pairs={{0,2},{1,3},{2,0},{3,1},{4,6},{5,7},{6,4},{7,5},{8,10},{9,11},{10,... | collective-permute-start | bytes 589832 | tf_op jit(solution)/shard_map/ppermute | solution.py:420
  124.5 11.5 %collective-permute-start.23 = (bf16[128,768]{1,0:T(8,128)(2,1)S(1)}, bf16[128,768]{1,0:T(8,128)(2,1)S(1)}, u32[]{:S(2)}, u32[]{:S(2)}) collective-permute-start(bf16[128,768]{1,0:T(8,128)(2,1)S(1)} %get-tuple-element.126), channel_id=1, source_target_pairs={{0,3},{1,2},{2,1},{3,0},{4,7},{5,6},{6,5},{7,4},{8,11},{9,10},{10,... | collective-permute-start | bytes 589832 | tf_op jit(solution)/shard_map/ppermute | solution.py:420
  126.7 11.9 %collective-permute-start.29 = (bf16[416,384]{1,0:T(8,128)(2,1)S(1)}, bf16[416,384]{1,0:T(8,128)(2,1)S(1)}, u32[]{:S(2)}, u32[]{:S(2)}) collective-permute-start(bf16[416,384]{1,0:T(8,128)(2,1)S(1)} %rest1.1.refs_4_), channel_id=1, source_target_pairs={{0,8},{1,9},{2,10},{3,11},{4,12},{5,13},{6,14},{7,15},{8,0},{9,1},... | collective-permute-start | bytes 958472 | tf_op jit(solution)/shard_map/ppermute | solution.py:447
  129.9 7.6 %collective-permute-start.32 = (bf16[192,384]{1,0:T(8,128)(2,1)S(1)}, bf16[192,384]{1,0:T(8,128)(2,1)S(1)}, u32[]{:S(2)}, u32[]{:S(2)}) collective-permute-start(bf16[192,384]{1,0:T(8,128)(2,1)S(1)} %outer3.1.refs_4_.refs_0_), channel_id=1, source_target_pairs={{0,2},{1,3},{2,0},{3,1},{4,6},{5,7},{6,4},{7,5},{8,10},{9,11},{10,... | collective-permute-start | bytes 442376 | tf_op jit(solution)/shard_map/ppermute | solution.py:420
  130.9 10.7 %collective-permute-start.33 = (bf16[192,384]{1,0:T(8,128)(2,1)S(1)}, bf16[192,384]{1,0:T(8,128)(2,1)S(1)}, u32[]{:S(2)}, u32[]{:S(2)}) collective-permute-start(bf16[192,384]{1,0:T(8,128)(2,1)S(1)} %outer3.1.refs_4_.refs_0_), channel_id=1, source_target_pairs={{0,1},{1,0},{2,3},{3,2},{4,5},{5,4},{6,7},{7,6},{8,9},{9,8},{10,11... | collective-permute-start | bytes 442376 | tf_op jit(solution)/shard_map/ppermute | solution.py:420
  131.2 12.1 %collective-permute-start.31 = (bf16[48,1536]{1,0:T(8,128)(2,1)S(1)}, bf16[48,1536]{1,0:T(8,128)(2,1)S(1)}, u32[]{:S(2)}, u32[]{:S(2)}) collective-permute-start(bf16[48,1536]{1,0:T(8,128)(2,1)S(1)} %inner2.1.refs_5_), channel_id=1, source_target_pairs={{0,16},{1,17},{2,18},{3,19},{4,20},{5,21},{6,22},{7,23},{8,24},{9,... | collective-permute-start | bytes 442376 | tf_op jit(solution)/shard_map/ppermute | solution.py:447
  137.5 4.1 %collective-permute-start.34 = (bf16[192,384]{1,0:T(8,128)(2,1)S(1)}, bf16[192,384]{1,0:T(8,128)(2,1)S(1)}, u32[]{:S(2)}, u32[]{:S(2)}) collective-permute-start(bf16[192,384]{1,0:T(8,128)(2,1)S(1)} %collective-permute-done.32.refs_1_), channel_id=1, source_target_pairs={{0,1},{1,0},{2,3},{3,2},{4,5},{5,4},{6,7},{7,6},{8,9},{9,8},{10,11... | collective-permute-start | bytes 442376 | tf_op jit(solution)/shard_map/ppermute | solution.py:420
  140.4 10.6 %collective-permute-start.30 = (bf16[224,384]{1,0:T(8,128)(2,1)S(1)}, bf16[224,384]{1,0:T(8,128)(2,1)S(1)}, u32[]{:S(2)}, u32[]{:S(2)}) collective-permute-start(bf16[224,384]{1,0:T(8,128)(2,1)S(1)} %rest2.1.refs_4_.refs_5_), channel_id=1, source_target_pairs={{0,16},{1,17},{2,18},{3,19},{4,20},{5,21},{6,22},{7,23},{8,24},{9,... | collective-permute-start | bytes 516104 | tf_op jit(solution)/shard_map/ppermute | solution.py:447
  145.2 8.7 %collective-permute-start.38 = (bf16[48,1536]{1,0:T(8,128)(2,1)S(1)}, bf16[48,1536]{1,0:T(8,128)(2,1)S(1)}, u32[]{:S(2)}, u32[]{:S(2)}) collective-permute-start(bf16[48,1536]{1,0:T(8,128)(2,1)S(1)} %inner3.1.refs_6_.refs_0_), channel_id=1, source_target_pairs={{0,2},{1,3},{2,0},{3,1},{4,6},{5,7},{6,4},{7,5},{8,10},{9,11},{10,... | collective-permute-start | bytes 442376 | tf_op jit(solution)/shard_map/ppermute | solution.py:420
  151.6 5.1 %collective-permute-start.35 = (bf16[224,384]{1,0:T(8,128)(2,1)S(1)}, bf16[224,384]{1,0:T(8,128)(2,1)S(1)}, u32[]{:S(2)}, u32[]{:S(2)}) collective-permute-start(bf16[224,384]{1,0:T(8,128)(2,1)S(1)} %rest3.1.refs_4_.refs_0_), channel_id=1, source_target_pairs={{0,2},{1,3},{2,0},{3,1},{4,6},{5,7},{6,4},{7,5},{8,10},{9,11},{10,... | collective-permute-start | bytes 516104 | tf_op jit(solution)/shard_map/ppermute | solution.py:420
  152.5 6.0 %collective-permute-start.39 = (bf16[48,1536]{1,0:T(8,128)(2,1)S(1)}, bf16[48,1536]{1,0:T(8,128)(2,1)S(1)}, u32[]{:S(2)}, u32[]{:S(2)}) collective-permute-start(bf16[48,1536]{1,0:T(8,128)(2,1)S(1)} %inner3.1.refs_6_.refs_0_), channel_id=1, source_target_pairs={{0,1},{1,0},{2,3},{3,2},{4,5},{5,4},{6,7},{7,6},{8,9},{9,8},{10,11... | collective-permute-start | bytes 442376 | tf_op jit(solution)/shard_map/ppermute | solution.py:420
  153.9 4.6 %collective-permute-start.40 = (bf16[48,1536]{1,0:T(8,128)(2,1)S(1)}, bf16[48,1536]{1,0:T(8,128)(2,1)S(1)}, u32[]{:S(2)}, u32[]{:S(2)}) collective-permute-start(bf16[48,1536]{1,0:T(8,128)(2,1)S(1)} %collective-permute-done.38.refs_1_), channel_id=1, source_target_pairs={{0,1},{1,0},{2,3},{3,2},{4,5},{5,4},{6,7},{7,6},{8,9},{9,8},{10,11... | collective-permute-start | bytes 442376 | tf_op jit(solution)/shard_map/ppermute | solution.py:420
  153.9 6.2 %collective-permute-start.36 = (bf16[224,384]{1,0:T(8,128)(2,1)S(1)}, bf16[224,384]{1,0:T(8,128)(2,1)S(1)}, u32[]{:S(2)}, u32[]{:S(2)}) collective-permute-start(bf16[224,384]{1,0:T(8,128)(2,1)S(1)} %rest3.1.refs_4_.refs_0_), channel_id=1, source_target_pairs={{0,1},{1,0},{2,3},{3,2},{4,5},{5,4},{6,7},{7,6},{8,9},{9,8},{10,11... | collective-permute-start | bytes 516104 | tf_op jit(solution)/shard_map/ppermute | solution.py:420
  156.8 3.4 %collective-permute-start.37 = (bf16[224,384]{1,0:T(8,128)(2,1)S(1)}, bf16[224,384]{1,0:T(8,128)(2,1)S(1)}, u32[]{:S(2)}, u32[]{:S(2)}) collective-permute-start(bf16[224,384]{1,0:T(8,128)(2,1)S(1)} %collective-permute-done.35.refs_1_), channel_id=1, source_target_pairs={{0,1},{1,0},{2,3},{3,2},{4,5},{5,4},{6,7},{7,6},{8,9},{9,8},{10,11... | collective-permute-start | bytes 516104 | tf_op jit(solution)/shard_map/ppermute | solution.py:420
  (14 other events, 33.1 us)

commit v2 on v1

--- a/solution.py
+++ b/solution.py
@@ -110,18 +110,18 @@
     for i, part in enumerate((x0, x1, x2, x3)):
         x_ref[i * block : (i + 1) * block, :] = part[...]
     x = x_ref[...]
-    copies[0].wait()
-    for at in columns(width):
+    for c in copies[:3]:
+        c.wait()
+
+    def tile(at):
         q = (nn(x, wq_ref[:, at]) + bq_ref[:, at].astype(F32)).astype(BF16)
         q_ref[:, at] = q * jnp.asarray(HD ** -0.5, BF16)
-    copies[1].wait()
-    for at in columns(width):
         k_ref[:, at] = nn(x, wk_ref[:, at]).astype(BF16)
-    copies[2].wait()
-    for at in columns(width):
         v_ref[:, at] = (nn(x, wv_ref[:, at]) + bv_ref[:, at].astype(F32)).astype(BF16)
-    def pair(p):
-        at = pl.ds(pl.multiple_of(p * PAIR, PAIR), PAIR)
+
+    tiles_loop(width, 1, tile)
+    for p in range(width // PAIR):
+        at = slice(p * PAIR, (p + 1) * PAIR)
         q, k, v = q_ref[:, at], k_ref[:, at], v_ref[:, at]
         vt = v.astype(F32).T.astype(BF16)
         out = []
@@ -132,13 +132,6 @@
             p_ref[2 * p + i] = w
             out.append(nn(vt[i * HD : (i + 1) * HD], w))
         ctx_ref[:, at] = jnp.concatenate(out, axis=0).T.astype(BF16)
-
-    def step(i, carry):
-        for j in range(3):
-            pair(3 * i + j)
-        return carry
-
-    lax.fori_loop(0, width // PAIR // 3, step, 0)
     copies[3].wait()
     v1 = jnp.concatenate([nn(ctx_ref[...], wo_ref[:, at]) for at in columns(width)], axis=1)
     v1 = x_ref[...].astype(F32) + (v1 + bo_ref[...].astype(F32))
@@ -305,8 +298,10 @@
 
 def inner_kernel(base, rows):
     def kernel(info_ref, la, lb, ra, rb, keep_ref, send_ref, buf_ref):
-        for at in columns(ra.shape[1]):
+        def tile(at):
             buf_ref[:, at] = (tn(la[...], ra[:, at]) + tn(lb[...], rb[:, at])).astype(BF16)
+
+        tiles_loop(ra.shape[1], 3, tile)
         place(info_ref, base, rows, buf_ref, keep_ref, send_ref)
 
     return kernel

time: 165 us -> 164 us (level)
  no operation moved by 1% of the time
where the time goes in v2:
time: 164 us
  Pallas kernels  83 us (51%)
  starting transfers between devices  35.9 us (22%)
  waiting for transfers between devices  35.8 us (22%)
  local copies, waits for them, and re-layouts  6.8 us (4%)
    pallas_call x31, Pallas kernels, call(): pl.pallas_call(run, in_specs=[pl.BlockSpec(memory_space=pltpu.SMEM)] + [p...  83 us
    ppermute x12, waiting for transfers between devices, exchange(): return lax.ppermute(value, ('dp', 'seq'), moves)  25 us
    ppermute x29, starting transfers between devices, swap(): return lax.ppermute(value, axis, [(i, i ^ bit) for i in range(size)])  20.7 us
    ppermute x12, starting transfers between devices, exchange(): return lax.ppermute(value, ('dp', 'seq'), moves)  15.3 us
    ppermute x29, waiting for transfers between devices, swap(): return lax.ppermute(value, axis, [(i, i ^ bit) for i in range(size)])  10.8 us
    unnamed x74, local copies, waits for them, and re-layouts  6.12 us
  transfers between devices with their start and end apart: 41, of which 8 were waited for; matrix products, arithmetic and copies ran while one was open for 0% of the time, Pallas kernels for 45%

profile of v2, /device:TPU:1, one launch (start us, length us, event | category | flops | bytes accessed | tf_op | source)
XLA Modules:
  0.0 163.7 jit_solution(281601038836418307)
XLA Ops:
  0.8 1.1 copy-done.5
  1.9 1.6 deal_inputs.1
  3.7 2.7 %collective-permute-start.1 = (bf16[128,768]{1,0:T(8,128)(2,1)S(1)}, bf16[128,768]{1,0:T(8,128)(2,1)S(1)}, u32[]{:S(2)}, u32[]{:S(2)}) collective-permute-start(bf16[128,768]{1,0:T(8,128)(2,1)S(1)} %get-tuple-element.77), channel_id=1, source_target_pairs={{0,2},{1,3},{2,0},{3,1},{4,6},{5,7},{6,4},{7,5},{8,10},{9,11},{10,... | collective-permute-start | bytes 589832 | tf_op jit(solution)/shard_map/ppermute | solution.py:415
  6.7 1.6 deal_cotangent.1
  8.7 1.4 collective-permute-start.4
  10.7 0.8 collective-permute-done.1.refs_2_
  11.5 4.4 %collective-permute-done.2.refs_3_ = bf16[128,768]{1,0:T(8,128)(2,1)S(1)} collective-permute-done((bf16[128,768]{1,0:T(8,128)(2,1)S(1)}, bf16[128,768]{1,0:T(8,128)(2,1)S(1)}, u32[]{:S(2)}, u32[]{:S(2)}) %collective-permute-start.2) | collective-permute-done | bytes 196640 | tf_op jit(solution)/shard_map/ppermute | solution.py:415
  16.0 12.4 %attention.1 = (bf16[512,768]{1,0:T(8,128)(2,1)S(1)}, bf16[512,768]{1,0:T(8,128)(2,1)S(1)}, bf16[512,768]{1,0:T(8,128)(2,1)S(1)}, bf16[512,768]{1,0:T(8,128)(2,1...) custom-call(s32[51]{0:T(128)S(1)} %concatenate.3.info_ref, ...), custom_call_target="tpu_custom_call" | custom-call | flops 38999998464 | bytes 1 | tf_op jit(solution)/shard_map/attention/pallas_call | solution.py:45
  28.6 6.1 %hidden.1 = (bf16[512,3072]{1,0:T(8,128)(2,1)S(1)}, bf16[512,3072]{1,0:T(8,128)(2,1)S(1)}) custom-call(s32[51]{0:T(128)S(1)} %concatenate.3.info_ref, bf16[512,768]{1,0:T(8,128)(2,1)S(1)} %get-tuple-element.79.refs_0_, bf16[768,3072]{1,0:T(8,128)(2,1)S(1)} %bitcast.22, bf16[1,3072]{1,0:T(2,128)(2,1)S(1)} %reshape.71.refs_2_, ...), custom_call_target="tpu_custom_call" | custom-call | flops 27000000512 | bytes 1 | tf_op jit(solution)/shard_map/hidden/pallas_call | solution.py:45
  35.3 4.5 %branch.1 = (bf16[128,768]{1,0:T(8,128)(2,1)S(1)}, bf16[128,768]{1,0:T(8,128)(2,1)S(1)}, bf16[128,768]{1,0:T(8,128)(2,1)S(1)}, bf16[128,768]{1,0:T(8,128)(2,1)S(...) custom-call(s32[51]{0:T(128)S(1)} %concatenate.3.info_ref, ...), custom_call_target="tpu_custom_call" | custom-call | flops 12000000000 | bytes 1 | tf_op jit(solution)/shard_map/branch/pallas_call | solution.py:45
  40.4 1.7 %collective-permute-start.7 = (bf16[128,768]{1,0:T(8,128)(2,1)S(1)}, bf16[128,768]{1,0:T(8,128)(2,1)S(1)}, u32[]{:S(2)}, u32[]{:S(2)}) collective-permute-start(bf16[128,768]{1,0:T(8,128)(2,1)S(1)} %get-tuple-element.88), channel_id=1, source_target_pairs={{0,2},{1,3},{2,0},{3,1},{4,6},{5,7},{6,4},{7,5},{8,10},{9,11},{10,... | collective-permute-start | bytes 589832 | tf_op jit(solution)/shard_map/ppermute | solution.py:415
  42.2 2.0 %hidden_back_other.1 = (bf16[512,1536]{1,0:T(8,128)(2,1)S(1)}, f32[1,1536]{1,0:T(1,128)S(1)}) custom-call(s32[51]{0:T(128)S(1)} %concatenate.3.info_ref, bf16[512,768]{1,0:T(8,128)(2,1)S(1)} %get-tuple-element.92.refs_0_, bf16[3072,768]{1,0:T(8,128)(2,1)S(1)} %bitcast.20, bf16[512,3072]{1,0:T(8,128)(2,1)S(1)} %get-tuple-element.93.refs_2_, ...), custom_call_target="tpu_custom_call" | custom-call | flops 8999999488 | bytes 1 | tf_op jit(solution)/shard_map/hidden_back_other/pallas_call | solution.py:45
  44.7 2.0 %hidden_back_mine.1 = (bf16[512,1536]{1,0:T(8,128)(2,1)S(1)}, f32[1,1536]{1,0:T(1,128)S(1)}) custom-call(s32[51]{0:T(128)S(1)} %concatenate.3.info_ref, bf16[512,768]{1,0:T(8,128)(2,1)S(1)} %get-tuple-element.92.refs_0_, bf16[3072,768]{1,0:T(8,128)(2,1)S(1)} %bitcast.20, bf16[512,3072]{1,0:T(8,128)(2,1)S(1)} %get-tuple-element.93.refs_2_, ...), custom_call_target="tpu_custom_call" | custom-call | flops 8999999488 | bytes 1 | tf_op jit(solution)/shard_map/hidden_back_mine/pallas_call | solution.py:45
  46.7 5.1 %grad_outer.1 = (bf16[1536,384]{1,0:T(8,128)(2,1)S(1)}, bf16[1536,384]{1,0:T(8,128)(2,1)S(1)}) custom-call(s32[51]{0:T(128)S(1)} %concatenate.3.info_ref, bf16[512,3072]{1,0:T(8,128)(2,1)S(1)} %get-tuple-element.84.refs_0_, bf16[512,3072]{1,0:T(8,128)(2,1)S(1)} %collective-permute-done.9.refs_3_.refs_1_, bf16[512,384]{1,0:T(8,128)(2,1)S(1)} %get-tuple-element.90.refs_2_, ...), custom_call_target="tpu_custom_call" | custom-call | flops 15000000512 | bytes 1 | tf_op jit(solution)/shard_map/grad_outer/pallas_call | solution.py:45
  51.9 1.5 collective-permute-start.13
  53.4 1.5 collect_outputs.1.refs_4_
  54.9 1.1 copy-done.8
  56.0 3.7 %grad_inner.1 = (bf16[384,1536]{1,0:T(8,128)(2,1)S(1)}, bf16[384,1536]{1,0:T(8,128)(2,1)S(1)}) custom-call(s32[51]{0:T(128)S(1)} %concatenate.3.info_ref, bf16[512,768]{1,0:T(8,128)(2,1)S(1)} %get-tuple-element.79.refs_0_, bf16[512,768]{1,0:T(8,128)(2,1)S(1)} %collective-permute-done.11.refs_1_, bf16[512,1536]{1,0:T(8,128)(2,1)S(1)} %get-tuple-element.101.refs_2_.refs_0_, ...), custom_call_target="tpu_custom_call" | custom-call | flops 12000000000 | bytes 1 | tf_op jit(solution)/shard_map/grad_inner/pallas_call | solution.py:45
  59.8 5.5 %first_back.1 = (f32[512,768]{1,0:T(8,128)S(1)}, bf16[512,768]{1,0:T(8,128)(2,1)S(1)}, bf16[512,384]{1,0:T(8,128)(2,1)S(1)}, bf16[512,384]{1,0:T(8,128)(2,1)S(1)}, f32[3,768]{1,0:T(4,128)S(1)}) custom-call(s32[51]{0:T(128)S(1)} %concatenate.3.info_ref, bf16[512,1536]{1,0:T(8,128)(2,1)S(1)} %get-tuple-element.101.refs_2_.refs_0_, ...), custom_call_target="tpu_custom_call" | custom-call | flops 17999998976 | bytes 1 | tf_op jit(solution)/shard_map/first_back/pallas_call | solution.py:45
  65.3 5.8 %attention_back_other.1 = (bf16[3,512,384]{2,1,0:T(8,128)(2,1)S(1)}, f32[3,384]{1,0:T(4,128)S(1)}) custom-call(s32[51]{0:T(128)S(1)} %concatenate.3.info_ref, bf16[512,768]{1,0:T(8,128)(2,1)S(1)} %get-tuple-element.97.refs_0_, bf16[512,768]{1,0:T(8,128)(2,1)S(1)} %get-tuple-element.98.refs_1_, bf16[512,768]{1,0:T(8,128)(2,1)S(1)} %get-tuple-element.99.refs_2_, ...), custom_call_target="tpu_custom_call" | custom-call | flops 3000000000 | bytes 1 | tf_op jit(solution)/shard_map/attention_back_other/pallas_call | solution.py:45
  71.0 0.7 collective-permute-start.16
  71.8 0.7 outer0.1.refs_5_
  72.5 0.8 collective-permute-start.18
  73.3 0.9 collective-permute-start.14
  74.7 5.6 %attention_back_mine.1 = (bf16[3,512,384]{2,1,0:T(8,128)(2,1)S(1)}, f32[3,384]{1,0:T(4,128)S(1)}) custom-call(s32[51]{0:T(128)S(1)} %concatenate.3.info_ref, bf16[512,768]{1,0:T(8,128)(2,1)S(1)} %get-tuple-element.97.refs_0_, bf16[512,768]{1,0:T(8,128)(2,1)S(1)} %get-tuple-element.98.refs_1_, bf16[512,768]{1,0:T(8,128)(2,1)S(1)} %get-tuple-element.99.refs_2_, ...), custom_call_target="tpu_custom_call" | custom-call | flops 3000000000 | bytes 1 | tf_op jit(solution)/shard_map/attention_back_mine/pallas_call | solution.py:45
  80.3 1.3 collective-permute-done.18.refs_2_
  81.6 1.2 collective-permute-start.20
  82.8 0.7 outer1.1.refs_14_
  83.5 4.1 %grad_rest.1 = (bf16[1536,384]{1,0:T(8,128)(2,1)S(1)}, bf16[1568,384]{1,0:T(8,128)(2,1)S(1)}, f32[16,768]{1,0:T(8,128)S(1)}) custom-call(s32[51]{0:T(128)S(1)} %concatenate.3.info_ref, bf16[512,768]{1,0:T(8,128)(2,1)S(1)} %get-tuple-element.113.refs_0_, bf16[512,768]{1,0:T(8,128)(2,1)S(1)} %collective-permute-done.14.refs_1_, ...), custom_call_target="tpu_custom_call" | custom-call | flops 3000000000 | bytes 1 | tf_op jit(solution)/shard_map/grad_rest/pallas_call | solution.py:45
  87.9 1.3 collective-permute-start.24
  89.2 7.7 %collective-permute-done.20.refs_1_ = bf16[384,1536]{1,0:T(8,128)(2,1)S(1)} collective-permute-done((bf16[384,1536]{1,0:T(8,128)(2,1)S(1)}, bf16[384,1536]{1,0:T(8,128)(2,1)S(1)}, u32[]{:S(2)}, u32[]{:S(2)}) %collective-permute-start.20) | collective-permute-done | bytes 1179680 | tf_op jit(solution)/shard_map/ppermute | solution.py:442
  96.9 0.7 inner0.1.refs_3_
  97.6 1.4 collective-permute-start.25
  99.0 11.2 %collective-permute-done.19.refs_1_ = bf16[1568,384]{1,0:T(8,128)(2,1)S(1)} collective-permute-done((bf16[1568,384]{1,0:T(8,128)(2,1)S(1)}, bf16[1568,384]{1,0:T(8,128)(2,1)S(1)}, u32[]{:S(2)}, u32[]{:S(2)}) %collective-permute-start.19) | collective-permute-done | bytes 1204256 | tf_op jit(solution)/shard_map/ppermute | solution.py:442
  110.1 0.7 rest0.1.refs_6_.refs_3_
  110.8 0.7 collective-permute-start.28
  111.5 7.2 %input_back.1 = (bf16[128,768]{1,0:T(8,128)(2,1)S(1)}, bf16[128,768]{1,0:T(8,128)(2,1)S(1)}, bf16[128,768]{1,0:T(8,128)(2,1)S(1)}, bf16[128,768]{1,0:T(8,128)(2,1)S(1)}) custom-call(s32[51]{0:T(128)S(1)} %concatenate.3.info_ref, bf16[3,512,384]{2,1,0:T(8,128)(2,1)} %copy-done.12, bf16[3,512,384]{2,1,0:T(8,128)(2,1)} %copy-done.4, f32[512,768]{1,0:T(8,128)} %copy-done.17, ...), custom_call_target="tpu_custom_call" | custom-call | flops 6000000000 | bytes 1 | tf_op jit(solution)/shard_map/input_back/pallas_call | solution.py:45
  118.8 0.7 inner1.1.refs_4_
  119.5 0.9 collective-permute-start.27
  121.0 2.4 %collective-permute-start.26 = (bf16[192,384]{1,0:T(8,128)(2,1)S(1)}, bf16[192,384]{1,0:T(8,128)(2,1)S(1)}, u32[]{:S(2)}, u32[]{:S(2)}) collective-permute-start(bf16[192,384]{1,0:T(8,128)(2,1)S(1)} %outer2.1.refs_4_), channel_id=1, source_target_pairs={{0,16},{1,17},{2,18},{3,19},{4,20},{5,21},{6,22},{7,23},{8,24},{9,... | collective-permute-start | bytes 442376 | tf_op jit(solution)/shard_map/ppermute | solution.py:442
  123.9 1.6 collective-permute-start.23
  125.5 0.7 rest1.1.refs_4_
  126.2 1.9 %collective-permute-start.29 = (bf16[416,384]{1,0:T(8,128)(2,1)S(1)}, bf16[416,384]{1,0:T(8,128)(2,1)S(1)}, u32[]{:S(2)}, u32[]{:S(2)}) collective-permute-start(bf16[416,384]{1,0:T(8,128)(2,1)S(1)} %rest1.1.refs_4_), channel_id=1, source_target_pairs={{0,8},{1,9},{2,10},{3,11},{4,12},{5,13},{6,14},{7,15},{8,0},{9,1},... | collective-permute-start | bytes 958472 | tf_op jit(solution)/shard_map/ppermute | solution.py:442
  128.7 0.6 outer3.1.refs_4_.refs_0_
  129.4 1.0 collective-permute-start.32
  130.6 1.7 %collective-permute-start.31 = (bf16[48,1536]{1,0:T(8,128)(2,1)S(1)}, bf16[48,1536]{1,0:T(8,128)(2,1)S(1)}, u32[]{:S(2)}, u32[]{:S(2)}) collective-permute-start(bf16[48,1536]{1,0:T(8,128)(2,1)S(1)} %inner2.1.refs_5_), channel_id=1, source_target_pairs={{0,16},{1,17},{2,18},{3,19},{4,20},{5,21},{6,22},{7,23},{8,24},{9,... | collective-permute-start | bytes 442376 | tf_op jit(solution)/shard_map/ppermute | solution.py:442
  132.3 3.2 %collective-permute-done.23.refs_3_ = bf16[128,768]{1,0:T(8,128)(2,1)S(1)} collective-permute-done((bf16[128,768]{1,0:T(8,128)(2,1)S(1)}, bf16[128,768]{1,0:T(8,128)(2,1)S(1)}, u32[]{:S(2)}, u32[]{:S(2)}) %collective-permute-start.23) | collective-permute-done | bytes 196640 | tf_op jit(solution)/shard_map/ppermute | solution.py:415
  135.5 1.5 collect_inputs.1.refs_5_
  136.9 1.1 collective-permute-start.34
  138.1 1.1 copy-done.9
  139.8 1.2 collective-permute-start.30
  141.1 1.6 %finish_outer.1.refs_5_ = f32[384,768]{1,0:T(8,128)} custom-call(s32[51]{0:T(128)S(1)} %concatenate.3.info_ref, bf16[192,384]{1,0:T(8,128)(2,1)S(1)} %outer3.1.refs_4_.refs_0_, bf16[192,384]{1,0:T(8,128)(2,1)S(1)} %collective-permute-done.32.refs_1_, bf16[192,384]{1,0:T(8,128)(2,1)S(1)} %collective-permute-done.33.refs_2_, ...), custom_call_target="tpu_custom_call" | custom-call | flops 3000000000 | bytes 1 | tf_op jit(solution)/shard_map/finish_outer/pallas_call | solution.py:45
  142.7 1.3 copy-done.6
  144.0 0.6 inner3.1.refs_6_.refs_0_
  144.6 1.0 collective-permute-start.38
  145.6 4.8 %collective-permute-done.30.refs_4_ = bf16[224,384]{1,0:T(8,128)(2,1)S(1)} collective-permute-done((bf16[224,384]{1,0:T(8,128)(2,1)S(1)}, bf16[224,384]{1,0:T(8,128)(2,1)S(1)}, u32[]{:S(2)}, u32[]{:S(2)}) %collective-permute-start.30) | collective-permute-done | bytes 172064 | tf_op jit(solution)/shard_map/ppermute | solution.py:442
  150.4 0.7 rest3.1.refs_4_.refs_0_
  151.1 0.9 collective-permute-start.35
  152.0 1.4 collective-permute-start.39
  153.9 2.3 %collective-permute-done.35.refs_1_ = bf16[224,384]{1,0:T(8,128)(2,1)S(1)} collective-permute-done((bf16[224,384]{1,0:T(8,128)(2,1)S(1)}, bf16[224,384]{1,0:T(8,128)(2,1)S(1)}, u32[]{:S(2)}, u32[]{:S(2)}) %collective-permute-start.35) | collective-permute-done | bytes 172064 | tf_op jit(solution)/shard_map/ppermute | solution.py:415
  156.2 1.7 %collective-permute-start.37 = (bf16[224,384]{1,0:T(8,128)(2,1)S(1)}, bf16[224,384]{1,0:T(8,128)(2,1)S(1)}, u32[]{:S(2)}, u32[]{:S(2)}) collective-permute-start(bf16[224,384]{1,0:T(8,128)(2,1)S(1)} %collective-permute-done.35.refs_1_), channel_id=1, source_target_pairs={{0,1},{1,0},{2,3},{3,2},{4,5},{5,4},{6,7},{7,6},{8,9},{9,8},{10,11... | collective-permute-start | bytes 516104 | tf_op jit(solution)/shard_map/ppermute | solution.py:415
  158.0 1.6 %finish_inner.1.refs_4_ = f32[96,3072]{1,0:T(8,128)} custom-call(s32[51]{0:T(128)S(1)} %concatenate.3.info_ref, bf16[48,1536]{1,0:T(8,128)(2,1)S(1)} %inner3.1.refs_6_.refs_0_, bf16[48,1536]{1,0:T(8,128)(2,1)S(1)} %collective-permute-done.38.refs_1_, bf16[48,1536]{1,0:T(8,128)(2,1)S(1)} %collective-permute-done.39.refs_2_, ...), custom_call_target="tpu_custom_call" | custom-call | flops 3000000000 | bytes 1 | tf_op jit(solution)/shard_map/finish_inner/pallas_call | solution.py:45
  159.6 1.3 copy-done.7
  160.9 1.7 %finish_rest.1 = (f32[96,768]{1,0:T(8,128)}, f32[96,768]{1,0:T(8,128)}, f32[96,768]{1,0:T(8,128)}, f32[96,768]{1,0:T(8,128)}, f32[16,128]{1,0:T(8,128)S(1)}, /*index=5*/f32[1,384]{1,0:T(1,128)S(1)}) custom-call(s32[51]{0:T(128)S(1)} %concatenate.3.info_ref, bf16[224,384]{1,0:T(8,128)(2,1)S(1)} %rest3.1.refs_4_.refs_0_, ...), custom_call_target="tpu_custom_call" | custom-call | flops 3000000000 | bytes 1 | tf_op jit(solution)/shard_map/finish_rest/pallas_call | solution.py:45
  (140 shorter events, 8.4 us)
Async XLA Ops:
  1.9 4.5 %copy-start.24 = (s32[4,128]{1,0:T(4,128)S(1)}, s32[4,128]{1,0:T(4,128)}, u32[]{:S(2)}) copy-start(s32[4,128]{1,0:T(4,128)} %param.20) | copy-start | bytes 6148
  1.9 4.5 %copy-start.22 = (bf16[4,128,768]{2,1,0:T(8,128)(2,1)S(1)}, bf16[4,128,768]{2,1,0:T(8,128)(2,1)}, u32[]{:S(2)}) copy-start(bf16[4,128,768]{2,1,0:T(8,128)(2,1)} %param.19) | copy-start | bytes 2359300
  1.9 14.1 %copy-start.3 = (bf16[768,768]{1,0:T(8,128)(2,1)S(1)}, bf16[768,768]{1,0:T(8,128)(2,1)}, u32[]{:S(2)}) copy-start(bf16[768,768]{1,0:T(8,128)(2,1)} %refs_5_.1) | copy-start | bytes 3538948
  3.5 6.8 %collective-permute-start = (bf16[128,768]{1,0:T(8,128)(2,1)S(1)}, bf16[128,768]{1,0:T(8,128)(2,1)S(1)}, u32[]{:S(2)}, u32[]{:S(2)}) collective-permute-start(bf16[128,768]{1,0:T(8,128)(2,1)S(1)} %get-tuple-element.76), channel_id=1, source_target_pairs={{0,1},{1,0},{2,3},{3,2},{4,5},{5,4},{6,7},{7,6},{8,9},{9,8},{10,11... | collective-permute-start | bytes 589832 | tf_op jit(solution)/shard_map/ppermute | solution.py:415
  3.7 7.9 %collective-permute-start.1 = (bf16[128,768]{1,0:T(8,128)(2,1)S(1)}, bf16[128,768]{1,0:T(8,128)(2,1)S(1)}, u32[]{:S(2)}, u32[]{:S(2)}) collective-permute-start(bf16[128,768]{1,0:T(8,128)(2,1)S(1)} %get-tuple-element.77), channel_id=1, source_target_pairs={{0,2},{1,3},{2,0},{3,1},{4,6},{5,7},{6,4},{7,5},{8,10},{9,11},{10,... | collective-permute-start | bytes 589832 | tf_op jit(solution)/shard_map/ppermute | solution.py:415
  6.4 9.6 %collective-permute-start.2 = (bf16[128,768]{1,0:T(8,128)(2,1)S(1)}, bf16[128,768]{1,0:T(8,128)(2,1)S(1)}, u32[]{:S(2)}, u32[]{:S(2)}) collective-permute-start(bf16[128,768]{1,0:T(8,128)(2,1)S(1)} %get-tuple-element.78), channel_id=1, source_target_pairs={{0,3},{1,2},{2,1},{3,0},{4,7},{5,6},{6,5},{7,4},{8,11},{9,10},{10,... | collective-permute-start | bytes 589832 | tf_op jit(solution)/shard_map/ppermute | solution.py:415
  6.4 9.6 %copy-start.2 = (bf16[768,768]{1,0:T(8,128)(2,1)S(1)}, bf16[768,768]{1,0:T(8,128)(2,1)}, u32[]{:S(2)}) copy-start(bf16[768,768]{1,0:T(8,128)(2,1)} %refs_4_.1) | copy-start | bytes 3538948
  6.6 3.7 %copy-start.23 = (bf16[3072]{0:T(1024)(128)(2,1)S(1)}, bf16[3072]{0:T(1024)(128)(2,1)}, u32[]{:S(2)}) copy-start(bf16[3072]{0:T(1024)(128)(2,1)} %param.31) | copy-start | bytes 18436
  6.6 9.3 %copy-start = (bf16[768,768]{1,0:T(8,128)(2,1)S(1)}, bf16[768,768]{1,0:T(8,128)(2,1)}, u32[]{:S(2)}) copy-start(bf16[768,768]{1,0:T(8,128)(2,1)} %refs_7_.1) | copy-start | bytes 3538948
  6.7 9.3 %copy-start.1 = (bf16[768,768]{1,0:T(8,128)(2,1)S(1)}, bf16[768,768]{1,0:T(8,128)(2,1)}, u32[]{:S(2)}) copy-start(bf16[768,768]{1,0:T(8,128)(2,1)} %refs_3_.1) | copy-start | bytes 3538948
  6.7 21.8 %slice-start.2 = ((s8[4718592]{0:T(1024)(128)(4,1)}), s8[4194304]{0:T(1024)(128)(4,1)S(1)}, s32[]{:S(2)}) async-start(s8[4718592]{0:T(1024)(128)(4,1)} %bitcast.21), calls=%async_computation.2 | async-start | bytes 8388608
  6.7 28.6 %slice-start = ((s8[4718592]{0:T(1024)(128)(4,1)}), s8[4194304]{0:T(1024)(128)(4,1)S(1)}, s32[]{:S(2)}) async-start(s8[4718592]{0:T(1024)(128)(4,1)} %bitcast.19), calls=%async_computation | async-start | bytes 8388608
  8.3 20.2 %collective-permute-start.3 = (bf16[128,768]{1,0:T(8,128)(2,1)S(1)}, bf16[128,768]{1,0:T(8,128)(2,1)S(1)}, u32[]{:S(2)}, u32[]{:S(2)}) collective-permute-start(bf16[128,768]{1,0:T(8,128)(2,1)S(1)} %get-tuple-element.81), channel_id=1, source_target_pairs={{0,1},{1,0},{2,3},{3,2},{4,5},{5,4},{6,7},{7,6},{8,9},{9,8},{10,11... | collective-permute-start | bytes 589832 | tf_op jit(solution)/shard_map/ppermute | solution.py:415
  8.7 19.7 %collective-permute-start.4 = (bf16[128,768]{1,0:T(8,128)(2,1)S(1)}, bf16[128,768]{1,0:T(8,128)(2,1)S(1)}, u32[]{:S(2)}, u32[]{:S(2)}) collective-permute-start(bf16[128,768]{1,0:T(8,128)(2,1)S(1)} %get-tuple-element.82), channel_id=1, source_target_pairs={{0,2},{1,3},{2,0},{3,1},{4,6},{5,7},{6,4},{7,5},{8,10},{9,11},{10,... | collective-permute-start | bytes 589832 | tf_op jit(solution)/shard_map/ppermute | solution.py:415
  10.3 18.2 %collective-permute-start.5 = (bf16[128,768]{1,0:T(8,128)(2,1)S(1)}, bf16[128,768]{1,0:T(8,128)(2,1)S(1)}, u32[]{:S(2)}, u32[]{:S(2)}) collective-permute-start(bf16[128,768]{1,0:T(8,128)(2,1)S(1)} %get-tuple-element.83), channel_id=1, source_target_pairs={{0,3},{1,2},{2,1},{3,0},{4,7},{5,6},{6,5},{7,4},{8,11},{9,10},{10,... | collective-permute-start | bytes 589832 | tf_op jit(solution)/shard_map/ppermute | solution.py:415
  16.0 12.5 %slice-start.3 = ((s8[4718592]{0:T(1024)(128)(4,1)}), s8[524288]{0:T(1024)(128)(4,1)S(1)}, s32[]{:S(2)}) async-start(s8[4718592]{0:T(1024)(128)(4,1)} %bitcast.21), calls=%async_computation.3 | async-start | bytes 1048576
  16.0 19.3 %slice-start.1 = ((s8[4718592]{0:T(1024)(128)(4,1)}), s8[524288]{0:T(1024)(128)(4,1)S(1)}, s32[]{:S(2)}) async-start(s8[4718592]{0:T(1024)(128)(4,1)} %bitcast.19), calls=%async_computation.1 | async-start | bytes 1048576
  28.5 6.9 %copy-start.18 = (f32[512,768]{1,0:T(8,128)}, f32[512,768]{1,0:T(8,128)S(1)}, u32[]{:S(2)}) copy-start(f32[512,768]{1,0:T(8,128)S(1)} %get-tuple-element.85.refs_3_.refs_4_) | copy-start | bytes 4718596
  28.5 36.8 %copy-start.10 = (bf16[12,512,512]{2,1,0:T(8,128)(2,1)}, bf16[12,512,512]{2,1,0:T(8,128)(2,1)S(1)}, u32[]{:S(2)}) copy-start(bf16[12,512,512]{2,1,0:T(8,128)(2,1)S(1)} %get-tuple-element.100.refs_3_) | copy-start | bytes 18874372
  28.5 6.3 %copy-start.30 = (bf16[768]{0:T(1024)(128)(2,1)S(1)}, bf16[768]{0:T(1024)(128)(2,1)}, u32[]{:S(2)}) copy-start(bf16[768]{0:T(1024)(128)(2,1)} %param.33) | copy-start | bytes 4612
  28.5 6.3 %copy-start.31 = (bf16[768]{0:T(1024)(128)(2,1)S(1)}, bf16[768]{0:T(1024)(128)(2,1)}, u32[]{:S(2)}) copy-start(bf16[768]{0:T(1024)(128)(2,1)} %param.34) | copy-start | bytes 4612
  28.6 6.3 %copy-start.32 = (bf16[768]{0:T(1024)(128)(2,1)S(1)}, bf16[768]{0:T(1024)(128)(2,1)}, u32[]{:S(2)}) copy-start(bf16[768]{0:T(1024)(128)(2,1)} %param.35) | copy-start | bytes 4612
  34.6 7.5 %collective-permute-start.9 = (bf16[512,3072]{1,0:T(8,128)(2,1)S(1)}, bf16[512,3072]{1,0:T(8,128)(2,1)S(1)}, u32[]{:S(2)}, u32[]{:S(2)}) collective-permute-start(bf16[512,3072]{1,0:T(8,128)(2,1)S(1)} %get-tuple-element.84.refs_0_), channel_id=1, source_target_pairs={{0,1},{1,0},{2,3},{3,2},{4,5},{5,4},{6,7},{7,6},{8,9},{9,8},{10,11... | collective-permute-start | bytes 9437192 | tf_op jit(solution)/shard_map/ppermute | solution.py:415
  34.9 20.0 %collective-permute-start.11 = (bf16[512,768]{1,0:T(8,128)(2,1)S(1)}, bf16[512,768]{1,0:T(8,128)(2,1)S(1)}, u32[]{:S(2)}, u32[]{:S(2)}) collective-permute-start(bf16[512,768]{1,0:T(8,128)(2,1)S(1)} %get-tuple-element.79.refs_0_), channel_id=1, source_target_pairs={{0,1},{1,0},{2,3},{3,2},{4,5},{5,4},{6,7},{7,6},{8,9},{9,8},{10,11... | collective-permute-start | bytes 2359304 | tf_op jit(solution)/shard_map/ppermute | solution.py:415
  39.9 4.5 %copy-start.20 = (f32[512,768]{1,0:T(8,128)}, f32[512,768]{1,0:T(8,128)S(1)}, u32[]{:S(2)}) copy-start(f32[512,768]{1,0:T(8,128)S(1)} %get-tuple-element.103.refs_3_) | copy-start | bytes 4718596
  39.9 4.5 %collective-permute-start.10 = (bf16[512,384]{1,0:T(8,128)(2,1)S(1)}, bf16[512,384]{1,0:T(8,128)(2,1)S(1)}, u32[]{:S(2)}, u32[]{:S(2)}) collective-permute-start(bf16[512,384]{1,0:T(8,128)(2,1)S(1)} %get-tuple-element.91), channel_id=1, source_target_pairs={{0,1},{1,0},{2,3},{3,2},{4,5},{5,4},{6,7},{7,6},{8,9},{9,8},{10,11... | collective-permute-start | bytes 1179656 | tf_op jit(solution)/shard_map/ppermute | solution.py:415
  40.1 11.8 %collective-permute-start.6 = (bf16[128,768]{1,0:T(8,128)(2,1)S(1)}, bf16[128,768]{1,0:T(8,128)(2,1)S(1)}, u32[]{:S(2)}, u32[]{:S(2)}) collective-permute-start(bf16[128,768]{1,0:T(8,128)(2,1)S(1)} %get-tuple-element.87), channel_id=1, source_target_pairs={{0,1},{1,0},{2,3},{3,2},{4,5},{5,4},{6,7},{7,6},{8,9},{9,8},{10,11... | collective-permute-start | bytes 589832 | tf_op jit(solution)/shard_map/ppermute | solution.py:415
  40.4 12.9 %collective-permute-start.7 = (bf16[128,768]{1,0:T(8,128)(2,1)S(1)}, bf16[128,768]{1,0:T(8,128)(2,1)S(1)}, u32[]{:S(2)}, u32[]{:S(2)}) collective-permute-start(bf16[128,768]{1,0:T(8,128)(2,1)S(1)} %get-tuple-element.88), channel_id=1, source_target_pairs={{0,2},{1,3},{2,0},{3,1},{4,6},{5,7},{6,4},{7,5},{8,10},{9,11},{10,... | collective-permute-start | bytes 589832 | tf_op jit(solution)/shard_map/ppermute | solution.py:415
  42.1 11.3 %collective-permute-start.8 = (bf16[128,768]{1,0:T(8,128)(2,1)S(1)}, bf16[128,768]{1,0:T(8,128)(2,1)S(1)}, u32[]{:S(2)}, u32[]{:S(2)}) collective-permute-start(bf16[128,768]{1,0:T(8,128)(2,1)S(1)} %get-tuple-element.89), channel_id=1, source_target_pairs={{0,3},{1,2},{2,1},{3,0},{4,7},{5,6},{6,5},{7,4},{8,11},{9,10},{10,... | collective-permute-start | bytes 589832 | tf_op jit(solution)/shard_map/ppermute | solution.py:415
  44.3 10.6 %collective-permute-start.12 = (bf16[512,1536]{1,0:T(8,128)(2,1)S(1)}, bf16[512,1536]{1,0:T(8,128)(2,1)S(1)}, u32[]{:S(2)}, u32[]{:S(2)}) collective-permute-start(bf16[512,1536]{1,0:T(8,128)(2,1)S(1)} %get-tuple-element.102.refs_1_), channel_id=1, source_target_pairs={{0,1},{1,0},{2,3},{3,2},{4,5},{5,4},{6,7},{7,6},{8,9},{9,8},{10,11... | collective-permute-start | bytes 4718600 | tf_op jit(solution)/shard_map/ppermute | solution.py:415
  51.9 30.9 %copy-start.15 = (bf16[1536,384]{1,0:T(8,128)(2,1)}, bf16[1536,384]{1,0:T(8,128)(2,1)S(1)}, u32[]{:S(2)}) copy-start(bf16[1536,384]{1,0:T(8,128)(2,1)S(1)} %get-tuple-element.107.refs_0_) | copy-start | bytes 3538948
  51.9 19.9 %collective-permute-start.13 = (bf16[1536,384]{1,0:T(8,128)(2,1)S(1)}, bf16[1536,384]{1,0:T(8,128)(2,1)S(1)}, u32[]{:S(2)}, u32[]{:S(2)}) collective-permute-start(bf16[1536,384]{1,0:T(8,128)(2,1)S(1)} %get-tuple-element.96.refs_4_), channel_id=1, source_target_pairs={{0,2},{1,5},{2,0},{3,7},{4,6},{5,1},{6,4},{7,3},{8,10},{9,13},{10,... | collective-permute-start | bytes 3538952 | tf_op jit(solution)/shard_map/ppermute | solution.py:442
  56.0 3.7 %copy-start.19 = (f32[512,768]{1,0:T(8,128)S(1)}, f32[512,768]{1,0:T(8,128)}, u32[]{:S(2)}) copy-start(f32[512,768]{1,0:T(8,128)} %copy-done.18) | copy-start | bytes 4718596
  56.0 3.7 %copy-start.21 = (f32[512,768]{1,0:T(8,128)S(1)}, f32[512,768]{1,0:T(8,128)}, u32[]{:S(2)}) copy-start(f32[512,768]{1,0:T(8,128)} %copy-done.20) | copy-start | bytes 4718596
  59.7 37.2 %copy-start.13 = (bf16[384,1536]{1,0:T(8,128)(2,1)}, bf16[384,1536]{1,0:T(8,128)(2,1)S(1)}, u32[]{:S(2)}) copy-start(bf16[384,1536]{1,0:T(8,128)(2,1)S(1)} %get-tuple-element.121.refs_0_) | copy-start | bytes 3538948
  65.2 5.8 %copy-start.17 = (f32[512,768]{1,0:T(8,128)}, f32[512,768]{1,0:T(8,128)S(1)}, u32[]{:S(2)}) copy-start(f32[512,768]{1,0:T(8,128)S(1)} %get-tuple-element.112.refs_2_) | copy-start | bytes 4718596
  71.0 12.5 %collective-permute-start.16 = (bf16[3,512,384]{2,1,0:T(8,128)(2,1)S(1)}, bf16[3,512,384]{2,1,0:T(8,128)(2,1)S(1)}, u32[]{:S(2)}, u32[]{:S(2)}) collective-permute-start(bf16[3,512,384]{2,1,0:T(8,128)(2,1)S(1)} %get-tuple-element.111.refs_1_), channel_id=1, source_target_pairs={{0,1},{1,0},{2,3},{3,2},{4,5},{5,4},{6,7},{7,6},{8,9},{9,8},{10,11... | collective-permute-start | bytes 3538952 | tf_op jit(solution)/shard_map/ppermute | solution.py:415
  72.5 9.1 %collective-permute-start.18 = (bf16[768,384]{1,0:T(8,128)(2,1)S(1)}, bf16[768,384]{1,0:T(8,128)(2,1)S(1)}, u32[]{:S(2)}, u32[]{:S(2)}) collective-permute-start(bf16[768,384]{1,0:T(8,128)(2,1)S(1)} %outer0.1.refs_5_), channel_id=1, source_target_pairs={{0,4},{1,3},{2,6},{3,1},{4,0},{5,7},{6,2},{7,5},{8,12},{9,11},{10,... | collective-permute-start | bytes 1769480 | tf_op jit(solution)/shard_map/ppermute | solution.py:442
  73.3 10.2 %collective-permute-start.14 = (bf16[512,768]{1,0:T(8,128)(2,1)S(1)}, bf16[512,768]{1,0:T(8,128)(2,1)S(1)}, u32[]{:S(2)}, u32[]{:S(2)}) collective-permute-start(bf16[512,768]{1,0:T(8,128)(2,1)S(1)} %get-tuple-element.113.refs_0_), channel_id=1, source_target_pairs={{0,1},{1,0},{2,3},{3,2},{4,5},{5,4},{6,7},{7,6},{8,9},{9,8},{10,11... | collective-permute-start | bytes 2359304 | tf_op jit(solution)/shard_map/ppermute | solution.py:415
  74.2 9.3 %collective-permute-start.15 = (bf16[512,768]{1,0:T(8,128)(2,1)S(1)}, bf16[512,768]{1,0:T(8,128)(2,1)S(1)}, u32[]{:S(2)}, u32[]{:S(2)}) collective-permute-start(bf16[512,768]{1,0:T(8,128)(2,1)S(1)} %get-tuple-element.114.refs_2_), channel_id=1, source_target_pairs={{0,1},{1,0},{2,3},{3,2},{4,5},{5,4},{6,7},{7,6},{8,9},{9,8},{10,11... | collective-permute-start | bytes 2359304 | tf_op jit(solution)/shard_map/ppermute | solution.py:415
  74.2 9.3 %collective-permute-start.17 = (bf16[512,384]{1,0:T(8,128)(2,1)S(1)}, bf16[512,384]{1,0:T(8,128)(2,1)S(1)}, u32[]{:S(2)}, u32[]{:S(2)}) collective-permute-start(bf16[512,384]{1,0:T(8,128)(2,1)S(1)} %get-tuple-element.116), channel_id=1, source_target_pairs={{0,1},{1,0},{2,3},{3,2},{4,5},{5,4},{6,7},{7,6},{8,9},{9,8},{10,11... | collective-permute-start | bytes 1179656 | tf_op jit(solution)/shard_map/ppermute | solution.py:415
  81.6 15.3 %collective-permute-start.20 = (bf16[384,1536]{1,0:T(8,128)(2,1)S(1)}, bf16[384,1536]{1,0:T(8,128)(2,1)S(1)}, u32[]{:S(2)}, u32[]{:S(2)}) collective-permute-start(bf16[384,1536]{1,0:T(8,128)(2,1)S(1)} %get-tuple-element.105.refs_8_), channel_id=1, source_target_pairs={{0,8},{1,5},{2,10},{3,7},{4,12},{5,1},{6,14},{7,3},{8,0},{9,13},{1... | collective-permute-start | bytes 3538952 | tf_op jit(solution)/shard_map/ppermute | solution.py:442
  87.6 22.5 %collective-permute-start.19 = (bf16[1568,384]{1,0:T(8,128)(2,1)S(1)}, bf16[1568,384]{1,0:T(8,128)(2,1)S(1)}, u32[]{:S(2)}, u32[]{:S(2)}) collective-permute-start(bf16[1568,384]{1,0:T(8,128)(2,1)S(1)} %get-tuple-element.120.refs_2_), channel_id=1, source_target_pairs={{0,2},{1,5},{2,0},{3,7},{4,6},{5,1},{6,4},{7,3},{8,10},{9,13},{10,... | collective-permute-start | bytes 3612680 | tf_op jit(solution)/shard_map/ppermute | solution.py:442
  87.9 32.5 %collective-permute-start.24 = (bf16[384,384]{1,0:T(8,128)(2,1)S(1)}, bf16[384,384]{1,0:T(8,128)(2,1)S(1)}, u32[]{:S(2)}, u32[]{:S(2)}) collective-permute-start(bf16[384,384]{1,0:T(8,128)(2,1)S(1)} %outer1.1.refs_14_), channel_id=1, source_target_pairs={{0,8},{1,9},{2,10},{3,11},{4,12},{5,13},{6,14},{7,15},{8,0},{9,1},... | collective-permute-start | bytes 884744 | tf_op jit(solution)/shard_map/ppermute | solution.py:442
  97.6 21.2 %collective-permute-start.25 = (bf16[192,1536]{1,0:T(8,128)(2,1)S(1)}, bf16[192,1536]{1,0:T(8,128)(2,1)S(1)}, u32[]{:S(2)}, u32[]{:S(2)}) collective-permute-start(bf16[192,1536]{1,0:T(8,128)(2,1)S(1)} %inner0.1.refs_3_), channel_id=1, source_target_pairs={{0,2},{1,9},{2,0},{3,11},{4,6},{5,13},{6,4},{7,15},{8,10},{9,1},{1... | collective-permute-start | bytes 1769480 | tf_op jit(solution)/shard_map/ppermute | solution.py:442
  110.8 13.1 %collective-permute-start.28 = (bf16[800,384]{1,0:T(8,128)(2,1)S(1)}, bf16[800,384]{1,0:T(8,128)(2,1)S(1)}, u32[]{:S(2)}, u32[]{:S(2)}) collective-permute-start(bf16[800,384]{1,0:T(8,128)(2,1)S(1)} %rest0.1.refs_6_.refs_3_), channel_id=1, source_target_pairs={{0,4},{1,3},{2,6},{3,1},{4,0},{5,7},{6,2},{7,5},{8,12},{9,11},{10,... | collective-permute-start | bytes 1843208 | tf_op jit(solution)/shard_map/ppermute | solution.py:442
  111.5 7.3 %copy-start.14 = (bf16[384,1536]{1,0:T(8,128)(2,1)S(1)}, bf16[384,1536]{1,0:T(8,128)(2,1)}, u32[]{:S(2)}) copy-start(bf16[384,1536]{1,0:T(8,128)(2,1)} %copy-done.13) | copy-start | bytes 3538948
  119.5 6.7 %collective-permute-start.27 = (bf16[96,1536]{1,0:T(8,128)(2,1)S(1)}, bf16[96,1536]{1,0:T(8,128)(2,1)S(1)}, u32[]{:S(2)}, u32[]{:S(2)}) collective-permute-start(bf16[96,1536]{1,0:T(8,128)(2,1)S(1)} %inner1.1.refs_4_), channel_id=1, source_target_pairs={{0,4},{1,3},{2,6},{3,1},{4,0},{5,7},{6,2},{7,5},{8,12},{9,11},{10,... | collective-permute-start | bytes 884744 | tf_op jit(solution)/shard_map/ppermute | solution.py:442
  121.0 7.7 %collective-permute-start.26 = (bf16[192,384]{1,0:T(8,128)(2,1)S(1)}, bf16[192,384]{1,0:T(8,128)(2,1)S(1)}, u32[]{:S(2)}, u32[]{:S(2)}) collective-permute-start(bf16[192,384]{1,0:T(8,128)(2,1)S(1)} %outer2.1.refs_4_), channel_id=1, source_target_pairs={{0,16},{1,17},{2,18},{3,19},{4,20},{5,21},{6,22},{7,23},{8,24},{9,... | collective-permute-start | bytes 442376 | tf_op jit(solution)/shard_map/ppermute | solution.py:442
  123.4 7.0 %collective-permute-start.21 = (bf16[128,768]{1,0:T(8,128)(2,1)S(1)}, bf16[128,768]{1,0:T(8,128)(2,1)S(1)}, u32[]{:S(2)}, u32[]{:S(2)}) collective-permute-start(bf16[128,768]{1,0:T(8,128)(2,1)S(1)} %get-tuple-element.124), channel_id=1, source_target_pairs={{0,1},{1,0},{2,3},{3,2},{4,5},{5,4},{6,7},{7,6},{8,9},{9,8},{10,11... | collective-permute-start | bytes 589832 | tf_op jit(solution)/shard_map/ppermute | solution.py:415
  123.4 7.3 %collective-permute-start.22 = (bf16[128,768]{1,0:T(8,128)(2,1)S(1)}, bf16[128,768]{1,0:T(8,128)(2,1)S(1)}, u32[]{:S(2)}, u32[]{:S(2)}) collective-permute-start(bf16[128,768]{1,0:T(8,128)(2,1)S(1)} %get-tuple-element.125), channel_id=1, source_target_pairs={{0,2},{1,3},{2,0},{3,1},{4,6},{5,7},{6,4},{7,5},{8,10},{9,11},{10,... | collective-permute-start | bytes 589832 | tf_op jit(solution)/shard_map/ppermute | solution.py:415
  123.9 11.5 %collective-permute-start.23 = (bf16[128,768]{1,0:T(8,128)(2,1)S(1)}, bf16[128,768]{1,0:T(8,128)(2,1)S(1)}, u32[]{:S(2)}, u32[]{:S(2)}) collective-permute-start(bf16[128,768]{1,0:T(8,128)(2,1)S(1)} %get-tuple-element.126), channel_id=1, source_target_pairs={{0,3},{1,2},{2,1},{3,0},{4,7},{5,6},{6,5},{7,4},{8,11},{9,10},{10,... | collective-permute-start | bytes 589832 | tf_op jit(solution)/shard_map/ppermute | solution.py:415
  126.2 11.9 %collective-permute-start.29 = (bf16[416,384]{1,0:T(8,128)(2,1)S(1)}, bf16[416,384]{1,0:T(8,128)(2,1)S(1)}, u32[]{:S(2)}, u32[]{:S(2)}) collective-permute-start(bf16[416,384]{1,0:T(8,128)(2,1)S(1)} %rest1.1.refs_4_), channel_id=1, source_target_pairs={{0,8},{1,9},{2,10},{3,11},{4,12},{5,13},{6,14},{7,15},{8,0},{9,1},... | collective-permute-start | bytes 958472 | tf_op jit(solution)/shard_map/ppermute | solution.py:442
  129.4 7.6 %collective-permute-start.32 = (bf16[192,384]{1,0:T(8,128)(2,1)S(1)}, bf16[192,384]{1,0:T(8,128)(2,1)S(1)}, u32[]{:S(2)}, u32[]{:S(2)}) collective-permute-start(bf16[192,384]{1,0:T(8,128)(2,1)S(1)} %outer3.1.refs_4_.refs_0_), channel_id=1, source_target_pairs={{0,2},{1,3},{2,0},{3,1},{4,6},{5,7},{6,4},{7,5},{8,10},{9,11},{10,... | collective-permute-start | bytes 442376 | tf_op jit(solution)/shard_map/ppermute | solution.py:415
  130.4 10.7 %collective-permute-start.33 = (bf16[192,384]{1,0:T(8,128)(2,1)S(1)}, bf16[192,384]{1,0:T(8,128)(2,1)S(1)}, u32[]{:S(2)}, u32[]{:S(2)}) collective-permute-start(bf16[192,384]{1,0:T(8,128)(2,1)S(1)} %outer3.1.refs_4_.refs_0_), channel_id=1, source_target_pairs={{0,1},{1,0},{2,3},{3,2},{4,5},{5,4},{6,7},{7,6},{8,9},{9,8},{10,11... | collective-permute-start | bytes 442376 | tf_op jit(solution)/shard_map/ppermute | solution.py:415
  130.6 12.1 %collective-permute-start.31 = (bf16[48,1536]{1,0:T(8,128)(2,1)S(1)}, bf16[48,1536]{1,0:T(8,128)(2,1)S(1)}, u32[]{:S(2)}, u32[]{:S(2)}) collective-permute-start(bf16[48,1536]{1,0:T(8,128)(2,1)S(1)} %inner2.1.refs_5_), channel_id=1, source_target_pairs={{0,16},{1,17},{2,18},{3,19},{4,20},{5,21},{6,22},{7,23},{8,24},{9,... | collective-permute-start | bytes 442376 | tf_op jit(solution)/shard_map/ppermute | solution.py:442
  136.9 4.1 %collective-permute-start.34 = (bf16[192,384]{1,0:T(8,128)(2,1)S(1)}, bf16[192,384]{1,0:T(8,128)(2,1)S(1)}, u32[]{:S(2)}, u32[]{:S(2)}) collective-permute-start(bf16[192,384]{1,0:T(8,128)(2,1)S(1)} %collective-permute-done.32.refs_1_), channel_id=1, source_target_pairs={{0,1},{1,0},{2,3},{3,2},{4,5},{5,4},{6,7},{7,6},{8,9},{9,8},{10,11... | collective-permute-start | bytes 442376 | tf_op jit(solution)/shard_map/ppermute | solution.py:415
  139.8 10.6 %collective-permute-start.30 = (bf16[224,384]{1,0:T(8,128)(2,1)S(1)}, bf16[224,384]{1,0:T(8,128)(2,1)S(1)}, u32[]{:S(2)}, u32[]{:S(2)}) collective-permute-start(bf16[224,384]{1,0:T(8,128)(2,1)S(1)} %rest2.1.refs_4_.refs_5_), channel_id=1, source_target_pairs={{0,16},{1,17},{2,18},{3,19},{4,20},{5,21},{6,22},{7,23},{8,24},{9,... | collective-permute-start | bytes 516104 | tf_op jit(solution)/shard_map/ppermute | solution.py:442
  144.6 8.7 %collective-permute-start.38 = (bf16[48,1536]{1,0:T(8,128)(2,1)S(1)}, bf16[48,1536]{1,0:T(8,128)(2,1)S(1)}, u32[]{:S(2)}, u32[]{:S(2)}) collective-permute-start(bf16[48,1536]{1,0:T(8,128)(2,1)S(1)} %inner3.1.refs_6_.refs_0_), channel_id=1, source_target_pairs={{0,2},{1,3},{2,0},{3,1},{4,6},{5,7},{6,4},{7,5},{8,10},{9,11},{10,... | collective-permute-start | bytes 442376 | tf_op jit(solution)/shard_map/ppermute | solution.py:415
  151.1 5.1 %collective-permute-start.35 = (bf16[224,384]{1,0:T(8,128)(2,1)S(1)}, bf16[224,384]{1,0:T(8,128)(2,1)S(1)}, u32[]{:S(2)}, u32[]{:S(2)}) collective-permute-start(bf16[224,384]{1,0:T(8,128)(2,1)S(1)} %rest3.1.refs_4_.refs_0_), channel_id=1, source_target_pairs={{0,2},{1,3},{2,0},{3,1},{4,6},{5,7},{6,4},{7,5},{8,10},{9,11},{10,... | collective-permute-start | bytes 516104 | tf_op jit(solution)/shard_map/ppermute | solution.py:415
  152.0 6.0 %collective-permute-start.39 = (bf16[48,1536]{1,0:T(8,128)(2,1)S(1)}, bf16[48,1536]{1,0:T(8,128)(2,1)S(1)}, u32[]{:S(2)}, u32[]{:S(2)}) collective-permute-start(bf16[48,1536]{1,0:T(8,128)(2,1)S(1)} %inner3.1.refs_6_.refs_0_), channel_id=1, source_target_pairs={{0,1},{1,0},{2,3},{3,2},{4,5},{5,4},{6,7},{7,6},{8,9},{9,8},{10,11... | collective-permute-start | bytes 442376 | tf_op jit(solution)/shard_map/ppermute | solution.py:415
  153.4 4.6 %collective-permute-start.40 = (bf16[48,1536]{1,0:T(8,128)(2,1)S(1)}, bf16[48,1536]{1,0:T(8,128)(2,1)S(1)}, u32[]{:S(2)}, u32[]{:S(2)}) collective-permute-start(bf16[48,1536]{1,0:T(8,128)(2,1)S(1)} %collective-permute-done.38.refs_1_), channel_id=1, source_target_pairs={{0,1},{1,0},{2,3},{3,2},{4,5},{5,4},{6,7},{7,6},{8,9},{9,8},{10,11... | collective-permute-start | bytes 442376 | tf_op jit(solution)/shard_map/ppermute | solution.py:415
  153.4 6.2 %collective-permute-start.36 = (bf16[224,384]{1,0:T(8,128)(2,1)S(1)}, bf16[224,384]{1,0:T(8,128)(2,1)S(1)}, u32[]{:S(2)}, u32[]{:S(2)}) collective-permute-start(bf16[224,384]{1,0:T(8,128)(2,1)S(1)} %rest3.1.refs_4_.refs_0_), channel_id=1, source_target_pairs={{0,1},{1,0},{2,3},{3,2},{4,5},{5,4},{6,7},{7,6},{8,9},{9,8},{10,11... | collective-permute-start | bytes 516104 | tf_op jit(solution)/shard_map/ppermute | solution.py:415
  156.2 3.4 %collective-permute-start.37 = (bf16[224,384]{1,0:T(8,128)(2,1)S(1)}, bf16[224,384]{1,0:T(8,128)(2,1)S(1)}, u32[]{:S(2)}, u32[]{:S(2)}) collective-permute-start(bf16[224,384]{1,0:T(8,128)(2,1)S(1)} %collective-permute-done.35.refs_1_), channel_id=1, source_target_pairs={{0,1},{1,0},{2,3},{3,2},{4,5},{5,4},{6,7},{7,6},{8,9},{9,8},{10,11... | collective-permute-start | bytes 516104 | tf_op jit(solution)/shard_map/ppermute | solution.py:415
  (14 other events, 33.3 us)
